TPU v7x, 32 devices: a whole 2x2x4 slice. The times are simulated.
32 devices in a mesh: seq: 8 (over z, y), head: 4 (over x, core).
Axes of the slice: x: 2, y: 2, z: 4, core: 2. Of those that a mesh axis runs over, the one named last changes fastest.
Arguments:
- hidden: float32 [8192, 2048], P('seq'), may hold values from -6 to 6
- doc_starts: int32 [7], replicated, may hold values from 0 to 8191, as said below
- norm_gain: float32 [2048], replicated, may hold values from 0.1 to 1.9
- w_query: bfloat16 [2048, 2048], P(None, 'head'), may hold values from -0.125 to 0.125
- w_key: bfloat16 [2048, 2048], P(None, 'head'), may hold values from -0.125 to 0.125
- w_value: bfloat16 [2048, 2048], P(None, 'head'), may hold values from -0.125 to 0.125
- w_strength: bfloat16 [2048, 16], P(None, 'head'), may hold values from -0.125 to 0.125
- strength_bias: float32 [16], P('head'), may hold values from -8.5 to -0.8
- conv_query: bfloat16 [4, 2048], P(None, 'head'), may hold values from -2.5 to 2.5
- conv_key: bfloat16 [4, 2048], P(None, 'head'), may hold values from -2.5 to 2.5
- conv_value: bfloat16 [4, 2048], P(None, 'head'), may hold values from -2.5 to 2.5
- head_gain: float32 [128], replicated, may hold values from 0.1 to 1.9
- w_output: bfloat16 [2048, 2048], P('head'), may hold values from -0.125 to 0.125
- ffn_gain: float32 [2048], replicated, may hold values from 0.1 to 1.9
- w_gate: bfloat16 [2048, 5632], P(None, 'head'), may hold values from -0.125 to 0.125
- w_up: bfloat16 [2048, 5632], P(None, 'head'), may hold values from -0.125 to 0.125
- w_down: bfloat16 [5632, 2048], P('head'), may hold values from -0.078125 to 0.078125
- out_grad: float32 [8192, 2048], P('seq'), may hold values from -6 to 6
Outputs:
- block_output: float32 [8192, 2048], P('seq')
- hidden_grad: float32 [8192, 2048], P('seq')
- norm_gain_grad: float32 [2048], P('seq')
- w_query_grad: float32 [2048, 2048], P('seq', 'head')
- w_key_grad: float32 [2048, 2048], P('seq', 'head')
- w_value_grad: float32 [2048, 2048], P('seq', 'head')
- w_strength_grad: float32 [2048, 16], P('seq', 'head')
- strength_bias_grad: float32 [16], P('head')
- conv_query_grad: float32 [4, 2048], P(None, 'head')
- conv_key_grad: float32 [4, 2048], P(None, 'head')
- conv_value_grad: float32 [4, 2048], P(None, 'head')
- head_gain_grad: float32 [128], replicated
- w_output_grad: float32 [2048, 2048], P('head', 'seq')
- ffn_gain_grad: float32 [2048], P('seq')
- w_gate_grad: float32 [2048, 5632], P('seq', 'head')
- w_up_grad: float32 [2048, 5632], P('seq', 'head')
- w_down_grad: float32 [5632, 2048], P('head', 'seq')
Inputs may be any that keep to these rules, and one draw needn't show every extreme that they name: doc_starts rise strictly; the first is 0; the next two lie in tokens 1 to 1023; the fourth lies in tokens 8192 // 2 - 1024 // 2 to 4095; the fifth in tokens 8192 - 1023 to 7680; the sixth in tokens 8192 - 1024 // 2 + 1 to 8190; the last is token 8191.
All inputs are finite; a program needn't handle non-finite values.
Results may differ from a plain program's by a relative error of at most 0.014.
Values sent between devices are 32-bit elements; how exact they have to be, the bound alone decides.
No kernel may reach another device: no remote copies, remote signals or barrier semaphores. Data moves between devices by JAX's collectives and lax.ppermute only.
A program may use at most 320 MiB of HBM per device.

v0:
```python
import jax
import jax.numpy as jnp
from jax import lax
from jax.sharding import PartitionSpec as P

CONV = 4
GROUP = 64


HIGH = lax.Precision.HIGHEST


def from_behind(block, axis, distance):
    devices = range(lax.axis_size(axis))
    route = [(i - distance, i) for i in devices if i - distance in devices]
    return lax.ppermute(block, axis, route)


def entering(shard, axis, combine, identity, reverse):
    length, here = (lax.axis_size(axis), lax.axis_index(axis))
    everything = jax.tree.map(lambda part: lax.all_gather(part, axis), shard)
    start = jax.tree.map(
        lambda part, zero: jnp.broadcast_to(jnp.asarray(zero, part.dtype), part.shape),
        shard,
        identity,
    )

    def hop(k, before):
        at = length - 1 - k if reverse else k
        reached = at > here if reverse else at < here
        new = combine(before, jax.tree.map(lambda part: part[at], everything))
        return jax.tree.map(lambda a, b: jnp.where(reached, a, b), new, before)

    return lax.fori_loop(0, length, hop, start)


def doc_index(starts, places):
    return jnp.sum((starts[None, :] <= places[:, None]).astype(jnp.int32), axis=1) - 1


def rms_norm(values, scaling):
    return values * lax.rsqrt(jnp.mean(values * values, axis=-1, keepdims=True) + 1e-05) * scaling


def unit_rows(values):
    return values * lax.rsqrt(jnp.sum(values * values, axis=-1, keepdims=True) + 1e-06)


def short_conv(linear, border, kernel, doc_ids, border_ids):
    length = linear.shape[0]
    joined = jnp.concatenate([border, linear], axis=0)
    joined_ids = jnp.concatenate([border_ids, doc_ids])
    summed = jnp.zeros_like(linear)
    for offset in range(kernel.shape[0]):
        same_doc = (joined_ids[offset : offset + length] == doc_ids).astype(jnp.float32)
        summed = (
            summed + kernel[offset][None, :] * joined[offset : offset + length] * same_doc[:, None]
        )
    return summed


def prepare(
    lin_query,
    lin_key,
    lin_value,
    border,
    conv_query,
    conv_key,
    conv_value,
    logits,
    doc_ids,
    border_ids,
    head_size,
):
    length = lin_query.shape[0]
    inner_width = lin_query.shape[1]
    pieces = []
    for number, (linear, kernel) in enumerate(
        ((lin_query, conv_query), (lin_key, conv_key), (lin_value, conv_value))
    ):
        edge_part = border[:, number * inner_width : (number + 1) * inner_width]
        mixed_rows = jax.nn.silu(short_conv(linear, edge_part, kernel, doc_ids, border_ids))
        pieces.append(mixed_rows.reshape(length, inner_width // head_size, head_size))
    return (unit_rows(pieces[0]), unit_rows(pieces[1]), pieces[2], jax.nn.sigmoid(logits))


def nilpotent_inverse(strict):
    extent = strict.shape[-1]
    eye_block = jnp.eye(extent, dtype=jnp.float32)
    inverse = eye_block - strict
    square = strict
    covered = 2
    while covered < extent:
        square = jnp.einsum("hij,hjk->hik", square, square, precision=HIGH)
        inverse = jnp.einsum("hij,hjk->hik", inverse, eye_block + square, precision=HIGH)
        covered = covered * 2
    return inverse


def solve_group(key_rows, strength, same_doc):
    extent = key_rows.shape[0]
    below = jnp.tril(jnp.ones((extent, extent), jnp.float32), -1)
    key_key = jnp.einsum("ihd,jhd->hij", key_rows, key_rows, precision=HIGH)
    rates = jnp.transpose(strength)
    strict = key_key * rates[:, :, None] * (same_doc * below)[None]
    return nilpotent_inverse(strict) * rates[:, None, :]


def group_terms(queries, key_rows, values, strength, carried, same_doc):
    extent = queries.shape[0]
    through = jnp.tril(jnp.ones((extent, extent), jnp.float32), 0)
    solved = solve_group(key_rows, strength, same_doc)
    query_key = jnp.einsum("ihd,jhd->hij", queries, key_rows, precision=HIGH)
    write_keys = jnp.einsum(
        "hij,jhd->hid", solved, key_rows * carried[:, None, None], precision=HIGH
    )
    write_values = jnp.einsum("hij,jhd->hid", solved, values, precision=HIGH)
    scores = query_key * (same_doc * through)[None]
    return (write_keys, write_values, scores)


def group_state(memory, queries, key_rows, write_keys, write_values, scores, carried, final_doc):
    residue = write_values - jnp.einsum("hid,hde->hie", write_keys, memory, precision=HIGH)
    outputs = jnp.einsum("ihd,hde->ihe", queries * carried[:, None, None], memory, precision=HIGH)
    outputs = outputs + jnp.einsum("hij,hje->ihe", scores, residue, precision=HIGH)
    updated = carried[-1] * memory + jnp.einsum(
        "ihd,hie->hde", key_rows * final_doc[:, None, None], residue, precision=HIGH
    )
    return (updated, outputs)


def group_masks(doc_ids, prior_ids):
    carried = (doc_ids == prior_ids[:, None]).astype(jnp.float32)
    same_doc = (doc_ids[:, :, None] == doc_ids[:, None, :]).astype(jnp.float32)
    final_doc = (doc_ids == doc_ids[:, -1:]).astype(jnp.float32)
    return (carried, same_doc, final_doc)


def local_pass(
    queries, key_rows, values, strength, carried, same_doc, final_doc, identity, zero_memory
):

    @jax.checkpoint
    def advance(carry, pieces):
        memory, product = carry
        write_keys, write_values, scores = group_terms(
            pieces[0], pieces[1], pieces[2], pieces[3], pieces[4], pieces[5]
        )
        updated, outputs = group_state(
            memory, pieces[0], pieces[1], write_keys, write_values, scores, pieces[4], pieces[6]
        )
        reading = jnp.transpose(pieces[0] * pieces[4][:, None, None], (1, 0, 2))
        reading = reading - jnp.einsum("hij,hjd->hid", scores, write_keys, precision=HIGH)
        effective = jnp.einsum("hid,hde->ihe", reading, product, precision=HIGH)
        step_map = pieces[4][-1] * identity - jnp.einsum(
            "ihd,hie->hde", pieces[1] * pieces[6][:, None, None], write_keys, precision=HIGH
        )
        advanced = jnp.einsum("hij,hjk->hik", step_map, product, precision=HIGH)
        return ((updated, advanced), (outputs, effective))

    finals, stacked = lax.scan(
        advance,
        (zero_memory, identity),
        (queries, key_rows, values, strength, carried, same_doc, final_doc),
    )
    return (finals[0], finals[1], stacked[0], stacked[1])


def compose(earlier, later):
    joined_map = jnp.einsum("hij,hjk->hik", later[0], earlier[0], precision=HIGH)
    joined_add = jnp.einsum("hij,hjk->hik", later[0], earlier[1], precision=HIGH) + later[1]
    return (joined_map, joined_add)


def shards(
    hidden,
    doc_starts,
    norm_gain,
    w_query,
    w_key,
    w_value,
    w_strength,
    strength_bias,
    conv_query,
    conv_key,
    conv_value,
    head_gain,
    w_output,
    ffn_gain,
    w_gate,
    w_up,
    w_down,
    out_grad,
):
    length = hidden.shape[0]
    head_size = head_gain.shape[0]
    head_count = strength_bias.shape[0]
    inner_width = head_count * head_size
    group_count = length // GROUP
    margin = CONV - 1
    seq_rank = lax.axis_index("seq")
    first_place = seq_rank * length
    places = first_place + jnp.arange(length, dtype=jnp.int32)
    doc_ids = doc_index(doc_starts, places)
    border_ids = doc_index(doc_starts, first_place - margin + jnp.arange(margin, dtype=jnp.int32))
    prior_ids = doc_index(doc_starts, places[::GROUP] - 1)
    mask_set = group_masks(doc_ids.reshape(group_count, GROUP), prior_ids)
    identity = jnp.broadcast_to(
        jnp.eye(head_size, dtype=jnp.float32), (head_count, head_size, head_size)
    )
    zero_memory = jnp.zeros((head_count, head_size, head_size), jnp.float32)

    def reshape_groups(member):
        return member.reshape((group_count, GROUP) + member.shape[1:])

    normed_full, norm_pull = jax.vjp(rms_norm, hidden, norm_gain)
    normed = normed_full.astype(jnp.bfloat16)
    lin_query = jnp.dot(normed, w_query, preferred_element_type=jnp.float32)
    lin_key = jnp.dot(normed, w_key, preferred_element_type=jnp.float32)
    lin_value = jnp.dot(normed, w_value, preferred_element_type=jnp.float32)
    logits = jnp.dot(normed, w_strength, preferred_element_type=jnp.float32) + strength_bias
    tail_rows = jnp.concatenate(
        [lin_query[-margin:], lin_key[-margin:], lin_value[-margin:]], axis=1
    )
    border = from_behind(tail_rows, "seq", 1)

    def prepare_local(
        lin_query, lin_key, lin_value, border, conv_query, conv_key, conv_value, logits
    ):
        return prepare(
            lin_query,
            lin_key,
            lin_value,
            border,
            conv_query,
            conv_key,
            conv_value,
            logits,
            doc_ids,
            border_ids,
            head_size,
        )

    prepared, prepare_pull = jax.vjp(
        prepare_local,
        lin_query,
        lin_key,
        lin_value,
        border,
        conv_query.astype(jnp.float32),
        conv_key.astype(jnp.float32),
        conv_value.astype(jnp.float32),
        logits,
    )
    grouped = tuple((reshape_groups(member) for member in prepared))

    def delta_local(queries, key_rows, values, strength):
        return local_pass(
            queries,
            key_rows,
            values,
            strength,
            mask_set[0],
            mask_set[1],
            mask_set[2],
            identity,
            zero_memory,
        )

    delta_out, delta_pull = jax.vjp(delta_local, grouped[0], grouped[1], grouped[2], grouped[3])
    shard_offset, transfer, local_rows, effective = delta_out
    state_in = entering((transfer, shard_offset), "seq", compose, (identity, zero_memory), False)[1]
    mixed_blocks = local_rows + jnp.einsum("cihd,hde->cihe", effective, state_in, precision=HIGH)
    mixed_rows = mixed_blocks.reshape(length, head_count, head_size)
    headed_full, head_pull = jax.vjp(rms_norm, mixed_rows, head_gain)
    headed = headed_full.reshape(length, inner_width).astype(jnp.bfloat16)
    branch = lax.psum(jnp.dot(headed, w_output, preferred_element_type=jnp.float32), "head")
    middle = hidden + branch
    normed_two_full, ffn_norm_pull = jax.vjp(rms_norm, middle, ffn_gain)
    normed_two = normed_two_full.astype(jnp.bfloat16)
    gate_rows = jnp.dot(normed_two, w_gate, preferred_element_type=jnp.float32)
    upward = jnp.dot(normed_two, w_up, preferred_element_type=jnp.float32)
    silu_gate = jax.nn.silu(gate_rows)
    active = (silu_gate * upward).astype(jnp.bfloat16)
    ffn_out = lax.psum(jnp.dot(active, w_down, preferred_element_type=jnp.float32), "head")
    block_output = middle + ffn_out
    ffn_cot = out_grad.astype(jnp.bfloat16)
    down_term = jnp.einsum("tf,td->fd", active, ffn_cot, preferred_element_type=jnp.float32)
    active_grad = jnp.einsum("td,fd->tf", ffn_cot, w_down, preferred_element_type=jnp.float32)
    sigma = jax.nn.sigmoid(gate_rows)
    gate_cot = (active_grad * upward * sigma * (1.0 + gate_rows * (1.0 - sigma))).astype(
        jnp.bfloat16
    )
    up_cot = (active_grad * silu_gate).astype(jnp.bfloat16)
    gate_term = jnp.einsum("td,tf->df", normed_two, gate_cot, preferred_element_type=jnp.float32)
    up_term = jnp.einsum("td,tf->df", normed_two, up_cot, preferred_element_type=jnp.float32)
    two_part = jnp.einsum("tf,df->td", gate_cot, w_gate, preferred_element_type=jnp.float32)
    two_part = two_part + jnp.einsum("tf,df->td", up_cot, w_up, preferred_element_type=jnp.float32)
    normed_two_grad = lax.psum(two_part, "head")
    middle_norm_grad, ffn_gain_part = ffn_norm_pull(normed_two_grad)
    middle_grad = out_grad + middle_norm_grad
    branch_cot = middle_grad.astype(jnp.bfloat16)
    output_term = jnp.einsum("ti,td->id", headed, branch_cot, preferred_element_type=jnp.float32)
    headed_grad = jnp.einsum("td,id->ti", branch_cot, w_output, preferred_element_type=jnp.float32)
    mixed_grad, head_gain_part = head_pull(headed_grad.reshape(length, head_count, head_size))
    mixed_cot = reshape_groups(mixed_grad)
    local_part = jnp.einsum("cihd,cihe->hde", effective, mixed_cot, precision=HIGH)
    back_maps = jnp.transpose(transfer, (0, 2, 1))
    later_grad = entering((back_maps, local_part), "seq", compose, (identity, zero_memory), True)[1]
    transfer_cot = jnp.einsum("hdf,hef->hde", later_grad, state_in, precision=HIGH)
    effective_cot = jnp.einsum("cihf,hdf->cihd", mixed_cot, state_in, precision=HIGH)
    delta_grads = delta_pull((later_grad, transfer_cot, mixed_cot, effective_cot))
    prepare_grads = prepare_pull(
        (
            delta_grads[0].reshape(length, head_count, head_size),
            delta_grads[1].reshape(length, head_count, head_size),
            delta_grads[2].reshape(length, head_count, head_size),
            delta_grads[3].reshape(length, head_count),
        )
    )
    returned = from_behind(prepare_grads[3], "seq", -1)
    stacked = jnp.concatenate([prepare_grads[0], prepare_grads[1], prepare_grads[2]], axis=1)
    stacked = stacked + jnp.concatenate(
        [jnp.zeros((length - margin, 3 * inner_width), jnp.float32), returned], axis=0
    )
    lin_cot = stacked.astype(jnp.bfloat16)
    query_cot = lin_cot[:, :inner_width]
    key_cot = lin_cot[:, inner_width : 2 * inner_width]
    value_cot = lin_cot[:, 2 * inner_width :]
    logit_grad = prepare_grads[7]
    strength_cot = logit_grad.astype(jnp.bfloat16)
    bias_part = jnp.sum(logit_grad, axis=0)
    query_term = jnp.einsum("td,ti->di", normed, query_cot, preferred_element_type=jnp.float32)
    key_term = jnp.einsum("td,ti->di", normed, key_cot, preferred_element_type=jnp.float32)
    value_term = jnp.einsum("td,ti->di", normed, value_cot, preferred_element_type=jnp.float32)
    strength_term = jnp.einsum(
        "td,th->dh", normed, strength_cot, preferred_element_type=jnp.float32
    )
    first_part = jnp.einsum("ti,di->td", query_cot, w_query, preferred_element_type=jnp.float32)
    first_part = first_part + jnp.einsum(
        "ti,di->td", key_cot, w_key, preferred_element_type=jnp.float32
    )
    first_part = first_part + jnp.einsum(
        "ti,di->td", value_cot, w_value, preferred_element_type=jnp.float32
    )
    first_part = first_part + jnp.einsum(
        "th,dh->td", strength_cot, w_strength, preferred_element_type=jnp.float32
    )
    normed_grad, head_gain_sum = lax.psum((first_part, head_gain_part), "head")
    hidden_norm_grad, norm_gain_part = norm_pull(normed_grad)
    hidden_grad = middle_grad + hidden_norm_grad
    summed_terms = (
        lax.psum_scatter(query_term, "seq", scatter_dimension=0, tiled=True),
        lax.psum_scatter(key_term, "seq", scatter_dimension=0, tiled=True),
        lax.psum_scatter(value_term, "seq", scatter_dimension=0, tiled=True),
        lax.psum_scatter(strength_term, "seq", scatter_dimension=0, tiled=True),
        lax.psum_scatter(output_term, "seq", scatter_dimension=1, tiled=True),
        lax.psum_scatter(gate_term, "seq", scatter_dimension=0, tiled=True),
        lax.psum_scatter(up_term, "seq", scatter_dimension=0, tiled=True),
        lax.psum_scatter(down_term, "seq", scatter_dimension=1, tiled=True),
        lax.psum_scatter(norm_gain_part, "seq", scatter_dimension=0, tiled=True),
        lax.psum_scatter(ffn_gain_part, "seq", scatter_dimension=0, tiled=True),
    )
    small_terms = lax.psum(
        (prepare_grads[4], prepare_grads[5], prepare_grads[6], bias_part, head_gain_sum), "seq"
    )
    return (
        block_output,
        hidden_grad,
        summed_terms[8],
        summed_terms[0],
        summed_terms[1],
        summed_terms[2],
        summed_terms[3],
        small_terms[3],
        small_terms[0],
        small_terms[1],
        small_terms[2],
        small_terms[4],
        summed_terms[4],
        summed_terms[9],
        summed_terms[5],
        summed_terms[6],
        summed_terms[7],
    )


def solution(mesh):
    return jax.shard_map(
        shards,
        mesh=mesh,
        in_specs=(
            P("seq", None),
            P(),
            P(),
            P(None, "head"),
            P(None, "head"),
            P(None, "head"),
            P(None, "head"),
            P("head"),
            P(None, "head"),
            P(None, "head"),
            P(None, "head"),
            P(),
            P("head", None),
            P(),
            P(None, "head"),
            P(None, "head"),
            P("head", None),
            P("seq", None),
        ),
        out_specs=(
            P("seq", None),
            P("seq", None),
            P("seq"),
            P("seq", "head"),
            P("seq", "head"),
            P("seq", "head"),
            P("seq", "head"),
            P("head"),
            P(None, "head"),
            P(None, "head"),
            P(None, "head"),
            P(),
            P("head", "seq"),
            P("seq"),
            P("seq", "head"),
            P("seq", "head"),
            P("head", "seq"),
        ),
        check_vma=False,
    )
```

profile of v0, /device:TPU:0, one launch (start us, length us, event | category | flops | bytes accessed | tf_op | source)
XLA Modules:
  0.0 3122.2 jit_solution(4417089619876002499)
XLA Ops:
  95.4 372.8 %while.81 = (s32[]{:T(128)}, f32[4,128,128]{2,1,0:T(8,128)S(1)}, f32[4,128,128]{2,1,0:T(8,128)S(1)}, f32[16,64,4,128]{3,1,0,2:T(8,128)}, f32[16,64,4,128]{3,1,2,...) while((s32[]{:T(128)}, f32[4,128,128]{2,1,0:T(8,128)S(1)}, ...), condition=%wide.region_7.8_spmd.clone.clone, body=%wide.region_6.7_spmd.clone.clone.sunk | while | flops 630079488 | bytes 9499862 | solution.py:161
  472.9 45.7 %all-gather.9.cloned.1.call-done = f32[32,128,128]{2,1,0:T(8,128)} async-done(((f32[4,128,128]{2,1,0:T(8,128)}), f32[32,128,128]{2,1,0:T(8,128)}) %all-gather.9.cloned.1.call-update) | async-done | bytes 2097168 | tf_op jit(solution)/shard_map/all_gather | solution.py:21
  518.6 50.5 %all-gather.11.cloned.1.call-done = f32[32,128,128]{2,1,0:T(8,128)} async-done(((f32[4,128,128]{2,1,0:T(8,128)}), f32[32,128,128]{2,1,0:T(8,128)}) %all-gather.11.cloned.1.call-update) | async-done | bytes 2097168 | tf_op jit(solution)/shard_map/all_gather | solution.py:21
  569.2 12.1 while.79
  599.3 151.4 %all-reduce.36.cloned.1.call-done = f32[1024,2048]{1,0:T(8,128)} async-done(((f32[1024,2048]{1,0:T(8,128)}), f32[1024,2048]{1,0:T(8,128)}) %all-reduce.36.cloned.1.call-update) | async-done | bytes 8388624 | tf_op jit(solution)/shard_map/psum | solution.py:277
  765.1 12.2 fusion.280
  785.8 17.1 multiply_convert_fusion.2
  825.5 151.3 %all-reduce.38.cloned.1.call-done = f32[1024,2048]{1,0:T(8,128)} async-done(((f32[1024,2048]{1,0:T(8,128)}), f32[1024,2048]{1,0:T(8,128)}) %all-reduce.38.cloned.1.call-update) | async-done | bytes 8388624 | tf_op jit(solution)/shard_map/psum | solution.py:299
  1031.0 48.3 %all-gather.15.cloned.1.call-done = f32[32,128,128]{2,1,0:T(8,128)} async-done(((f32[4,128,128]{2,1,0:T(8,128)}), f32[32,128,128]{2,1,0:T(8,128)}) %all-gather.15.cloned.1.call-update) | async-done | bytes 2097168 | tf_op jit(solution)/shard_map/all_gather | solution.py:21
  1079.3 11.9 while.80
  1097.5 644.8 %while.78 = (s32[]{:T(128)}, f32[4,128,128]{2,1,0:T(8,128)S(1)}, f32[4,128,128]{2,1,0:T(8,128)S(1)}, f32[16,64,4,128]{3,1,2,0:T(8,128)}, f32[16,64,4,128]{3,1,2,...) while((s32[]{:T(128)}, f32[4,128,128]{2,1,0:T(8,128)S(1)}, ...), condition=%wide.region_22.23_spmd.clone, body=%wide.region_19.22_spmd.clone.sunk | while | flops 1612758784 | bytes 30435932 | solution.py:161
  1870.1 12.5 fusion.287
  1882.9 11.9 fusion.206
  1905.1 250.5 %all-reduce.40.cloned.1.call-done = (f32[1024,2048]{1,0:T(8,128)}, f32[1024,2048]{1,0:T(8,128)}) async-done(((f32[1024,2048]{1,0:T(8,128)}, f32[1024,2048]{1,0:T(8,128)}), (f32[1024,2048]{1,0:T(8,128)}, f32[1024,2048]{1,0:T(8,128)})) %all-reduce.40.cloned.1.call-update) | async-done | bytes 16777232 | tf_op jit(solution)/shard_map/psum | solution.py:285
  2162.7 40.0 %all-reduce.30 = (f32[2048]{0:T(1024)S(1)}, f32[4]{0:T(128)}, f32[4,512]{1,0:T(4,128)}, f32[4,512]{1,0:T(4,128)}, f32[4,512]{1,0:T(4,128)}, /*index=5*/f32[128]{0:T(128)}, f32[2048]{0:T(1024)S(1)}) all-reduce(f32[2048]{0:T(1024)S(1)} %get-tuple-element.1225, f32[4]{0:T(128)S(1)} %fusion.246, ...), channel_id=6, replica_groups=mesh['seq'=8,'head'=4] {'seq'}, use_global_device_ids=true, to_apply=%region_28.29.clone | all-reduce | flops 10372 | bytes 82976
  2203.9 12.0 add.543
  2216.0 13.0 fusion.185
  2229.0 20.7 reduce-scatter.17.cloned.1.call-done
  2249.7 91.7 %reduce-scatter.11.cloned.1.call-done = f32[256,512]{1,0:T(8,128)} async-done(((f32[2048,512]{1,0:T(8,128)}), f32[256,512]{1,0:T(8,128)}) %reduce-scatter.11.cloned.1.call-update) | async-done | bytes 524304 | tf_op jit(solution)/shard_map/reduce_scatter | solution.py:353
  2341.4 92.4 %reduce-scatter.13.cloned.1.call-done = f32[256,512]{1,0:T(8,128)} async-done(((f32[2048,512]{1,0:T(8,128)}), f32[256,512]{1,0:T(8,128)}) %reduce-scatter.13.cloned.1.call-update) | async-done | bytes 524304 | tf_op jit(solution)/shard_map/reduce_scatter | solution.py:354
  2433.8 91.8 %reduce-scatter.15.cloned.1.call-done = f32[256,512]{1,0:T(8,128)} async-done(((f32[2048,512]{1,0:T(8,128)}), f32[256,512]{1,0:T(8,128)}) %reduce-scatter.15.cloned.1.call-update) | async-done | bytes 524304 | tf_op jit(solution)/shard_map/reduce_scatter | solution.py:355
  2525.6 196.9 %reduce-scatter.19.cloned.1.call-done = f32[256,1408]{1,0:T(8,128)} async-done(((f32[2048,1408]{1,0:T(8,128)}), f32[256,1408]{1,0:T(8,128)}) %reduce-scatter.19.cloned.1.call-update) | async-done | bytes 1441808 | tf_op jit(solution)/shard_map/reduce_scatter | solution.py:358
  2722.5 196.3 %reduce-scatter.21.cloned.1.call-done = f32[256,1408]{1,0:T(8,128)} async-done(((f32[2048,1408]{1,0:T(8,128)}), f32[256,1408]{1,0:T(8,128)}) %reduce-scatter.21.cloned.1.call-update) | async-done | bytes 1441808 | tf_op jit(solution)/shard_map/reduce_scatter | solution.py:359
  2918.8 196.7 %reduce-scatter.23.cloned.1.call-done = f32[1408,256]{1,0:T(8,128)} async-done(((f32[1408,2048]{1,0:T(8,128)}), f32[1408,256]{1,0:T(8,128)}) %reduce-scatter.23.cloned.1.call-update) | async-done | bytes 1441808 | tf_op jit(solution)/shard_map/reduce_scatter | solution.py:360
  (2671 shorter events, 1387.7 us)
Async XLA Ops:
  7.2 586.3 %copy-start = (bf16[512,2048]{1,0:T(8,128)(2,1)S(1)}, bf16[512,2048]{1,0:T(8,128)(2,1)}, u32[]{:S(2)}) copy-start(bf16[512,2048]{1,0:T(8,128)(2,1)} %param.38) | copy-start | bytes 6291460
  7.2 511.4 %all-gather.9.cloned.1.call-start = ((), (), s32[]{:S(2)}) async-start(), calls=%async_computation.17 | async-start | bytes 2359296 | tf_op jit(solution)/shard_map/all_gather | solution.py:21
  24.5 12.9 collective-permute-start
  32.3 43.3 %copy-start.64 = (f32[1024]{0:T(1024)}, f32[1024]{0:T(1024)S(1)}, u32[]{:S(2)}) copy-start(f32[1024]{0:T(1024)S(1)} %get-tuple-element.1399) | copy-start | bytes 12292
  95.4 374.4 %copy-start.120 = (f32[128]{0:T(128)S(1)}, f32[128]{0:T(128)}, u32[]{:S(2)}) copy-start(f32[128]{0:T(128)} %param.37) | copy-start | bytes 1540
  468.9 100.2 %all-gather.11.cloned.1.call-start = ((), (), s32[]{:S(2)}) async-start(), calls=%async_computation.18 | async-start | bytes 2359296 | tf_op jit(solution)/shard_map/all_gather | solution.py:21
  469.7 281.1 %all-reduce.36.cloned.1.call-start = ((), (), s32[]{:S(2)}) async-start(), calls=%async_computation.8 | async-start | bytes 16777216 | tf_op jit(solution)/shard_map/psum | solution.py:277
  599.2 161.6 %copy-start.82 = (f32[2048]{0:T(1024)S(1)}, f32[2048]{0:T(1024)}, u32[]{:S(2)}) copy-start(f32[2048]{0:T(1024)} %param.39) | copy-start | bytes 24580
  599.3 377.6 %all-reduce.38.cloned.1.call-start = ((), (), s32[]{:S(2)}) async-start(), calls=%async_computation.9 | async-start | bytes 16777216 | tf_op jit(solution)/shard_map/psum | solution.py:299
  823.7 207.3 %all-gather.13.cloned.1.call-start = ((), (), s32[]{:S(2)}) async-start(), calls=%async_computation.19 | async-start | bytes 2359296 | tf_op jit(solution)/shard_map/all_gather | solution.py:21
  825.5 253.8 %all-gather.15.cloned.1.call-start = ((), (), s32[]{:S(2)}) async-start(), calls=%async_computation.20 | async-start | bytes 2359296 | tf_op jit(solution)/shard_map/all_gather | solution.py:21
  1012.4 891.1 %reduce-scatter.25.cloned.1.call-start = ((), (), s32[]{:S(2)}) async-start(), calls=%async_computation.21 | async-start | bytes 1179648
  1792.4 8.0 collective-permute-start.1
  1800.4 355.3 %all-reduce.40.cloned.1.call-start = ((), (), s32[]{:S(2)}) async-start(), calls=%async_computation.22 | async-start | bytes 33554432 | tf_op jit(solution)/shard_map/psum | solution.py:285
  1827.8 421.9 %reduce-scatter.17.cloned.1.call-start = ((), (), s32[]{:S(2)}) async-start(), calls=%async_computation.13 | async-start | bytes 4718592 | tf_op jit(solution)/shard_map/reduce_scatter | solution.py:357
  1836.8 504.6 %reduce-scatter.11.cloned.1.call-start = ((), (), s32[]{:S(2)}) async-start(), calls=%async_computation.10 | async-start | bytes 4718592 | tf_op jit(solution)/shard_map/reduce_scatter | solution.py:353
  1843.9 589.9 %reduce-scatter.13.cloned.1.call-start = ((), (), s32[]{:S(2)}) async-start(), calls=%async_computation.11 | async-start | bytes 4718592 | tf_op jit(solution)/shard_map/reduce_scatter | solution.py:354
  1851.0 674.6 %reduce-scatter.15.cloned.1.call-start = ((), (), s32[]{:S(2)}) async-start(), calls=%async_computation.12 | async-start | bytes 4718592 | tf_op jit(solution)/shard_map/reduce_scatter | solution.py:355
  1858.1 864.4 %reduce-scatter.19.cloned.1.call-start = ((), (), s32[]{:S(2)}) async-start(), calls=%async_computation.14 | async-start | bytes 12976128 | tf_op jit(solution)/shard_map/reduce_scatter | solution.py:358
  1870.1 1048.7 %reduce-scatter.21.cloned.1.call-start = ((), (), s32[]{:S(2)}) async-start(), calls=%async_computation.15 | async-start | bytes 12976128 | tf_op jit(solution)/shard_map/reduce_scatter | solution.py:359
  1882.6 1232.8 %reduce-scatter.23.cloned.1.call-start = ((), (), s32[]{:S(2)}) async-start(), calls=%async_computation.16 | async-start | bytes 12976128 | tf_op jit(solution)/shard_map/reduce_scatter | solution.py:360
  1894.8 260.8 %copy-start.84 = (f32[2048]{0:T(1024)S(1)}, f32[2048]{0:T(1024)}, u32[]{:S(2)}) copy-start(f32[2048]{0:T(1024)} %param.28) | copy-start | bytes 24580
  1894.9 260.8 %copy-start.88 = (f32[1024]{0:T(1024)S(1)}, f32[1024]{0:T(1024)}, u32[]{:S(2)}) copy-start(f32[1024]{0:T(1024)} %copy-done.87) | copy-start | bytes 12292
  2216.0 899.5 %copy-start.1 = (bf16[512,2048]{1,0:T(8,128)(2,1)S(1)}, bf16[512,2048]{1,0:T(8,128)(2,1)}, u32[]{:S(2)}) copy-start(bf16[512,2048]{1,0:T(8,128)(2,1)} %param.38) | copy-start | bytes 6291460
  (306 other events, 1580.1 us)
Sparse Core Ops, SparseCore 0:
  469.0 49.5 all-gather.8
  521.3 47.7 all-gather.10
  599.4 151.3 all-reduce.35
  823.8 153.0 all-reduce.37
  979.4 49.4 all-gather.12
  1031.4 47.8 all-gather.14
  1800.5 63.6 reduce-scatter.24
  1867.6 287.9 all-reduce.39
  2160.3 89.3 reduce-scatter.16
  2253.7 87.6 reduce-scatter.10
  2346.1 87.6 reduce-scatter.12
  2437.9 87.6 reduce-scatter.14
  2530.1 192.2 reduce-scatter.18
  2726.9 191.7 reduce-scatter.20
  2923.2 192.1 reduce-scatter.22
where the time goes:
time: 3140 us; the launch traced here: 3120 us
  waiting for transfers between devices  1590 us (51%)
  matrix products  942 us (30%)
  local copies, waits for them, and re-layouts  320 us (10%)
  other arithmetic  190 us (6%)
  blocking collectives  46.6 us (1%)
    psum x1, waiting for transfers between devices, shards(): lax.psum(jnp.dot(active, w_down, preferred_element_type=jnp.float32), 'he...  251 us
    reduce_scatter x1, waiting for transfers between devices, shards(): lax.psum_scatter(gate_term, 'seq', scatter_dimension=0, tiled=True)  197 us
    reduce_scatter x1, waiting for transfers between devices, shards(): lax.psum_scatter(down_term, 'seq', scatter_dimension=1, tiled=True)  197 us
    reduce_scatter x1, waiting for transfers between devices, shards(): lax.psum_scatter(up_term, 'seq', scatter_dimension=0, tiled=True)  196 us
    psum x1, waiting for transfers between devices, shards(): lax.psum(jnp.dot(headed, w_output, preferred_element_type=jnp.float32), '...  151 us
    psum x1, waiting for transfers between devices, shards(): normed_two_grad = lax.psum(two_part, 'head')  151 us
    all_gather x4, waiting for transfers between devices, entering(): everything = jax.tree.map(lambda part: lax.all_gather(part, axis), shard)  145 us
    dot_general x320, matrix products, nilpotent_inverse(): jnp.einsum('hij,hjk->hik', inverse, eye_block + square, precision=HIGH)  128 us
  transfers between devices with their start and end apart: 17, of which 13 were waited for; matrix products, arithmetic and copies ran while one was open for 6% of the time, Pallas kernels for 0%

commit v1 on v0

v1 whole, which is shorter than its diff:
```python
import jax
import jax.numpy as jnp
from jax import lax
from jax.experimental import pallas as pl
from jax.experimental.pallas import tpu as pltpu
from jax.sharding import PartitionSpec as P

BLOCK = 128
SUB = 32
EDGE = 8
F32 = jnp.float32
BF16 = jnp.bfloat16


def mm(left, right, left_dim=1, right_dim=0, passes=3):
    dims = (((left_dim,), (right_dim,)), ((), ()))
    if passes == 1:
        return lax.dot_general(
            left.astype(BF16), right.astype(BF16), dims, preferred_element_type=F32
        )
    precision = lax.Precision.HIGH if passes == 3 else lax.Precision.HIGHEST
    return lax.dot_general(left, right, dims, precision=precision, preferred_element_type=F32)


def doc_of(places, starts, count):
    total = jnp.full(places.shape, -1, jnp.int32) if places.shape else jnp.int32(-1)
    for index in range(count):
        total = total + jnp.where(starts[index] <= places, 1, 0).astype(jnp.int32)
    return total


def sigmoid(value):
    return 1.0 / (1.0 + jnp.exp(-value))


def block_masks(first, starts, count):
    rows = lax.broadcasted_iota(jnp.int32, (BLOCK, BLOCK), 0)
    columns = lax.broadcasted_iota(jnp.int32, (BLOCK, BLOCK), 1)
    row_docs = doc_of(first + rows, starts, count)
    column_docs = doc_of(first + columns, starts, count)
    same = row_docs == column_docs
    prior_doc = doc_of(first - 1, starts, count)
    last_doc = doc_of(first + BLOCK - 1, starts, count)
    carried = (row_docs == prior_doc).astype(F32)
    final = (row_docs == last_doc).astype(F32)
    through = jnp.where(prior_doc == last_doc, 1.0, 0.0).astype(F32)
    reach = [None]
    for back in range(1, 4):
        reach.append((row_docs == doc_of(first - back + rows, starts, count)).astype(F32))
    return rows, columns, same, carried, final, through, reach


def short_conv(joined, taps, reach):
    total = taps[3:4] * joined[EDGE:]
    for back in range(1, 4):
        total = total + taps[3 - back : 4 - back] * (
            joined[EDGE - back : EDGE - back + BLOCK] * reach[back]
        )
    return total


def block_inverse(strict, rows, columns, passes=3):
    near = jnp.where(rows // SUB == columns // SUB, strict, 0.0)
    far = strict - near
    eye = jnp.where(rows == columns, 1.0, 0.0)
    inverse = eye - near
    power = mm(near, near, passes=passes)
    covered = 2
    while covered * 2 < SUB:
        both = mm(jnp.concatenate([power, inverse], axis=0), power, passes=passes)
        power, inverse = both[:BLOCK], inverse + both[BLOCK:]
        covered *= 2
    inverse = inverse + mm(inverse, power, passes=passes)
    chain = mm(inverse, far, passes=passes)
    both = mm(chain, jnp.concatenate([inverse, chain], axis=1), passes=passes)
    partial = inverse - both[:, :BLOCK]
    return partial + mm(both[:, BLOCK:], partial, passes=passes)


def forward_kernel(
    starts,
    base,
    lin_query,
    lin_key,
    lin_value,
    edge,
    taps_query,
    taps_key,
    taps_value,
    rates,
    inverse_out,
    effective_out,
    local_out,
    memory_out,
    final_out,
    before,
    memory,
):
    heads, size = memory.shape[0], memory.shape[1]
    width = heads * size
    step = pl.program_id(0)
    count = starts.shape[0]

    @pl.when(step == 0)
    def _():
        before[...] = edge[...]
        line = lax.broadcasted_iota(jnp.int32, (size, 2 * size), 0)
        lane = lax.broadcasted_iota(jnp.int32, (size, 2 * size), 1)
        start = jnp.where(line == lane, 1.0, 0.0).astype(F32)
        for head in range(heads):
            memory[head] = start

    first = base[0] + step * BLOCK
    rows, columns, same, carried, final, through, reach = block_masks(first, starts, count)
    below = jnp.logical_and(same, columns < rows)
    upto = jnp.logical_and(same, columns <= rows)
    for head in range(heads):
        span = slice(head * size, (head + 1) * size)
        pieces = []
        for number, (lin, taps) in enumerate(
            ((lin_query, taps_query), (lin_key, taps_key), (lin_value, taps_value))
        ):
            place = slice(number * width + head * size, number * width + (head + 1) * size)
            joined = jnp.concatenate([before[:, place], lin[:, span]], axis=0)
            conv = short_conv(joined, taps[:, span], reach)
            pieces.append(conv * sigmoid(conv))
        query = pieces[0] * lax.rsqrt(jnp.sum(pieces[0] * pieces[0], axis=1, keepdims=True) + 1e-6)
        key = pieces[1] * lax.rsqrt(jnp.sum(pieces[1] * pieces[1], axis=1, keepdims=True) + 1e-6)
        value = pieces[2]
        rate = jnp.broadcast_to(rates[:, head : head + 1], (BLOCK, size))
        products = mm(jnp.concatenate([query, key], axis=0), key, 1, 1)
        scores = jnp.where(upto, products[:BLOCK], 0.0)
        strict = jnp.where(below, products[BLOCK:] * rate, 0.0)
        inverse = block_inverse(strict, rows, columns)
        inverse_out[0, head] = inverse
        writes = mm(inverse, jnp.concatenate([rate * carried * key, rate * value], axis=1))
        held = memory[head]
        memory_out[0, head] = held
        read = mm(jnp.concatenate([writes[:, :size], carried * query], axis=0), held)
        residue = (
            jnp.concatenate([jnp.zeros((BLOCK, size), F32), writes[:, size:]], axis=1)
            - read[:BLOCK]
        )
        result = read[BLOCK:] + mm(scores, residue)
        effective_out[:, span] = result[:, :size]
        local_out[:, span] = result[:, size:]
        updated = through * held + mm(final * key, residue, 0, 0)
        memory[head] = updated
        final_out[head] = updated
    for number, lin in enumerate((lin_query, lin_key, lin_value)):
        before[:, number * width : (number + 1) * width] = lin[BLOCK - EDGE :, :]


def output_kernel(effective, local, entering, gain, mixed_out, headed_out):
    heads, size = entering.shape[0], entering.shape[1]
    for head in range(heads):
        span = slice(head * size, (head + 1) * size)
        mixed = local[:, span] + mm(effective[:, span], entering[head])
        mixed_out[:, span] = mixed
        scale = lax.rsqrt(jnp.mean(mixed * mixed, axis=1, keepdims=True) + 1e-5)
        headed_out[:, span] = (mixed * scale * gain[...]).astype(headed_out.dtype)


def norm_back_kernel(headed_grad, mixed_rows, effective, gain, grad_out, gain_out, local_out):
    heads, size = local_out.shape[0], local_out.shape[1]
    step = pl.program_id(0)

    @pl.when(step == 0)
    def _():
        gain_out[...] = jnp.zeros_like(gain_out)
        local_out[...] = jnp.zeros_like(local_out)

    for head in range(heads):
        span = slice(head * size, (head + 1) * size)
        mixed = mixed_rows[:, span]
        scale = lax.rsqrt(jnp.mean(mixed * mixed, axis=1, keepdims=True) + 1e-5)
        given = headed_grad[:, span]
        gain_out[...] += jnp.sum(given * mixed * scale, axis=0, keepdims=True)
        scaled = gain[...] * given
        along = jnp.mean(mixed * scaled, axis=1, keepdims=True)
        grad = scale * scaled - mixed * (scale * scale * scale * along)
        grad_out[:, span] = grad
        local_out[head] += mm(effective[:, span], grad, 0, 0)


def backward_kernel(
    starts,
    base,
    lin_query,
    lin_key,
    lin_value,
    prior_query,
    prior_key,
    prior_value,
    edge,
    taps_query,
    taps_key,
    taps_value,
    rates,
    inverse_in,
    memory_in,
    entering,
    leaving,
    mixed_grad,
    query_out,
    key_out,
    value_out,
    edge_out,
    logit_out,
    taps_query_out,
    taps_key_out,
    taps_value_out,
    after,
    memory_grad,
):
    heads, size = entering.shape[0], entering.shape[1]
    width = heads * size
    step = pl.program_id(0)
    blocks = pl.num_programs(0)
    here = blocks - 1 - step
    count = starts.shape[0]

    @pl.when(step == 0)
    def _():
        after[...] = jnp.zeros_like(after)
        memory_grad[...] = leaving[...]
        taps_query_out[...] = jnp.zeros_like(taps_query_out)
        taps_key_out[...] = jnp.zeros_like(taps_key_out)
        taps_value_out[...] = jnp.zeros_like(taps_value_out)

    first = base[0] + here * BLOCK
    rows, columns, same, carried, final, through, reach = block_masks(first, starts, count)
    below = jnp.logical_and(same, columns < rows)
    upto = jnp.logical_and(same, columns <= rows)
    lanes = lax.broadcasted_iota(jnp.int32, (BLOCK, rates.shape[1]), 1)
    logit_grad = jnp.zeros((BLOCK, rates.shape[1]), F32)
    for head in range(heads):
        span = slice(head * size, (head + 1) * size)
        joins, convs, gates, pieces = [], [], [], []
        for number, (lin, prior, taps) in enumerate(
            (
                (lin_query, prior_query, taps_query),
                (lin_key, prior_key, taps_key),
                (lin_value, prior_value, taps_value),
            )
        ):
            place = slice(number * width + head * size, number * width + (head + 1) * size)
            border = jnp.where(here == 0, edge[:, place], prior[:, span])
            joined = jnp.concatenate([border, lin[:, span]], axis=0)
            conv = short_conv(joined, taps[:, span], reach)
            gate = sigmoid(conv)
            joins.append(joined)
            convs.append(conv)
            gates.append(gate)
            pieces.append(conv * gate)
        query_scale = lax.rsqrt(jnp.sum(pieces[0] * pieces[0], axis=1, keepdims=True) + 1e-6)
        key_scale = lax.rsqrt(jnp.sum(pieces[1] * pieces[1], axis=1, keepdims=True) + 1e-6)
        query = pieces[0] * query_scale
        key = pieces[1] * key_scale
        value = pieces[2]
        rate_column = rates[:, head : head + 1]
        rate = jnp.broadcast_to(rate_column, (BLOCK, size))
        products = mm(jnp.concatenate([query, key], axis=0), key, 1, 1)
        scores = jnp.where(upto, products[:BLOCK], 0.0)
        gram = products[BLOCK:]
        inverse = inverse_in[0, head]
        held = memory_in[0, head]
        memory = mm(held[:, :size], entering[head]) + held[:, size:]
        left = carried * key
        wanted = value - mm(left, memory)
        residue = mm(inverse, rate * wanted)
        grad_out = mixed_grad[:, span]
        grad_memory = memory_grad[head]
        last_keys = final * key
        residue_grad = mm(scores, grad_out, 0, 0) + mm(last_keys, grad_memory)
        solved_grad = mm(inverse, residue_grad, 0, 0)
        wanted_grad = rate * solved_grad
        outer = mm(jnp.concatenate([grad_out, solved_grad], axis=0), residue, 1, 1)
        scores_grad = jnp.where(upto, outer[:BLOCK], 0.0)
        strict_grad = jnp.where(below, -outer[BLOCK:], 0.0)
        gram_grad = rate * strict_grad
        rate_grad = jnp.sum(solved_grad * wanted + strict_grad * gram, axis=1, keepdims=True)
        state_side = mm(jnp.concatenate([grad_out, wanted_grad], axis=0), memory, 1, 1)
        key_side = mm(jnp.concatenate([scores_grad, gram_grad], axis=0), key)
        query_grad = carried * state_side[:BLOCK] + key_side[:BLOCK]
        key_grad = (
            key_side[BLOCK:]
            - carried * state_side[BLOCK:]
            + mm(
                jnp.concatenate([scores_grad, gram_grad], axis=0),
                jnp.concatenate([query, key], axis=0),
                0,
                0,
            )
            + final * mm(residue, grad_memory, 1, 1)
        )
        memory_grad[head] = through * grad_memory + mm(
            jnp.concatenate([carried * query, -left], axis=0),
            jnp.concatenate([grad_out, wanted_grad], axis=0),
            0,
            0,
        )
        logit_grad = jnp.where(
            lanes == head, rate_grad * rate_column * (1.0 - rate_column), logit_grad
        )
        query_grad = query_scale * (
            query_grad - query * jnp.sum(query * query_grad, axis=1, keepdims=True)
        )
        key_grad = key_scale * (key_grad - key * jnp.sum(key * key_grad, axis=1, keepdims=True))
        for number, (grad, taps, lin_out, taps_out) in enumerate(
            (
                (query_grad, taps_query, query_out, taps_query_out),
                (key_grad, taps_key, key_out, taps_key_out),
                (wanted_grad, taps_value, value_out, taps_value_out),
            )
        ):
            place = slice(number * width + head * size, number * width + (head + 1) * size)
            gate, conv, joined = gates[number], convs[number], joins[number]
            conv_grad = grad * gate * (1.0 + conv * (1.0 - gate))
            spare = jnp.zeros((EDGE, size), F32)
            lin_grad = taps[3:4, span] * conv_grad
            tail = jnp.zeros((EDGE, size), F32)
            taps_grad = [jnp.sum(conv_grad * joined[EDGE:], axis=0, keepdims=True)]
            for back in range(1, 4):
                part = conv_grad * reach[back]
                tap = taps[3 - back : 4 - back, span]
                lin_grad = lin_grad + tap * jnp.concatenate([part, spare], axis=0)[
                    back : back + BLOCK
                ]
                tail = tail + tap * jnp.concatenate([spare, part[:EDGE]], axis=0)[
                    back : back + EDGE
                ]
                taps_grad.append(
                    jnp.sum(part * joined[EDGE - back : EDGE - back + BLOCK], axis=0, keepdims=True)
                )
            taps_out[:, span] += jnp.concatenate(taps_grad[::-1], axis=0)
            carry = jnp.concatenate(
                [jnp.zeros((BLOCK - EDGE, size), F32), after[:, place]], axis=0
            )
            lin_out[:, span] = lin_grad + carry
            after[:, place] = tail
            edge_out[:, place] = tail
    logit_out[...] = logit_grad


def on_chip(kernel, name, **settings):
    return pl.pallas_call(
        kernel,
        name=name,
        compiler_params=pltpu.CompilerParams(
            dimension_semantics=("arbitrary",), vmem_limit_bytes=48 * 1024 * 1024
        ),
        **settings,
    )


def whole(shape):
    return pl.BlockSpec(shape, lambda i: (0,) * len(shape))


def scalars():
    return pl.BlockSpec(memory_space=pltpu.SMEM)


def delta_forward(starts, base, lins, edge, taps, rates, heads, size):
    length, width = lins[0].shape
    blocks = length // BLOCK
    row_block = pl.BlockSpec((BLOCK, width), lambda i: (i, 0))
    return on_chip(
        forward_kernel,
        "delta_forward",
        grid=(blocks,),
        in_specs=[scalars(), scalars()]
        + [row_block] * 3
        + [whole((EDGE, 3 * width))]
        + [whole((4, width))] * 3
        + [pl.BlockSpec((BLOCK, heads), lambda i: (i, 0))],
        out_specs=[
            pl.BlockSpec((1, heads, BLOCK, BLOCK), lambda i: (i, 0, 0, 0)),
            row_block,
            row_block,
            pl.BlockSpec((1, heads, size, 2 * size), lambda i: (i, 0, 0, 0)),
            whole((heads, size, 2 * size)),
        ],
        out_shape=[
            jax.ShapeDtypeStruct((blocks, heads, BLOCK, BLOCK), F32),
            jax.ShapeDtypeStruct((length, width), F32),
            jax.ShapeDtypeStruct((length, width), F32),
            jax.ShapeDtypeStruct((blocks, heads, size, 2 * size), F32),
            jax.ShapeDtypeStruct((heads, size, 2 * size), F32),
        ],
        scratch_shapes=[
            pltpu.VMEM((EDGE, 3 * width), F32),
            pltpu.VMEM((heads, size, 2 * size), F32),
        ],
    )(starts, base, *lins, edge, *taps, rates)


def delta_output(effective, local, entering, gain):
    length, width = local.shape
    heads, size = entering.shape[0], entering.shape[1]
    rows = min(length, 256)
    row_block = pl.BlockSpec((rows, width), lambda i: (i, 0))
    return on_chip(
        output_kernel,
        "delta_output",
        grid=(length // rows,),
        in_specs=[row_block, row_block, whole((heads, size, size)), whole((1, size))],
        out_specs=[row_block, row_block],
        out_shape=[
            jax.ShapeDtypeStruct((length, width), F32),
            jax.ShapeDtypeStruct((length, width), BF16),
        ],
    )(effective, local, entering, gain)


def norm_back(headed_grad, mixed_rows, effective, gain, heads, size):
    length, width = headed_grad.shape
    rows = min(length, 256)
    row_block = pl.BlockSpec((rows, width), lambda i: (i, 0))
    return on_chip(
        norm_back_kernel,
        "norm_back",
        grid=(length // rows,),
        in_specs=[row_block, row_block, row_block, whole((1, size))],
        out_specs=[row_block, whole((1, size)), whole((heads, size, size))],
        out_shape=[
            jax.ShapeDtypeStruct((length, width), F32),
            jax.ShapeDtypeStruct((1, size), F32),
            jax.ShapeDtypeStruct((heads, size, size), F32),
        ],
    )(headed_grad, mixed_rows, effective, gain)


def delta_backward(
    starts, base, lins, edge, taps, rates, inverse, memories, entering, leaving, mixed_grad
):
    length, width = lins[0].shape
    heads, size = entering.shape[0], entering.shape[1]
    blocks = length // BLOCK
    ratio = BLOCK // EDGE
    row_block = pl.BlockSpec((BLOCK, width), lambda i: (blocks - 1 - i, 0))
    prior = pl.BlockSpec(
        (EDGE, width), lambda i: (jnp.maximum((blocks - 1 - i) * ratio - 1, 0), 0)
    )
    rate_block = pl.BlockSpec((BLOCK, heads), lambda i: (blocks - 1 - i, 0))
    return on_chip(
        backward_kernel,
        "delta_backward",
        grid=(blocks,),
        in_specs=[scalars(), scalars()]
        + [row_block] * 3
        + [prior] * 3
        + [whole((EDGE, 3 * width))]
        + [whole((4, width))] * 3
        + [
            rate_block,
            pl.BlockSpec((1, heads, BLOCK, BLOCK), lambda i: (blocks - 1 - i, 0, 0, 0)),
            pl.BlockSpec((1, heads, size, 2 * size), lambda i: (blocks - 1 - i, 0, 0, 0)),
            whole((heads, size, size)),
            whole((heads, size, size)),
            row_block,
        ],
        out_specs=[row_block] * 3
        + [whole((EDGE, 3 * width)), rate_block]
        + [whole((4, width))] * 3,
        out_shape=[jax.ShapeDtypeStruct((length, width), F32)] * 3
        + [
            jax.ShapeDtypeStruct((EDGE, 3 * width), F32),
            jax.ShapeDtypeStruct((length, heads), F32),
        ]
        + [jax.ShapeDtypeStruct((4, width), F32)] * 3,
        scratch_shapes=[
            pltpu.VMEM((EDGE, 3 * width), F32),
            pltpu.VMEM((heads, size, size), F32),
        ],
    )(starts, base, *lins, *lins, edge, *taps, rates, inverse, memories, entering, leaving, mixed_grad)


def swap(block, axis, bit):
    count = lax.axis_size(axis)
    return lax.ppermute(block, axis, [(i, i ^ bit) for i in range(count)])


def shift(block, axis, distance):
    devices = range(lax.axis_size(axis))
    route = [(i - distance, i) for i in devices if i - distance in devices]
    return lax.ppermute(block, axis, route)


def sum_over_head(term):
    if lax.axis_size("head") != 4:
        return lax.psum(term, "head")
    odd = lax.axis_index("head") % 2
    half = term.shape[0] // 2
    keep = lax.dynamic_slice_in_dim(term, odd * half, half, 0)
    send = lax.dynamic_slice_in_dim(term, (1 - odd) * half, half, 0)
    part = keep + swap(send, "head", 1)
    part = part + swap(part, "head", 2)
    other = swap(part, "head", 1)
    return jnp.where(
        odd == 0,
        jnp.concatenate([part, other], axis=0),
        jnp.concatenate([other, part], axis=0),
    )


def relative_order(bits):
    if not bits:
        return [0]
    rest = relative_order(bits[1:])
    return [index ^ bits[0] for index in rest] + rest


def seq_bits(late):
    bits = []
    while 1 << len(bits) < lax.axis_size("seq"):
        bits.append(1 << len(bits))
    return bits[1:] + bits[:1] if late else bits


def arranged(rows, late=False):
    here = lax.axis_index("seq")
    size = rows.shape[1] // lax.axis_size("seq")
    return jnp.concatenate(
        [
            lax.dynamic_slice_in_dim(rows, (here ^ index) * size, size, 1)
            for index in relative_order(seq_bits(late))
        ],
        axis=1,
    )


def token_sum(rows, others, rows_first=True, late=False):
    half = rows.shape[1] // 2
    dim = 0 if rows_first else 1

    def product(piece):
        left, right = (piece, others) if rows_first else (others, piece)
        return lax.dot_general(
            left, right, (((0,), (0,)), ((), ())), preferred_element_type=F32
        )

    bits = seq_bits(late)
    given = product(rows[:, :half])
    kept = product(rows[:, half:])
    for place, bit in enumerate(bits):
        kept = kept + swap(given, "seq", bit)
        if place + 1 < len(bits):
            size = kept.shape[dim] // 2
            given = lax.slice_in_dim(kept, 0, size, axis=dim)
            kept = lax.slice_in_dim(kept, size, 2 * size, axis=dim)
    return kept


def chain(transfer, offset, distance):
    hops = max(lax.axis_size("seq") // 2, 1)
    state = shift(offset, "seq", distance)
    for _ in range(hops - 1):
        moved = jnp.einsum("hij,hjk->hik", transfer, state, precision=lax.Precision.HIGH) + offset
        state = shift(moved, "seq", distance)
    return state


def row_norm(values):
    return lax.rsqrt(jnp.mean(values * values, axis=-1, keepdims=True) + 1e-05)


def matmul(left, right, left_dim=1, right_dim=0):
    return lax.dot_general(
        left, right, (((left_dim,), (right_dim,)), ((), ())), preferred_element_type=F32
    )


def norm_pull(grad, values, scale, gain):
    scaled = gain * grad
    along = jnp.mean(values * scaled, axis=-1, keepdims=True)
    return scale * scaled - values * (scale * scale * scale * along)


def shards(
    hidden,
    doc_starts,
    norm_gain,
    w_query,
    w_key,
    w_value,
    w_strength,
    strength_bias,
    conv_query,
    conv_key,
    conv_value,
    head_gain,
    w_output,
    ffn_gain,
    w_gate,
    w_up,
    w_down,
    out_grad,
):
    length = hidden.shape[0]
    size = head_gain.shape[0]
    heads = strength_bias.shape[0]
    width = heads * size
    seq_rank = lax.axis_index("seq")
    seq_count = lax.axis_size("seq")
    base = (seq_rank * length).astype(jnp.int32).reshape(1)
    taps = tuple(part.astype(F32) for part in (conv_query, conv_key, conv_value))
    gain = head_gain.reshape(1, size)

    scale_one = row_norm(hidden)
    normed = (hidden * scale_one * norm_gain).astype(BF16)
    lins = tuple(matmul(normed, part) for part in (w_query, w_key, w_value))
    tails = jnp.concatenate([part[-EDGE:] for part in lins], axis=1)
    edge = shift(tails, "seq", 1)
    rates = jax.nn.sigmoid(matmul(normed, w_strength) + strength_bias)
    inverse, effective, local, memories, last = delta_forward(
        doc_starts, base, lins, edge, taps, rates, heads, size
    )
    transfer, offset = last[:, :, :size], last[:, :, size:]
    entering = chain(transfer, offset, 1)
    mixed_rows, headed = delta_output(effective, local, entering, gain)

    middle = hidden + sum_over_head(matmul(headed, w_output))
    scale_two = row_norm(middle)
    normed_two = (middle * scale_two * ffn_gain).astype(BF16)
    gate_rows = matmul(normed_two, w_gate)
    upward = matmul(normed_two, w_up)
    sigma = jax.nn.sigmoid(gate_rows)
    silu_gate = gate_rows * sigma
    active = (silu_gate * upward).astype(BF16)
    ffn_cot = out_grad.astype(BF16)
    active_grad = matmul(ffn_cot, w_down, 1, 1)
    gate_cot = (active_grad * upward * sigma * (1.0 + gate_rows * (1.0 - sigma))).astype(BF16)
    up_cot = (active_grad * silu_gate).astype(BF16)
    two_part = matmul(gate_cot, w_gate, 1, 1) + matmul(up_cot, w_up, 1, 1)
    normed_two_grad = sum_over_head(two_part)
    middle_grad = out_grad + norm_pull(normed_two_grad, middle, scale_two, ffn_gain)
    ffn_gain_part = jnp.sum(normed_two_grad * middle * scale_two, axis=0)
    branch_cot = middle_grad.astype(BF16)
    headed_grad = matmul(branch_cot, w_output, 1, 1)

    normed_two_ordered = arranged(normed_two)
    w_gate_grad = token_sum(normed_two_ordered, gate_cot)
    w_up_grad = token_sum(normed_two_ordered, up_cot)
    w_down_grad = token_sum(arranged(ffn_cot), active, False)
    block_output = middle + sum_over_head(matmul(active, w_down))

    mixed_grad, head_gain_part, local_grad = norm_back(
        headed_grad, mixed_rows, effective, gain, heads, size
    )
    leaving = chain(jnp.transpose(transfer, (0, 2, 1)), local_grad, -1)
    back = delta_backward(
        doc_starts, base, lins, edge, taps, rates, inverse, memories, entering, leaving, mixed_grad
    )
    returned = shift(back[3], "seq", -1)
    cots = tuple(
        jnp.concatenate(
            [part[:-EDGE], part[-EDGE:] + returned[:, index * width : (index + 1) * width]], axis=0
        ).astype(BF16)
        for index, part in enumerate(back[:3])
    )
    logit_grad = back[4]
    strength_cot = logit_grad.astype(BF16)
    first_part = matmul(cots[0], w_query, 1, 1)
    first_part = first_part + matmul(cots[1], w_key, 1, 1)
    first_part = first_part + matmul(cots[2], w_value, 1, 1)
    first_part = first_part + matmul(strength_cot, w_strength, 1, 1)
    normed_grad = sum_over_head(first_part)
    hidden_grad = middle_grad + norm_pull(normed_grad, hidden, scale_one, norm_gain)
    norm_gain_part = jnp.sum(first_part * hidden * scale_one, axis=0)

    w_output_grad = token_sum(arranged(branch_cot), headed, False)
    normed_ordered = arranged(normed)
    lin_grads = tuple(token_sum(normed_ordered, part) for part in cots)
    strength_term = matmul(strength_cot, normed, 0, 0)

    small = jnp.concatenate(
        [strength_term.reshape(-1), ffn_gain_part]
        + [part.reshape(-1) for part in back[5:8]]
        + [jnp.sum(logit_grad, axis=0)]
    )
    small = lax.psum(small, "seq")
    features = norm_gain.shape[0]
    block = features // seq_count
    cut = [heads * features, features] + [4 * width] * 3 + [heads]
    parts, at = [], 0
    for extent in cut:
        parts.append(small[at : at + extent])
        at += extent
    shared = lax.psum(
        jnp.concatenate([norm_gain_part, head_gain_part.reshape(-1)]), ("seq", "head")
    )

    def own(vector, axis=0):
        return lax.dynamic_slice_in_dim(vector, seq_rank * block, block, axis)

    return (
        block_output,
        hidden_grad,
        own(shared[:features]),
        lin_grads[0],
        lin_grads[1],
        lin_grads[2],
        own(parts[0].reshape(heads, features), 1).T,
        parts[5],
        parts[2].reshape(4, width),
        parts[3].reshape(4, width),
        parts[4].reshape(4, width),
        shared[features:],
        w_output_grad,
        own(parts[1]),
        w_gate_grad,
        w_up_grad,
        w_down_grad,
    )


def solution(mesh):
    return jax.shard_map(
        shards,
        mesh=mesh,
        in_specs=(
            P("seq", None),
            P(),
            P(),
            P(None, "head"),
            P(None, "head"),
            P(None, "head"),
            P(None, "head"),
            P("head"),
            P(None, "head"),
            P(None, "head"),
            P(None, "head"),
            P(),
            P("head", None),
            P(),
            P(None, "head"),
            P(None, "head"),
            P("head", None),
            P("seq", None),
        ),
        out_specs=(
            P("seq", None),
            P("seq", None),
            P("seq"),
            P("seq", "head"),
            P("seq", "head"),
            P("seq", "head"),
            P("seq", "head"),
            P("head"),
            P(None, "head"),
            P(None, "head"),
            P(None, "head"),
            P(),
            P("head", "seq"),
            P("seq"),
            P("seq", "head"),
            P("seq", "head"),
            P("head", "seq"),
        ),
        check_vma=False,
    )
```

time: 3140 us -> 1620 us (0.52)
  matrix products: 942 us -> 166 us
  waiting for transfers between devices: 1590 us -> 936 us
  local copies, waits for them, and re-layouts: 320 us -> 46.1 us
  Pallas kernels: 0 us -> 139 us
  starting transfers between devices: 7.94 us -> 135 us
  other arithmetic: 190 us -> 137 us
    ppermute x2 -> x43, waiting for transfers between devices: 0.01 us -> 936 us  [the longest x33 587 us: swap(): return lax.ppermute(block, axis, [(i, i ^ bit) for i in range(count)])]
    reduce_scatter x7 -> x0, waiting for transfers between devices: 886 us -> none  [the longest x1 197 us: shards(): lax.psum_scatter(gate_term, 'seq', scatter_dimension=0, tiled=True)]
    dot_general x1369 -> x37, matrix products: 933 us -> 166 us  [the longest x17 105 us: matmul(): lax.dot_general(left, right, (((left_dim,), (right_dim,)), ((), ())), pre...]
    psum x3 -> x1, waiting for transfers between devices: 553 us -> 0.01 us  [shards(): small = lax.psum(small, 'seq')]
    all_gather x4 -> x0, waiting for transfers between devices: 145 us -> none  [entering(): everything = jax.tree.map(lambda part: lax.all_gather(part, axis), shard)]
    pallas_call x0 -> x4, Pallas kernels: none -> 139 us  [the longest x1 79.8 us: delta_forward(): on_chip(forward_kernel, 'delta_forward', grid=(blocks,), in_specs=[scalar...]
    ppermute x2 -> x43, starting transfers between devices: 6.94 us -> 135 us  [the longest x33 103 us: swap(): return lax.ppermute(block, axis, [(i, i ^ bit) for i in range(count)])]
    squeeze x96 -> x0, local copies, waits for them, and re-layouts: 85.9 us -> none  [local_pass(): lax.scan(advance, (zero_memory, identity), (queries, key_rows, values, st...]
  transfers between devices with their start and end apart: 17 -> 44, of which waited for: 13 -> 24; matrix products, arithmetic and copies ran while one was open for 6% -> 14% of each run, Pallas kernels for 0% -> 3%
where the time goes in v1:
time: 1620 us; the launch traced here: 1610 us
  waiting for transfers between devices  936 us (58%)
  matrix products  166 us (10%)
  Pallas kernels  139 us (9%)
  other arithmetic  137 us (8%)
  starting transfers between devices  135 us (8%)
  local copies, waits for them, and re-layouts  46.1 us (3%)
  blocking collectives  37.9 us (2%)
    ppermute x33, waiting for transfers between devices, swap(): return lax.ppermute(block, axis, [(i, i ^ bit) for i in range(count)])  587 us
    ppermute x10, waiting for transfers between devices, shift(): return lax.ppermute(block, axis, route)  349 us
    dot_general x17, matrix products, matmul(): lax.dot_general(left, right, (((left_dim,), (right_dim,)), ((), ())), pre...  105 us
    ppermute x33, starting transfers between devices, swap(): return lax.ppermute(block, axis, [(i, i ^ bit) for i in range(count)])  103 us
    pallas_call x1, Pallas kernels, delta_forward(): on_chip(forward_kernel, 'delta_forward', grid=(blocks,), in_specs=[scalar...  79.8 us
    dot_general x14, matrix products, product(): lax.dot_general(left, right, (((0,), (0,)), ((), ())), preferred_element_...  59.1 us
    pallas_call x1, Pallas kernels, delta_backward(): on_chip(backward_kernel, 'delta_backward', grid=(blocks,), in_specs=[scal...  51 us
    psum x1, blocking collectives, shards(): lax.psum(jnp.concatenate([norm_gain_part, head_gain_part.reshape(-1)]), (...  37.9 us
  transfers between devices with their start and end apart: 44, of which 24 were waited for; matrix products, arithmetic and copies ran while one was open for 14% of the time, Pallas kernels for 3%

profile of v1, /device:TPU:0, one launch (start us, length us, event | category | flops | bytes accessed | tf_op | source)
XLA Modules:
  0.0 1613.6 jit_solution(11507590400535218093)
XLA Ops:
  29.4 79.8 %delta_forward.1 = (f32[8,4,128,128]{3,2,1,0:T(8,128)S(1)}, f32[1024,512]{1,0:T(8,128)S(1)}, f32[1024,512]{1,0:T(8,128)}, f32[8,4,128,256]{3,2,1,0:T(8,128)}, f32[4,128,256]{2,1,0:T(8,128)S(1)}) custom-call(s32[7]{0:T(128)S(1)} %copy-done.17, s32[1]{0:T(128)} %bitcast.base, f32[1024,512]{1,0:T(8,128)} %copy-done.26, f32[1024,512]{1,0:T(8,128)} %copy-done.27, ...), custom_call_target="tpu_custom_call" | custom-call | tf_op jit(solution)/shard_map/delta_forward/pallas_call | solution.py:369
  172.2 91.1 %collective-permute-done.6 = f32[512,2048]{1,0:T(8,128)S(1)} collective-permute-done((f32[512,2048]{1,0:T(8,128)S(1)}, f32[512,2048]{1,0:T(8,128)S(1)}, u32[]{:S(2)}, u32[]{:S(2)}) %collective-permute-start.6) | collective-permute-done | bytes 4194336 | tf_op jit(solution)/shard_map/ppermute | solution.py:482
  270.3 11.8 fusion.90
  296.5 11.8 fusion.88
  308.4 13.3 multiply_convert_fusion.2
  362.7 84.6 %collective-permute-done.12 = f32[512,2048]{1,0:T(8,128)S(1)} collective-permute-done((f32[512,2048]{1,0:T(8,128)S(1)}, f32[512,2048]{1,0:T(8,128)S(1)}, u32[]{:S(2)}, u32[]{:S(2)}) %collective-permute-start.12) | collective-permute-done | bytes 4194336 | tf_op jit(solution)/shard_map/ppermute | solution.py:482
  450.1 86.8 %collective-permute-done.9 = f32[512,2048]{1,0:T(8,128)S(1)} collective-permute-done((f32[512,2048]{1,0:T(8,128)S(1)}, f32[512,2048]{1,0:T(8,128)S(1)}, u32[]{:S(2)}, u32[]{:S(2)}) %collective-permute-start.9) | collective-permute-done | bytes 4194336 | tf_op jit(solution)/shard_map/ppermute | solution.py:482
  574.7 23.4 %fusion.81 = (bf16[1024,2048]{1,0:T(8,128)(2,1)S(1)}, f32[1024,2048]{1,0:T(8,128)}, f32[1024,2048]{1,0:T(8,128)}) fusion(f32[1024,2048]{1,0:T(8,128)} %param.35, f32[1024,2048]{1,0:T(8,128)} %get-tuple-element.60, f32[1024]{0:T(1024)S(1)} %fusion.61, f32[512,2048]{1,0:T(8,128)} %add.272, f32[512,2048]{1,0:T(8,128)} %collective-permute-done.13, pred[]{:T(512)S(6)} %eq.11, ...), kind=kLoop, calls=%fused_computation.193 | loop fusion | flops 27262976 | bytes 54542336 | tf_op jit(solution)/shard_map/convert_element_type | solution.py:640
  606.9 324.9 %collective-permute-done.14 = f32[4,128,128]{2,1,0:T(8,128)S(1)} collective-permute-done((f32[4,128,128]{2,1,0:T(8,128)S(1)}, f32[4,128,128]{2,1,0:T(8,128)S(1)}, u32[]{:S(2)}, u32[]{:S(2)}) %collective-permute-start.14) | collective-permute-done | bytes 262176 | tf_op jit(solution)/shard_map/ppermute | solution.py:488
  968.3 51.0 %delta_backward.1 = (f32[1024,512]{1,0:T(8,128)S(1)}, f32[1024,512]{1,0:T(8,128)S(1)}, f32[1024,512]{1,0:T(8,128)}, f32[8,1536]{1,0:T(8,128)S(1)}, f32[1024,4]{1...) custom-call(s32[7]{0:T(128)S(1)} %copy-done.18, s32[1]{0:T(128)} %bitcast.base, ...), custom_call_target="tpu_custom_call" | custom-call | tf_op jit(solution)/shard_map/delta_backward/pallas_call | solution.py:447
  1029.9 60.1 %collective-permute-start.35 = (f32[512,1408]{1,0:T(8,128)}, f32[512,1408]{1,0:T(8,128)}, u32[]{:S(2)}, u32[]{:S(2)}) collective-permute-start(f32[512,1408]{1,0:T(8,128)} %slice.259), channel_id=1, source_target_pairs={{0,8},{4,12},{8,0},{12,4},{16,24},{20,28},{24,16},{28,20},{1,9},{5... | collective-permute-start | bytes 8650760 | tf_op jit(solution)/shard_map/ppermute | solution.py:482
  1134.2 36.7 %collective-permute-done.35 = f32[512,1408]{1,0:T(8,128)} collective-permute-done((f32[512,1408]{1,0:T(8,128)}, f32[512,1408]{1,0:T(8,128)}, u32[]{:S(2)}, u32[]{:S(2)}) %collective-permute-start.35) | collective-permute-done | bytes 2883616 | tf_op jit(solution)/shard_map/ppermute | solution.py:482
  1185.9 70.0 %collective-permute-done.42 = f32[1408,256]{1,0:T(8,128)S(1)} collective-permute-done((f32[1408,256]{1,0:T(8,128)S(1)}, f32[1408,256]{1,0:T(8,128)S(1)}, u32[]{:S(2)}, u32[]{:S(2)}) %collective-permute-start.42) | collective-permute-done | bytes 1441824 | tf_op jit(solution)/shard_map/ppermute | solution.py:482
  1257.3 29.6 %collective-permute-done.39 = f32[256,1408]{1,0:T(8,128)} collective-permute-done((f32[256,1408]{1,0:T(8,128)}, f32[256,1408]{1,0:T(8,128)}, u32[]{:S(2)}, u32[]{:S(2)}) %collective-permute-start.39) | collective-permute-done | bytes 1441824 | tf_op jit(solution)/shard_map/ppermute | solution.py:482
  1289.5 25.2 %collective-permute-done.36 = f32[256,1408]{1,0:T(8,128)} collective-permute-done((f32[256,1408]{1,0:T(8,128)}, f32[256,1408]{1,0:T(8,128)}, u32[]{:S(2)}, u32[]{:S(2)}) %collective-permute-start.36) | collective-permute-done | bytes 1441824 | tf_op jit(solution)/shard_map/ppermute | solution.py:482
  1355.6 13.7 collective-permute-done.28
  1376.8 38.0 %collective-permute-done.25 = f32[1024,512]{1,0:T(8,128)} collective-permute-done((f32[1024,512]{1,0:T(8,128)}, f32[1024,512]{1,0:T(8,128)}, u32[]{:S(2)}, u32[]{:S(2)}) %collective-permute-start.25) | collective-permute-done | bytes 2097184 | tf_op jit(solution)/shard_map/ppermute | solution.py:482
  1421.5 34.2 %collective-permute-done.22 = f32[1024,512]{1,0:T(8,128)} collective-permute-done((f32[1024,512]{1,0:T(8,128)}, f32[1024,512]{1,0:T(8,128)}, u32[]{:S(2)}, u32[]{:S(2)}) %collective-permute-start.22) | collective-permute-done | bytes 2097184 | tf_op jit(solution)/shard_map/ppermute | solution.py:482
  1476.9 17.9 %collective-permute-done.23 = f32[512,512]{1,0:T(8,128)} collective-permute-done((f32[512,512]{1,0:T(8,128)}, f32[512,512]{1,0:T(8,128)}, u32[]{:S(2)}, u32[]{:S(2)}) %collective-permute-start.23) | collective-permute-done | bytes 1048608 | tf_op jit(solution)/shard_map/ppermute | solution.py:482
  1497.4 24.5 %collective-permute-done.30 = f32[256,512]{1,0:T(8,128)S(1)} collective-permute-done((f32[256,512]{1,0:T(8,128)S(1)}, f32[256,512]{1,0:T(8,128)S(1)}, u32[]{:S(2)}, u32[]{:S(2)}) %collective-permute-start.30) | collective-permute-done | bytes 524320 | tf_op jit(solution)/shard_map/ppermute | solution.py:482
  1522.8 10.4 collective-permute-done.27
  1540.1 11.8 multiply_reduce_fusion.1
  1552.0 37.9 %psum.14 = f32[2176]{0:T(1024)S(1)} all-reduce(f32[2176]{0:T(1024)S(1)} %pad_maximum_fusion.21), channel_id=1, replica_groups=mesh['seq'=8,'head'=4] {'seq','head'}, use_global_device_ids=true, to_apply=%region_5.6 | all-reduce | flops 2176 | bytes 17408 | tf_op jit(solution)/shard_map/psum | solution.py:691
  1591.0 15.2 subtract_add_fusion
  (408 shorter events, 393.7 us)
Async XLA Ops:
  7.2 1455.2 %all-reduce.2.cloned.1.call-start = ((), (), s32[]{:S(2)}) async-start(), calls=%async_computation | async-start | bytes 139264 | tf_op jit(solution)/shard_map/psum | solution.py:683
  170.6 92.7 %collective-permute-start.6 = (f32[512,2048]{1,0:T(8,128)S(1)}, f32[512,2048]{1,0:T(8,128)S(1)}, u32[]{:S(2)}, u32[]{:S(2)}) collective-permute-start(f32[512,2048]{1,0:T(8,128)S(1)} %dynamic-slice_add_fusion.3), channel_id=1, source_target_pairs={{0,2},{1,3},{2,0},{3,1},{4,6},{5,7},{6,4},{7,5},{8,10},{9,11},{10,... | collective-permute-start | bytes 12582920 | tf_op jit(solution)/shard_map/ppermute | solution.py:482
  353.9 93.4 %collective-permute-start.12 = (f32[512,2048]{1,0:T(8,128)S(1)}, f32[512,2048]{1,0:T(8,128)S(1)}, u32[]{:S(2)}, u32[]{:S(2)}) collective-permute-start(f32[512,2048]{1,0:T(8,128)S(1)} %dynamic-slice_add_fusion.1), channel_id=1, source_target_pairs={{0,2},{1,3},{2,0},{3,1},{4,6},{5,7},{6,4},{7,5},{8,10},{9,11},{10,... | collective-permute-start | bytes 12582920 | tf_op jit(solution)/shard_map/ppermute | solution.py:482
  361.2 175.6 %collective-permute-start.9 = (f32[512,2048]{1,0:T(8,128)S(1)}, f32[512,2048]{1,0:T(8,128)S(1)}, u32[]{:S(2)}, u32[]{:S(2)}) collective-permute-start(f32[512,2048]{1,0:T(8,128)S(1)} %dynamic-slice_add_fusion.2), channel_id=1, source_target_pairs={{0,2},{1,3},{2,0},{3,1},{4,6},{5,7},{6,4},{7,5},{8,10},{9,11},{10,... | collective-permute-start | bytes 12582920 | tf_op jit(solution)/shard_map/ppermute | solution.py:482
  450.1 116.8 %collective-permute-start.13 = (f32[512,2048]{1,0:T(8,128)}, f32[512,2048]{1,0:T(8,128)}, u32[]{:S(2)}, u32[]{:S(2)}) collective-permute-start(f32[512,2048]{1,0:T(8,128)} %add.272), channel_id=1, source_target_pairs={{0,1},{1,0},{2,3},{3,2},{4,5},{5,4},{6,7},{7,6},{8,9},{9,8},{10,11... | collective-permute-start | bytes 12582920 | tf_op jit(solution)/shard_map/ppermute | solution.py:482
  550.4 393.5 %collective-permute-start.40 = (f32[1408,1024]{1,0:T(8,128)}, f32[1408,1024]{1,0:T(8,128)}, u32[]{:S(2)}, u32[]{:S(2)}) collective-permute-start(f32[1408,1024]{1,0:T(8,128)} %fusion.27), channel_id=1, source_target_pairs={{0,4},{4,0},{8,12},{12,8},{16,20},{20,16},{24,28},{28,24},{1,5},{5... | collective-permute-start | bytes 17301512 | tf_op jit(solution)/shard_map/ppermute | solution.py:482
  559.3 398.2 %collective-permute-start.37 = (f32[1024,1408]{1,0:T(8,128)}, f32[1024,1408]{1,0:T(8,128)}, u32[]{:S(2)}, u32[]{:S(2)}) collective-permute-start(f32[1024,1408]{1,0:T(8,128)} %fusion.42), channel_id=1, source_target_pairs={{0,4},{4,0},{8,12},{12,8},{16,20},{20,16},{24,28},{28,24},{1,5},{5... | collective-permute-start | bytes 17301512 | tf_op jit(solution)/shard_map/ppermute | solution.py:482
  564.9 455.8 %collective-permute-start.34 = (f32[1024,1408]{1,0:T(8,128)}, f32[1024,1408]{1,0:T(8,128)}, u32[]{:S(2)}, u32[]{:S(2)}) collective-permute-start(f32[1024,1408]{1,0:T(8,128)} %fusion.43), channel_id=1, source_target_pairs={{0,4},{4,0},{8,12},{12,8},{16,20},{20,16},{24,28},{28,24},{1,5},{5... | collective-permute-start | bytes 17301512 | tf_op jit(solution)/shard_map/ppermute | solution.py:482
  605.6 326.2 %collective-permute-start.14 = (f32[4,128,128]{2,1,0:T(8,128)S(1)}, f32[4,128,128]{2,1,0:T(8,128)S(1)}, u32[]{:S(2)}, u32[]{:S(2)}) collective-permute-start(f32[4,128,128]{2,1,0:T(8,128)S(1)} %get-tuple-element.42), channel_id=1, source_target_pairs={{4,0},{8,4},{12,8},{16,12},{20,16},{24,20},{28,24},{5,1},{9,5},{13... | collective-permute-start | bytes 786440 | tf_op jit(solution)/shard_map/ppermute | solution.py:488
  950.5 174.1 %collective-permute-start.41 = (f32[1408,512]{1,0:T(8,128)S(1)}, f32[1408,512]{1,0:T(8,128)}, u32[]{:S(2)}, u32[]{:S(2)}) collective-permute-start(f32[1408,512]{1,0:T(8,128)S(1)} %slice.267), channel_id=1, source_target_pairs={{0,8},{4,12},{8,0},{12,4},{16,24},{20,28},{24,16},{28,20},{1,9},{5... | collective-permute-start | bytes 8650760 | tf_op jit(solution)/shard_map/ppermute | solution.py:482
  965.3 165.4 %collective-permute-start.38 = (f32[512,1408]{1,0:T(8,128)}, f32[512,1408]{1,0:T(8,128)}, u32[]{:S(2)}, u32[]{:S(2)}) collective-permute-start(f32[512,1408]{1,0:T(8,128)} %slice.263), channel_id=1, source_target_pairs={{0,8},{4,12},{8,0},{12,4},{16,24},{20,28},{24,16},{28,20},{1,9},{5... | collective-permute-start | bytes 8650760 | tf_op jit(solution)/shard_map/ppermute | solution.py:482
  1019.3 71.2 %collective-permute-start.18 = (f32[8,1536]{1,0:T(8,128)S(1)}, f32[8,1536]{1,0:T(8,128)S(1)}, u32[]{:S(2)}, u32[]{:S(2)}) collective-permute-start(f32[8,1536]{1,0:T(8,128)S(1)} %get-tuple-element.45), channel_id=1, source_target_pairs={{4,0},{8,4},{12,8},{16,12},{20,16},{24,20},{28,24},{5,1},{9,5},{13... | collective-permute-start | bytes 147464 | tf_op jit(solution)/shard_map/ppermute | solution.py:488
  1029.9 141.0 %collective-permute-start.35 = (f32[512,1408]{1,0:T(8,128)}, f32[512,1408]{1,0:T(8,128)}, u32[]{:S(2)}, u32[]{:S(2)}) collective-permute-start(f32[512,1408]{1,0:T(8,128)} %slice.259), channel_id=1, source_target_pairs={{0,8},{4,12},{8,0},{12,4},{16,24},{20,28},{24,16},{28,20},{1,9},{5... | collective-permute-start | bytes 8650760 | tf_op jit(solution)/shard_map/ppermute | solution.py:482
  1119.8 59.7 %collective-permute-start.19 = (f32[512,2048]{1,0:T(8,128)}, f32[512,2048]{1,0:T(8,128)}, u32[]{:S(2)}, u32[]{:S(2)}) collective-permute-start(f32[512,2048]{1,0:T(8,128)} %constant_dynamic-slice_fusion.33), channel_id=1, source_target_pairs={{0,1},{1,0},{2,3},{3,2},{4,5},{5,4},{6,7},{7,6},{8,9},{9,8},{10,11... | collective-permute-start | bytes 12582920 | tf_op jit(solution)/shard_map/ppermute | solution.py:482
  1127.6 128.3 %collective-permute-start.42 = (f32[1408,256]{1,0:T(8,128)S(1)}, f32[1408,256]{1,0:T(8,128)S(1)}, u32[]{:S(2)}, u32[]{:S(2)}) collective-permute-start(f32[1408,256]{1,0:T(8,128)S(1)} %slice.269), channel_id=1, source_target_pairs={{0,16},{4,20},{8,24},{12,28},{16,0},{20,4},{24,8},{28,12},{1,17},{... | collective-permute-start | bytes 4325384 | tf_op jit(solution)/shard_map/ppermute | solution.py:482
  1134.0 152.9 %collective-permute-start.39 = (f32[256,1408]{1,0:T(8,128)}, f32[256,1408]{1,0:T(8,128)}, u32[]{:S(2)}, u32[]{:S(2)}) collective-permute-start(f32[256,1408]{1,0:T(8,128)} %slice.265), channel_id=1, source_target_pairs={{0,16},{4,20},{8,24},{12,28},{16,0},{20,4},{24,8},{28,12},{1,17},{... | collective-permute-start | bytes 4325384 | tf_op jit(solution)/shard_map/ppermute | solution.py:482
  1175.1 139.7 %collective-permute-start.36 = (f32[256,1408]{1,0:T(8,128)}, f32[256,1408]{1,0:T(8,128)}, u32[]{:S(2)}, u32[]{:S(2)}) collective-permute-start(f32[256,1408]{1,0:T(8,128)} %slice.261), channel_id=1, source_target_pairs={{0,16},{4,20},{8,24},{12,28},{16,0},{20,4},{24,8},{28,12},{1,17},{... | collective-permute-start | bytes 4325384 | tf_op jit(solution)/shard_map/ppermute | solution.py:482
  1179.5 145.3 %collective-permute-start.31 = (f32[512,1024]{1,0:T(8,128)}, f32[512,1024]{1,0:T(8,128)}, u32[]{:S(2)}, u32[]{:S(2)}) collective-permute-start(f32[512,1024]{1,0:T(8,128)} %fusion.12), channel_id=1, source_target_pairs={{0,4},{4,0},{8,12},{12,8},{16,20},{20,16},{24,28},{28,24},{1,5},{5... | collective-permute-start | bytes 6291464 | tf_op jit(solution)/shard_map/ppermute | solution.py:482
  1184.4 149.4 %collective-permute-start.20 = (f32[512,2048]{1,0:T(8,128)}, f32[512,2048]{1,0:T(8,128)}, u32[]{:S(2)}, u32[]{:S(2)}) collective-permute-start(f32[512,2048]{1,0:T(8,128)} %dynamic-slice_add_fusion), channel_id=1, source_target_pairs={{0,2},{1,3},{2,0},{3,1},{4,6},{5,7},{6,4},{7,5},{8,10},{9,11},{10,... | collective-permute-start | bytes 12582920 | tf_op jit(solution)/shard_map/ppermute | solution.py:482
  1324.3 90.5 %collective-permute-start.25 = (f32[1024,512]{1,0:T(8,128)}, f32[1024,512]{1,0:T(8,128)}, u32[]{:S(2)}, u32[]{:S(2)}) collective-permute-start(f32[1024,512]{1,0:T(8,128)} %fusion.46), channel_id=1, source_target_pairs={{0,4},{4,0},{8,12},{12,8},{16,20},{20,16},{24,28},{28,24},{1,5},{5... | collective-permute-start | bytes 6291464 | tf_op jit(solution)/shard_map/ppermute | solution.py:482
  1332.9 122.9 %collective-permute-start.22 = (f32[1024,512]{1,0:T(8,128)}, f32[1024,512]{1,0:T(8,128)}, u32[]{:S(2)}, u32[]{:S(2)}) collective-permute-start(f32[1024,512]{1,0:T(8,128)} %fusion.48), channel_id=1, source_target_pairs={{0,4},{4,0},{8,12},{12,8},{16,20},{20,16},{24,28},{28,24},{1,5},{5... | collective-permute-start | bytes 6291464 | tf_op jit(solution)/shard_map/ppermute | solution.py:482
  1340.4 199.7 %collective-permute-start.21 = (f32[512,2048]{1,0:T(8,128)}, f32[512,2048]{1,0:T(8,128)}, u32[]{:S(2)}, u32[]{:S(2)}) collective-permute-start(f32[512,2048]{1,0:T(8,128)} %add.284), channel_id=1, source_target_pairs={{0,1},{1,0},{2,3},{3,2},{4,5},{5,4},{6,7},{7,6},{8,9},{9,8},{10,11... | collective-permute-start | bytes 12582920 | tf_op jit(solution)/shard_map/ppermute | solution.py:482
  1352.0 116.3 %collective-permute-start.33 = (f32[512,256]{1,0:T(8,128)}, f32[512,256]{1,0:T(8,128)}, u32[]{:S(2)}, u32[]{:S(2)}) collective-permute-start(f32[512,256]{1,0:T(8,128)} %slice.256), channel_id=1, source_target_pairs={{0,16},{4,20},{8,24},{12,28},{16,0},{20,4},{24,8},{28,12},{1,17},{... | collective-permute-start | bytes 1572872 | tf_op jit(solution)/shard_map/ppermute | solution.py:482
  1374.5 95.8 %collective-permute-start.29 = (f32[512,512]{1,0:T(8,128)}, f32[512,512]{1,0:T(8,128)S(1)}, u32[]{:S(2)}, u32[]{:S(2)}) collective-permute-start(f32[512,512]{1,0:T(8,128)} %slice.244), channel_id=1, source_target_pairs={{0,8},{4,12},{8,0},{12,4},{16,24},{20,28},{24,16},{28,20},{1,9},{5... | collective-permute-start | bytes 3145736 | tf_op jit(solution)/shard_map/ppermute | solution.py:482
  (123 other events, 4062.5 us)
Sparse Core Ops, SparseCore 0:
  1341.2 79.3 all-reduce.1

commit v2 on v1

--- a/solution.py
+++ b/solution.py
@@ -59,22 +59,35 @@
     return total
 
 
-def block_inverse(strict, rows, columns, passes=3):
-    near = jnp.where(rows // SUB == columns // SUB, strict, 0.0)
-    far = strict - near
+def block_inverses(stricts, rows, columns, passes=3):
+    near_mask = rows // SUB == columns // SUB
     eye = jnp.where(rows == columns, 1.0, 0.0)
-    inverse = eye - near
-    power = mm(near, near, passes=passes)
+    nears = [jnp.where(near_mask, strict, 0.0) for strict in stricts]
+    fars = [strict - near for strict, near in zip(stricts, nears)]
+    inverses = [eye - near for near in nears]
+    powers = [mm(near, near, passes=passes) for near in nears]
     covered = 2
     while covered * 2 < SUB:
-        both = mm(jnp.concatenate([power, inverse], axis=0), power, passes=passes)
-        power, inverse = both[:BLOCK], inverse + both[BLOCK:]
+        both = [
+            mm(jnp.concatenate([power, inverse], axis=0), power, passes=passes)
+            for power, inverse in zip(powers, inverses)
+        ]
+        powers = [part[:BLOCK] for part in both]
+        inverses = [inverse + part[BLOCK:] for inverse, part in zip(inverses, both)]
         covered *= 2
-    inverse = inverse + mm(inverse, power, passes=passes)
-    chain = mm(inverse, far, passes=passes)
-    both = mm(chain, jnp.concatenate([inverse, chain], axis=1), passes=passes)
-    partial = inverse - both[:, :BLOCK]
-    return partial + mm(both[:, BLOCK:], partial, passes=passes)
+    inverses = [
+        inverse + mm(inverse, power, passes=passes) for inverse, power in zip(inverses, powers)
+    ]
+    chains = [mm(inverse, far, passes=passes) for inverse, far in zip(inverses, fars)]
+    both = [
+        mm(link, jnp.concatenate([inverse, link], axis=1), passes=passes)
+        for link, inverse in zip(chains, inverses)
+    ]
+    partials = [inverse - part[:, :BLOCK] for inverse, part in zip(inverses, both)]
+    return [
+        partial + mm(part[:, BLOCK:], partial, passes=passes)
+        for partial, part in zip(partials, both)
+    ]
 
 
 def forward_kernel(
@@ -114,6 +127,7 @@
     rows, columns, same, carried, final, through, reach = block_masks(first, starts, count)
     below = jnp.logical_and(same, columns < rows)
     upto = jnp.logical_and(same, columns <= rows)
+    queries, keys, values, stricts, scores, rate_list = [], [], [], [], [], []
     for head in range(heads):
         span = slice(head * size, (head + 1) * size)
         pieces = []
@@ -126,39 +140,69 @@
             pieces.append(conv * sigmoid(conv))
         query = pieces[0] * lax.rsqrt(jnp.sum(pieces[0] * pieces[0], axis=1, keepdims=True) + 1e-6)
         key = pieces[1] * lax.rsqrt(jnp.sum(pieces[1] * pieces[1], axis=1, keepdims=True) + 1e-6)
-        value = pieces[2]
-        rate = jnp.broadcast_to(rates[:, head : head + 1], (BLOCK, size))
-        products = mm(jnp.concatenate([query, key], axis=0), key, 1, 1)
-        scores = jnp.where(upto, products[:BLOCK], 0.0)
-        strict = jnp.where(below, products[BLOCK:] * rate, 0.0)
-        inverse = block_inverse(strict, rows, columns)
-        inverse_out[0, head] = inverse
-        writes = mm(inverse, jnp.concatenate([rate * carried * key, rate * value], axis=1))
-        held = memory[head]
-        memory_out[0, head] = held
-        read = mm(jnp.concatenate([writes[:, :size], carried * query], axis=0), held)
-        residue = (
-            jnp.concatenate([jnp.zeros((BLOCK, size), F32), writes[:, size:]], axis=1)
-            - read[:BLOCK]
+        queries.append(query)
+        keys.append(key)
+        values.append(pieces[2])
+        rate_list.append(jnp.broadcast_to(rates[:, head : head + 1], (BLOCK, size)))
+    for number, lin in enumerate((lin_query, lin_key, lin_value)):
+        before[:, number * width : (number + 1) * width] = lin[BLOCK - EDGE :, :]
+    for head in range(heads):
+        products = mm(jnp.concatenate([queries[head], keys[head]], axis=0), keys[head], 1, 1)
+        scores.append(jnp.where(upto, products[:BLOCK], 0.0))
+        stricts.append(jnp.where(below, products[BLOCK:] * rate_list[head], 0.0))
+    inverses = block_inverses(stricts, rows, columns)
+    for head in range(heads):
+        inverse_out[0, head] = inverses[head]
+    writes = [
+        mm(
+            inverses[head],
+            jnp.concatenate(
+                [rate_list[head] * carried * keys[head], rate_list[head] * values[head]], axis=1
+            )
         )
-        result = read[BLOCK:] + mm(scores, residue)
+        for head in range(heads)
+    ]
+    helds = [memory[head] for head in range(heads)]
+    for head in range(heads):
+        memory_out[0, head] = helds[head]
+    reads = [
+        mm(
+            jnp.concatenate([writes[head][:, :size], carried * queries[head]], axis=0),
+            helds[head]
+        )
+        for head in range(heads)
+    ]
+    residues = [
+        jnp.concatenate(
+            [-reads[head][:BLOCK, :size], writes[head][:, size:] - reads[head][:BLOCK, size:]],
+            axis=1,
+        )
+        for head in range(heads)
+    ]
+    updates = [
+        through * helds[head] + mm(final * keys[head], residues[head], 0, 0)
+        for head in range(heads)
+    ]
+    for head in range(heads):
+        memory[head] = updates[head]
+        final_out[head] = updates[head]
+    for head in range(heads):
+        span = slice(head * size, (head + 1) * size)
+        result = reads[head][BLOCK:] + mm(scores[head], residues[head])
         effective_out[:, span] = result[:, :size]
         local_out[:, span] = result[:, size:]
-        updated = through * held + mm(final * key, residue, 0, 0)
-        memory[head] = updated
-        final_out[head] = updated
-    for number, lin in enumerate((lin_query, lin_key, lin_value)):
-        before[:, number * width : (number + 1) * width] = lin[BLOCK - EDGE :, :]
-
-
-def output_kernel(effective, local, entering, gain, mixed_out, headed_out):
+
+
+def output_kernel(effective, local, entering, gain, mixed_out, headed_out, rounded_out):
     heads, size = entering.shape[0], entering.shape[1]
     for head in range(heads):
         span = slice(head * size, (head + 1) * size)
         mixed = local[:, span] + mm(effective[:, span], entering[head])
         mixed_out[:, span] = mixed
         scale = lax.rsqrt(jnp.mean(mixed * mixed, axis=1, keepdims=True) + 1e-5)
-        headed_out[:, span] = (mixed * scale * gain[...]).astype(headed_out.dtype)
+        headed = mixed * scale * gain[...]
+        headed_out[:, span] = headed
+        rounded_out[:, span] = headed.astype(rounded_out.dtype)
 
 
 def norm_back_kernel(headed_grad, mixed_rows, effective, gain, grad_out, gain_out, local_out):
@@ -219,6 +263,8 @@
     blocks = pl.num_programs(0)
     here = blocks - 1 - step
     count = starts.shape[0]
+    every = range(heads)
+    spans = [slice(head * size, (head + 1) * size) for head in every]
 
     @pl.when(step == 0)
     def _():
@@ -232,94 +278,131 @@
     rows, columns, same, carried, final, through, reach = block_masks(first, starts, count)
     below = jnp.logical_and(same, columns < rows)
     upto = jnp.logical_and(same, columns <= rows)
-    lanes = lax.broadcasted_iota(jnp.int32, (BLOCK, rates.shape[1]), 1)
-    logit_grad = jnp.zeros((BLOCK, rates.shape[1]), F32)
-    for head in range(heads):
-        span = slice(head * size, (head + 1) * size)
-        joins, convs, gates, pieces = [], [], [], []
-        for number, (lin, prior, taps) in enumerate(
-            (
-                (lin_query, prior_query, taps_query),
-                (lin_key, prior_key, taps_key),
-                (lin_value, prior_value, taps_value),
-            )
-        ):
-            place = slice(number * width + head * size, number * width + (head + 1) * size)
-            border = jnp.where(here == 0, edge[:, place], prior[:, span])
-            joined = jnp.concatenate([border, lin[:, span]], axis=0)
-            conv = short_conv(joined, taps[:, span], reach)
-            gate = sigmoid(conv)
-            joins.append(joined)
-            convs.append(conv)
-            gates.append(gate)
-            pieces.append(conv * gate)
-        query_scale = lax.rsqrt(jnp.sum(pieces[0] * pieces[0], axis=1, keepdims=True) + 1e-6)
-        key_scale = lax.rsqrt(jnp.sum(pieces[1] * pieces[1], axis=1, keepdims=True) + 1e-6)
-        query = pieces[0] * query_scale
-        key = pieces[1] * key_scale
-        value = pieces[2]
-        rate_column = rates[:, head : head + 1]
-        rate = jnp.broadcast_to(rate_column, (BLOCK, size))
-        products = mm(jnp.concatenate([query, key], axis=0), key, 1, 1)
-        scores = jnp.where(upto, products[:BLOCK], 0.0)
-        gram = products[BLOCK:]
-        inverse = inverse_in[0, head]
-        held = memory_in[0, head]
-        memory = mm(held[:, :size], entering[head]) + held[:, size:]
-        left = carried * key
-        wanted = value - mm(left, memory)
-        residue = mm(inverse, rate * wanted)
-        grad_out = mixed_grad[:, span]
-        grad_memory = memory_grad[head]
-        last_keys = final * key
-        residue_grad = mm(scores, grad_out, 0, 0) + mm(last_keys, grad_memory)
-        solved_grad = mm(inverse, residue_grad, 0, 0)
-        wanted_grad = rate * solved_grad
-        outer = mm(jnp.concatenate([grad_out, solved_grad], axis=0), residue, 1, 1)
-        scores_grad = jnp.where(upto, outer[:BLOCK], 0.0)
-        strict_grad = jnp.where(below, -outer[BLOCK:], 0.0)
-        gram_grad = rate * strict_grad
-        rate_grad = jnp.sum(solved_grad * wanted + strict_grad * gram, axis=1, keepdims=True)
-        state_side = mm(jnp.concatenate([grad_out, wanted_grad], axis=0), memory, 1, 1)
-        key_side = mm(jnp.concatenate([scores_grad, gram_grad], axis=0), key)
-        query_grad = carried * state_side[:BLOCK] + key_side[:BLOCK]
-        key_grad = (
-            key_side[BLOCK:]
-            - carried * state_side[BLOCK:]
-            + mm(
-                jnp.concatenate([scores_grad, gram_grad], axis=0),
-                jnp.concatenate([query, key], axis=0),
-                0,
-                0,
-            )
-            + final * mm(residue, grad_memory, 1, 1)
-        )
-        memory_grad[head] = through * grad_memory + mm(
-            jnp.concatenate([carried * query, -left], axis=0),
-            jnp.concatenate([grad_out, wanted_grad], axis=0),
+
+    def convolved(number, lin, prior, taps, head):
+        place = slice(number * width + head * size, number * width + (head + 1) * size)
+        border = jnp.where(here == 0, edge[:, place], prior[:, spans[head]])
+        joined = jnp.concatenate([border, lin[:, spans[head]]], axis=0)
+        conv = short_conv(joined, taps[:, spans[head]], reach)
+        return joined, conv, sigmoid(conv)
+
+    def unit_scale(piece):
+        return lax.rsqrt(jnp.sum(piece * piece, axis=1, keepdims=True) + 1e-6)
+
+    query_parts = [convolved(0, lin_query, prior_query, taps_query, head) for head in every]
+    key_parts = [convolved(1, lin_key, prior_key, taps_key, head) for head in every]
+    value_parts = [convolved(2, lin_value, prior_value, taps_value, head) for head in every]
+    query_scales = [unit_scale(conv * gate) for _, conv, gate in query_parts]
+    key_scales = [unit_scale(conv * gate) for _, conv, gate in key_parts]
+    queries = [conv * gate * scale for (_, conv, gate), scale in zip(query_parts, query_scales)]
+    keys = [conv * gate * scale for (_, conv, gate), scale in zip(key_parts, key_scales)]
+    values = [conv * gate for _, conv, gate in value_parts]
+    rate_columns = [rates[:, head : head + 1] for head in every]
+    rate_wide = [jnp.broadcast_to(column, (BLOCK, size)) for column in rate_columns]
+    products = [
+        mm(jnp.concatenate([queries[head], keys[head]], axis=0), keys[head], 1, 1)
+        for head in every
+    ]
+    scores = [jnp.where(upto, part[:BLOCK], 0.0) for part in products]
+    grams = [part[BLOCK:] for part in products]
+    inverses = [inverse_in[0, head] for head in every]
+    memories = [
+        mm(memory_in[0, head][:, :size], entering[head]) + memory_in[0, head][:, size:]
+        for head in every
+    ]
+    lefts = [carried * key for key in keys]
+    wanted = [values[head] - mm(lefts[head], memories[head]) for head in every]
+    residues = [mm(inverses[head], rate_wide[head] * wanted[head]) for head in every]
+    given = [mixed_grad[:, span] for span in spans]
+    score_sides = [mm(scores[head], given[head], 0, 0) for head in every]
+    state_grads = [memory_grad[head] for head in every]
+    last_keys = [final * key for key in keys]
+    residue_grads = [
+        score_sides[head] + mm(last_keys[head], state_grads[head]) for head in every
+    ]
+    solved_grads = [mm(inverses[head], residue_grads[head], 0, 0) for head in every]
+    wanted_grads = [rate_wide[head] * solved_grads[head] for head in every]
+    updates = [
+        through * state_grads[head]
+        + mm(
+            jnp.concatenate([carried * queries[head], -lefts[head]], axis=0),
+            jnp.concatenate([given[head], wanted_grads[head]], axis=0),
             0,
             0,
         )
+        for head in every
+    ]
+    for head in every:
+        memory_grad[head] = updates[head]
+    outers = [
+        mm(jnp.concatenate([given[head], solved_grads[head]], axis=0), residues[head], 1, 1)
+        for head in every
+    ]
+    state_sides = [
+        mm(jnp.concatenate([given[head], wanted_grads[head]], axis=0), memories[head], 1, 1)
+        for head in every
+    ]
+    final_sides = [final * mm(residues[head], state_grads[head], 1, 1) for head in every]
+    score_grads = [jnp.where(upto, part[:BLOCK], 0.0) for part in outers]
+    strict_grads = [jnp.where(below, -part[BLOCK:], 0.0) for part in outers]
+    gram_grads = [rate_wide[head] * strict_grads[head] for head in every]
+    pairs = [
+        jnp.concatenate([score_grads[head], gram_grads[head]], axis=0) for head in every
+    ]
+    key_sides = [mm(pairs[head], keys[head]) for head in every]
+    turned_sides = [
+        mm(pairs[head], jnp.concatenate([queries[head], keys[head]], axis=0), 0, 0)
+        for head in every
+    ]
+    rate_grads = [
+        jnp.sum(
+            solved_grads[head] * wanted[head] + strict_grads[head] * grams[head],
+            axis=1,
+            keepdims=True,
+        )
+        for head in every
+    ]
+    lanes = lax.broadcasted_iota(jnp.int32, (BLOCK, rates.shape[1]), 1)
+    logit_grad = jnp.zeros((BLOCK, rates.shape[1]), F32)
+    for head in every:
+        column = rate_columns[head]
         logit_grad = jnp.where(
-            lanes == head, rate_grad * rate_column * (1.0 - rate_column), logit_grad
+            lanes == head, rate_grads[head] * column * (1.0 - column), logit_grad
         )
-        query_grad = query_scale * (
-            query_grad - query * jnp.sum(query * query_grad, axis=1, keepdims=True)
+    logit_out[...] = logit_grad
+    query_grads = [
+        carried * state_sides[head][:BLOCK] + key_sides[head][:BLOCK] for head in every
+    ]
+    key_grads = [
+        key_sides[head][BLOCK:]
+        - carried * state_sides[head][BLOCK:]
+        + turned_sides[head]
+        + final_sides[head]
+        for head in every
+    ]
+    query_grads = [
+        scale * (grad - query * jnp.sum(query * grad, axis=1, keepdims=True))
+        for scale, grad, query in zip(query_scales, query_grads, queries)
+    ]
+    key_grads = [
+        scale * (grad - key * jnp.sum(key * grad, axis=1, keepdims=True))
+        for scale, grad, key in zip(key_scales, key_grads, keys)
+    ]
+    spare = jnp.zeros((EDGE, size), F32)
+    for number, (grads, parts, taps, lin_out, taps_out) in enumerate(
+        (
+            (query_grads, query_parts, taps_query, query_out, taps_query_out),
+            (key_grads, key_parts, taps_key, key_out, taps_key_out),
+            (wanted_grads, value_parts, taps_value, value_out, taps_value_out),
         )
-        key_grad = key_scale * (key_grad - key * jnp.sum(key * key_grad, axis=1, keepdims=True))
-        for number, (grad, taps, lin_out, taps_out) in enumerate(
-            (
-                (query_grad, taps_query, query_out, taps_query_out),
-                (key_grad, taps_key, key_out, taps_key_out),
-                (wanted_grad, taps_value, value_out, taps_value_out),
-            )
-        ):
+    ):
+        for head in every:
+            span = spans[head]
             place = slice(number * width + head * size, number * width + (head + 1) * size)
-            gate, conv, joined = gates[number], convs[number], joins[number]
-            conv_grad = grad * gate * (1.0 + conv * (1.0 - gate))
-            spare = jnp.zeros((EDGE, size), F32)
+            joined, conv, gate = parts[head]
+            conv_grad = grads[head] * gate * (1.0 + conv * (1.0 - gate))
             lin_grad = taps[3:4, span] * conv_grad
-            tail = jnp.zeros((EDGE, size), F32)
+            tail = spare
             taps_grad = [jnp.sum(conv_grad * joined[EDGE:], axis=0, keepdims=True)]
             for back in range(1, 4):
                 part = conv_grad * reach[back]
@@ -334,19 +417,17 @@
                     jnp.sum(part * joined[EDGE - back : EDGE - back + BLOCK], axis=0, keepdims=True)
                 )
             taps_out[:, span] += jnp.concatenate(taps_grad[::-1], axis=0)
-            carry = jnp.concatenate(
-                [jnp.zeros((BLOCK - EDGE, size), F32), after[:, place]], axis=0
-            )
-            lin_out[:, span] = lin_grad + carry
+            lin_out[: BLOCK - EDGE, span] = lin_grad[: BLOCK - EDGE]
+            lin_out[BLOCK - EDGE :, span] = lin_grad[BLOCK - EDGE :] + after[:, place]
             after[:, place] = tail
             edge_out[:, place] = tail
-    logit_out[...] = logit_grad
 
 
 def on_chip(kernel, name, **settings):
     return pl.pallas_call(
         kernel,
         name=name,
+        cost_estimate=pl.CostEstimate(flops=1, bytes_accessed=1, transcendentals=0),
         compiler_params=pltpu.CompilerParams(
             dimension_semantics=("arbitrary",), vmem_limit_bytes=48 * 1024 * 1024
         ),
@@ -406,8 +487,9 @@
         "delta_output",
         grid=(length // rows,),
         in_specs=[row_block, row_block, whole((heads, size, size)), whole((1, size))],
-        out_specs=[row_block, row_block],
+        out_specs=[row_block, row_block, row_block],
         out_shape=[
+            jax.ShapeDtypeStruct((length, width), F32),
             jax.ShapeDtypeStruct((length, width), F32),
             jax.ShapeDtypeStruct((length, width), BF16),
         ],
@@ -430,6 +512,85 @@
             jax.ShapeDtypeStruct((heads, size, size), F32),
         ],
     )(headed_grad, mixed_rows, effective, gain)
+
+
+def norm_pull_kernel(odd, part, other, values, gain, given, grad_out, rounded_out, gain_out):
+    step = pl.program_id(0)
+    second = step * 2 // pl.num_programs(0)
+
+    @pl.when(step == 0)
+    def _():
+        gain_out[...] = jnp.zeros_like(gain_out)
+
+    grad = jnp.where(second == odd[0], part[...], other[...])
+    value = values[...]
+    scale = lax.rsqrt(jnp.mean(value * value, axis=1, keepdims=True) + 1e-5)
+    gain_out[...] += jnp.sum(grad * value * scale, axis=0, keepdims=True)
+    scaled = gain[...] * grad
+    along = jnp.mean(value * scaled, axis=1, keepdims=True)
+    result = given[...] + (scale * scaled - value * (scale * scale * scale * along))
+    grad_out[...] = result
+    rounded_out[...] = result.astype(rounded_out.dtype)
+
+
+def norm_pulled(halves, values, gain, given):
+    length, width = values.shape
+    rows = length // 8
+    odd = (lax.axis_index("head") % 2).astype(jnp.int32).reshape(1)
+    row_block = pl.BlockSpec((rows, width), lambda i: (i, 0))
+    half_block = pl.BlockSpec((rows, width), lambda i: (i % 4, 0))
+    return on_chip(
+        norm_pull_kernel,
+        "norm_pull",
+        grid=(8,),
+        in_specs=[scalars(), half_block, half_block, row_block, whole((1, width)), row_block],
+        out_specs=[row_block, row_block, whole((1, width))],
+        out_shape=[
+            jax.ShapeDtypeStruct((length, width), F32),
+            jax.ShapeDtypeStruct((length, width), BF16),
+            jax.ShapeDtypeStruct((1, width), F32),
+        ],
+    )(odd, *halves, values, gain.reshape(1, width), given)
+
+
+def beside_kernel(first, second, out):
+    width = first.shape[1]
+    out[:, :width] = first[...].astype(out.dtype)
+    out[:, width:] = second[...].astype(out.dtype)
+
+
+def above_kernel(first, second, out):
+    rows = first.shape[0]
+    out[:rows] = first[...].astype(out.dtype)
+    out[rows:] = second[...].astype(out.dtype)
+
+
+def rounded_beside(first, second):
+    length, width = first.shape
+    rows = min(length, 256)
+    block = pl.BlockSpec((rows, width), lambda i: (i, 0))
+    return on_chip(
+        beside_kernel,
+        "rounded_beside",
+        grid=(length // rows,),
+        in_specs=[block, block],
+        out_specs=pl.BlockSpec((rows, 2 * width), lambda i: (i, 0)),
+        out_shape=jax.ShapeDtypeStruct((length, 2 * width), BF16),
+    )(first, second)
+
+
+def rounded_above(first, second):
+    rows, width = first.shape
+    columns = min(width, 256)
+    block = pl.BlockSpec((rows, columns), lambda i: (0, i))
+    return on_chip(
+        above_kernel,
+        "rounded_above",
+        grid=(width // columns,),
+        in_specs=[block, block],
+        out_specs=pl.BlockSpec((2 * rows, columns), lambda i: (0, i)),
+        out_shape=jax.ShapeDtypeStruct((2 * rows, width), BF16),
+    )(first, second)
 
 
 def delta_backward(
@@ -488,21 +649,38 @@
     return lax.ppermute(block, axis, route)
 
 
-def sum_over_head(term):
-    if lax.axis_size("head") != 4:
-        return lax.psum(term, "head")
+def begun_over_head(term):
     odd = lax.axis_index("head") % 2
     half = term.shape[0] // 2
     keep = lax.dynamic_slice_in_dim(term, odd * half, half, 0)
     send = lax.dynamic_slice_in_dim(term, (1 - odd) * half, half, 0)
-    part = keep + swap(send, "head", 1)
-    part = part + swap(part, "head", 2)
-    other = swap(part, "head", 1)
+    return keep + swap(send, "head", 1)
+
+
+def ended_over_head(part, *gates):
+    part = part + after(swap(part, "head", 2), *gates)
+    return part, swap(part, "head", 1)
+
+
+def whole_rows(part, other):
     return jnp.where(
-        odd == 0,
+        lax.axis_index("head") % 2 == 0,
         jnp.concatenate([part, other], axis=0),
         jnp.concatenate([other, part], axis=0),
     )
+
+
+def after(value, *others):
+    return lax.optimization_barrier((value,) + others)[0] if others else value
+
+
+def summed_everywhere(vector, axis):
+    count = lax.axis_size(axis)
+    bit = 1
+    while bit < count:
+        vector = vector + swap(vector, axis, bit)
+        bit *= 2
+    return vector
 
 
 def relative_order(bits):
@@ -512,54 +690,81 @@
     return [index ^ bits[0] for index in rest] + rest
 
 
-def seq_bits(late):
+def seq_bits():
     bits = []
     while 1 << len(bits) < lax.axis_size("seq"):
         bits.append(1 << len(bits))
-    return bits[1:] + bits[:1] if late else bits
-
-
-def arranged(rows, late=False):
+    return bits
+
+
+def arrange_kernel(places, rows, out):
+    out[...] = rows[...]
+
+
+def arranged(rows, places):
+    length, size = rows.shape[0], rows.shape[1] // lax.axis_size("seq")
+    if size % 128:
+        return jnp.concatenate(
+            [lax.dynamic_slice_in_dim(rows, place * size, size, 1) for place in places], axis=1
+        )
+    return pl.pallas_call(
+        arrange_kernel,
+        name="arrange",
+        cost_estimate=pl.CostEstimate(flops=1, bytes_accessed=1, transcendentals=0),
+        grid_spec=pltpu.PrefetchScalarGridSpec(
+            num_scalar_prefetch=1,
+            grid=(len(places),),
+            in_specs=[pl.BlockSpec((length, size), lambda i, places: (0, places[i]))],
+            out_specs=pl.BlockSpec((length, size), lambda i, places: (0, i)),
+        ),
+        out_shape=jax.ShapeDtypeStruct(rows.shape, rows.dtype),
+        compiler_params=pltpu.CompilerParams(dimension_semantics=("arbitrary",)),
+    )(jnp.stack(places).astype(jnp.int32), rows)
+
+
+def relative_places():
     here = lax.axis_index("seq")
-    size = rows.shape[1] // lax.axis_size("seq")
-    return jnp.concatenate(
-        [
-            lax.dynamic_slice_in_dim(rows, (here ^ index) * size, size, 1)
-            for index in relative_order(seq_bits(late))
-        ],
-        axis=1,
-    )
-
-
-def token_sum(rows, others, rows_first=True, late=False):
-    half = rows.shape[1] // 2
-    dim = 0 if rows_first else 1
-
-    def product(piece):
-        left, right = (piece, others) if rows_first else (others, piece)
-        return lax.dot_general(
-            left, right, (((0,), (0,)), ((), ())), preferred_element_type=F32
-        )
-
-    bits = seq_bits(late)
-    given = product(rows[:, :half])
-    kept = product(rows[:, half:])
-    for place, bit in enumerate(bits):
-        kept = kept + swap(given, "seq", bit)
-        if place + 1 < len(bits):
-            size = kept.shape[dim] // 2
-            given = lax.slice_in_dim(kept, 0, size, axis=dim)
-            kept = lax.slice_in_dim(kept, size, 2 * size, axis=dim)
+    return [here ^ index for index in relative_order(seq_bits())]
+
+
+def product(rows, others, rows_first):
+    return matmul(rows, others, 0, 0) if rows_first else matmul(others, rows, 0, 0)
+
+
+def received(given, kept, axis, place):
+    bits = seq_bits()
+    kept = kept + swap(given, "seq", bits[place])
+    if place + 1 == len(bits):
+        return None, kept
+    size = kept.shape[axis] // 2
+    return lax.slice_in_dim(kept, 0, size, axis=axis), lax.slice_in_dim(
+        kept, size, 2 * size, axis=axis
+    )
+
+
+def finished(given, kept, axis, place):
+    while place < len(seq_bits()):
+        given, kept = received(given, kept, axis, place)
+        place += 1
     return kept
 
 
-def chain(transfer, offset, distance):
+def chain(transfer, offset, distance, turned=False, between=()):
     hops = max(lax.axis_size("seq") // 2, 1)
-    state = shift(offset, "seq", distance)
-    for _ in range(hops - 1):
-        moved = jnp.einsum("hij,hjk->hik", transfer, state, precision=lax.Precision.HIGH) + offset
-        state = shift(moved, "seq", distance)
-    return state
+    groups = 2
+    count = offset.shape[0] // groups
+    picks = [slice(index * count, (index + 1) * count) for index in range(groups)]
+    form = "hji,hjk->hik" if turned else "hij,hjk->hik"
+    states = [shift(offset[pick], "seq", distance) for pick in picks]
+    for hop in range(hops - 1):
+        if hop < len(between):
+            states[0] = after(states[0], between[hop])
+        moved = [
+            jnp.einsum(form, transfer[pick], state, precision=lax.Precision.HIGH) + offset[pick]
+            for pick, state in zip(picks, states)
+        ]
+        states = [shift(part, "seq", distance) for part in moved]
+    return jnp.concatenate(states, axis=0)
 
 
 def row_norm(values):
@@ -570,12 +775,6 @@
     return lax.dot_general(
         left, right, (((left_dim,), (right_dim,)), ((), ())), preferred_element_type=F32
     )
-
-
-def norm_pull(grad, values, scale, gain):
-    scaled = gain * grad
-    along = jnp.mean(values * scaled, axis=-1, keepdims=True)
-    return scale * scaled - values * (scale * scale * scale * along)
 
 
 def shards(
@@ -610,6 +809,8 @@
 
     scale_one = row_norm(hidden)
     normed = (hidden * scale_one * norm_gain).astype(BF16)
+    w_wide = w_output.astype(F32)
+    w_across = swap(w_wide, "head", 2)
     lins = tuple(matmul(normed, part) for part in (w_query, w_key, w_value))
     tails = jnp.concatenate([part[-EDGE:] for part in lins], axis=1)
     edge = shift(tails, "seq", 1)
@@ -619,9 +820,18 @@
     )
     transfer, offset = last[:, :, :size], last[:, :, size:]
     entering = chain(transfer, offset, 1)
-    mixed_rows, headed = delta_output(effective, local, entering, gain)
-
-    middle = hidden + sum_over_head(matmul(headed, w_output))
+    mixed_rows, headed_wide, headed = delta_output(effective, local, entering, gain)
+    h_across = swap(headed_wide, "head", 2)
+    h_core = swap(headed_wide, "head", 1)
+    w_late, w_across = after((w_wide, w_across), headed)
+    w_near = rounded_above(w_late, swap(w_late, "head", 1))
+    w_distant = rounded_above(w_across, swap(w_across, "head", 1))
+    middle = hidden + matmul(rounded_beside(headed_wide, h_core), w_near)
+    ffn_cot = after(out_grad, headed).astype(BF16)
+    cot_ordered = arranged(ffn_cot, relative_places())
+    h_across = after(h_across, middle, w_distant, cot_ordered)
+    h_far = swap(h_across, "head", 1)
+    middle = middle + matmul(rounded_beside(h_across, h_far), w_distant)
     scale_two = row_norm(middle)
     normed_two = (middle * scale_two * ffn_gain).astype(BF16)
     gate_rows = matmul(normed_two, w_gate)
@@ -629,68 +839,107 @@
     sigma = jax.nn.sigmoid(gate_rows)
     silu_gate = gate_rows * sigma
     active = (silu_gate * upward).astype(BF16)
-    ffn_cot = out_grad.astype(BF16)
+    half = ffn_cot.shape[1] // 2
+    split = active.shape[1] // 128 * 3 // 4 * 128
+    lead, rest = active[:, :split], active[:, split:]
+    lead_given = product(cot_ordered[:, :half], lead, False)
+    ffn_cot = after(ffn_cot, lead_given)
     active_grad = matmul(ffn_cot, w_down, 1, 1)
     gate_cot = (active_grad * upward * sigma * (1.0 + gate_rows * (1.0 - sigma))).astype(BF16)
     up_cot = (active_grad * silu_gate).astype(BF16)
-    two_part = matmul(gate_cot, w_gate, 1, 1) + matmul(up_cot, w_up, 1, 1)
-    normed_two_grad = sum_over_head(two_part)
-    middle_grad = out_grad + norm_pull(normed_two_grad, middle, scale_two, ffn_gain)
-    ffn_gain_part = jnp.sum(normed_two_grad * middle * scale_two, axis=0)
-    branch_cot = middle_grad.astype(BF16)
+    gate_term = matmul(normed_two, gate_cot, 0, 0)
+    w_gate_grad = lax.psum_scatter(gate_term, "seq", scatter_dimension=0, tiled=True)
+    gate_late, up_late = after(gate_cot, gate_term), after(up_cot, gate_term)
+    two_part = matmul(gate_late, w_gate, 1, 1) + matmul(up_late, w_up, 1, 1)
+    two_begun = begun_over_head(two_part)
+    ffn_begun = begun_over_head(matmul(after(active, two_begun), w_down))
+    up_term = matmul(normed_two, after(up_cot, two_begun), 0, 0)
+    w_up_grad = lax.psum_scatter(up_term, "seq", scatter_dimension=0, tiled=True)
+    cot_ordered = after(cot_ordered, two_begun)
+    lead_kept = product(cot_ordered[:, half:], lead, False)
+    rest_given = product(cot_ordered[:, :half], rest, False)
+    rest_kept = product(cot_ordered[:, half:], rest, False)
+    middle_grad, branch_cot, ffn_gain_part = norm_pulled(
+        ended_over_head(
+            two_begun, ffn_begun, up_term, lead_kept, rest_given, rest_kept
+        ),
+        middle,
+        ffn_gain,
+        out_grad,
+    )
     headed_grad = matmul(branch_cot, w_output, 1, 1)
-
-    normed_two_ordered = arranged(normed_two)
-    w_gate_grad = token_sum(normed_two_ordered, gate_cot)
-    w_up_grad = token_sum(normed_two_ordered, up_cot)
-    w_down_grad = token_sum(arranged(ffn_cot), active, False)
-    block_output = middle + sum_over_head(matmul(active, w_down))
-
+    branch_ordered = arranged(after(branch_cot, headed_grad), relative_places())
+    mix_given = jnp.concatenate(
+        [rest_given, product(branch_ordered[:, :half], headed, False)], axis=0
+    )
     mixed_grad, head_gain_part, local_grad = norm_back(
         headed_grad, mixed_rows, effective, gain, heads, size
     )
-    leaving = chain(jnp.transpose(transfer, (0, 2, 1)), local_grad, -1)
+    leaving = chain(transfer, local_grad, -1, True)
+    lead_given, lead_kept = received(lead_given, lead_kept, 1, 0)
+    lead_given, mix_given = after((lead_given, mix_given), leaving)
+    leaving = after(leaving, lead_given, mix_given)
     back = delta_backward(
         doc_starts, base, lins, edge, taps, rates, inverse, memories, entering, leaving, mixed_grad
     )
-    returned = shift(back[3], "seq", -1)
+    ffn_halves = ended_over_head(ffn_begun)
+    lead_given, lead_kept = received(lead_given, lead_kept, 1, 1)
+    returned, logit_grad = after(
+        (shift(back[3], "seq", -1), back[4]), lead_given, ffn_halves[0]
+    )
     cots = tuple(
         jnp.concatenate(
             [part[:-EDGE], part[-EDGE:] + returned[:, index * width : (index + 1) * width]], axis=0
         ).astype(BF16)
         for index, part in enumerate(back[:3])
     )
-    logit_grad = back[4]
     strength_cot = logit_grad.astype(BF16)
-    first_part = matmul(cots[0], w_query, 1, 1)
-    first_part = first_part + matmul(cots[1], w_key, 1, 1)
-    first_part = first_part + matmul(cots[2], w_value, 1, 1)
+    cot = after(jnp.concatenate(cots, axis=1), w_gate_grad, lead_given)
+    lin_term = product(normed, cot, True)
+    lin_grad = lax.psum_scatter(lin_term, "seq", scatter_dimension=0, tiled=True)
+    lin_grads = tuple(lin_grad[:, index * width : (index + 1) * width] for index in range(3))
+    mix_kept = jnp.concatenate(
+        [rest_kept, product(branch_ordered[:, half:], headed, False)], axis=0
+    )
+    late_cots, strength_cot = after((cots, strength_cot), lin_term)
+    first_part = matmul(late_cots[0], w_query, 1, 1)
+    first_part = first_part + matmul(late_cots[1], w_key, 1, 1)
+    first_part = first_part + matmul(late_cots[2], w_value, 1, 1)
     first_part = first_part + matmul(strength_cot, w_strength, 1, 1)
-    normed_grad = sum_over_head(first_part)
-    hidden_grad = middle_grad + norm_pull(normed_grad, hidden, scale_one, norm_gain)
     norm_gain_part = jnp.sum(first_part * hidden * scale_one, axis=0)
-
-    w_output_grad = token_sum(arranged(branch_cot), headed, False)
-    normed_ordered = arranged(normed)
-    lin_grads = tuple(token_sum(normed_ordered, part) for part in cots)
+    shared = summed_everywhere(
+        jnp.concatenate([norm_gain_part, head_gain_part.reshape(-1)]), "head"
+    )
+    first_begun = after(begun_over_head(first_part), shared)
+    mix_given, mix_kept = received(mix_given, after(mix_kept, first_begun), 1, 0)
+    lead_kept = finished(lead_given, lead_kept, 1, 2)
+    first_halves = ended_over_head(first_begun, mix_given, lead_kept, w_up_grad)
+    mix_given, mix_kept = received(mix_given, mix_kept, 1, 1)
+    hidden_grad = norm_pulled(first_halves, hidden, norm_gain, middle_grad)[0]
+    block_output = middle + whole_rows(*ffn_halves)
+    mix_kept = finished(mix_given, mix_kept, 1, 2)
+    rest_rows = rest.shape[1]
+    w_down_grad = jnp.concatenate([lead_kept, mix_kept[:rest_rows]], axis=0)
+    w_output_grad = mix_kept[rest_rows:]
     strength_term = matmul(strength_cot, normed, 0, 0)
 
     small = jnp.concatenate(
-        [strength_term.reshape(-1), ffn_gain_part]
+        [
+            shared,
+            strength_term.reshape(-1),
+            ffn_gain_part.reshape(-1),
+        ]
         + [part.reshape(-1) for part in back[5:8]]
         + [jnp.sum(logit_grad, axis=0)]
     )
-    small = lax.psum(small, "seq")
+    small = summed_everywhere(small, "seq")
     features = norm_gain.shape[0]
     block = features // seq_count
-    cut = [heads * features, features] + [4 * width] * 3 + [heads]
+    cut = [features, size, heads * features, features] + [4 * width] * 3 + [heads]
     parts, at = [], 0
     for extent in cut:
         parts.append(small[at : at + extent])
         at += extent
-    shared = lax.psum(
-        jnp.concatenate([norm_gain_part, head_gain_part.reshape(-1)]), ("seq", "head")
-    )
 
     def own(vector, axis=0):
         return lax.dynamic_slice_in_dim(vector, seq_rank * block, block, axis)
@@ -698,18 +947,18 @@
     return (
         block_output,
         hidden_grad,
-        own(shared[:features]),
+        own(parts[0]),
         lin_grads[0],
         lin_grads[1],
         lin_grads[2],
-        own(parts[0].reshape(heads, features), 1).T,
-        parts[5],
-        parts[2].reshape(4, width),
-        parts[3].reshape(4, width),
+        own(parts[2].reshape(heads, features), 1).T,
+        parts[7],
         parts[4].reshape(4, width),
-        shared[features:],
+        parts[5].reshape(4, width),
+        parts[6].reshape(4, width),
+        parts[1],
         w_output_grad,
-        own(parts[1]),
+        own(parts[3]),
         w_gate_grad,
         w_up_grad,
         w_down_grad,

time: 1620 us -> 1030 us (0.64)
  waiting for transfers between devices: 936 us -> 473 us
  starting transfers between devices: 135 us -> 80.3 us
  other arithmetic: 137 us -> 83.3 us
  blocking collectives: 37.9 us -> 0 us
    ppermute x10 -> x18, waiting for transfers between devices: 349 us -> 50.1 us  [shift(): return lax.ppermute(block, axis, route)]
    ppermute x33 -> x26, waiting for transfers between devices: 587 us -> 422 us  [swap(): return lax.ppermute(block, axis, [(i, i ^ bit) for i in range(count)])]
    ppermute x33 -> x26, starting transfers between devices: 103 us -> 30.3 us  [swap(): return lax.ppermute(block, axis, [(i, i ^ bit) for i in range(count)])]
    dot_general x17 -> x27, matrix products: 105 us -> 178 us  [matmul(): lax.dot_general(left, right, (((left_dim,), (right_dim,)), ((), ())), pre...]
    pallas_call x0 -> x8, Pallas kernels: none -> 67.3 us  [the longest x2 34.8 us: norm_pulled(): on_chip(norm_pull_kernel, 'norm_pull', grid=(8,), in_specs=[scalars(), ha...]
    dot_general x20 -> x12, matrix products: 61.1 us -> 2.94 us  [chain(): jnp.einsum(form, transfer[pick], state, precision=lax.Precision.HIGH)]
    pallas_call x1, Pallas kernels: 79.8 us -> 33.1 us  [delta_forward(): on_chip(forward_kernel, 'delta_forward', grid=(blocks,), in_specs=[scalar...]
    psum x1 -> x0, blocking collectives: 37.9 us -> none  [shards(): lax.psum(jnp.concatenate([norm_gain_part, head_gain_part.reshape(-1)]), (...]
  transfers between devices with their start and end apart: 44 -> 47, of which waited for: 24 -> 23; matrix products, arithmetic and copies ran while one was open for 14% -> 22% of each run, Pallas kernels for 3% -> 14%
where the time goes in v2:
time: 1030 us; the launch traced here: 1020 us
  waiting for transfers between devices  473 us (46%)
  matrix products  181 us (18%)
  Pallas kernels  148 us (14%)
  other arithmetic  83.3 us (8%)
  starting transfers between devices  80.3 us (8%)
  local copies, waits for them, and re-layouts  41.4 us (4%)
  between operations  15.8 us (2%)
    ppermute x26, waiting for transfers between devices, swap(): return lax.ppermute(block, axis, [(i, i ^ bit) for i in range(count)])  422 us
    dot_general x27, matrix products, matmul(): lax.dot_general(left, right, (((left_dim,), (right_dim,)), ((), ())), pre...  178 us
    ppermute x18, waiting for transfers between devices, shift(): return lax.ppermute(block, axis, route)  50.1 us
    ppermute x18, starting transfers between devices, shift(): return lax.ppermute(block, axis, route)  49.9 us
    pallas_call x1, Pallas kernels, delta_backward(): on_chip(backward_kernel, 'delta_backward', grid=(blocks,), in_specs=[scal...  37 us
    pallas_call x2, Pallas kernels, norm_pulled(): on_chip(norm_pull_kernel, 'norm_pull', grid=(8,), in_specs=[scalars(), ha...  34.8 us
    pallas_call x1, Pallas kernels, delta_forward(): on_chip(forward_kernel, 'delta_forward', grid=(blocks,), in_specs=[scalar...  33.1 us
    ppermute x26, starting transfers between devices, swap(): return lax.ppermute(block, axis, [(i, i ^ bit) for i in range(count)])  30.3 us
  transfers between devices with their start and end apart: 47, of which 23 were waited for; matrix products, arithmetic and copies ran while one was open for 22% of the time, Pallas kernels for 14%

profile of v2, /device:TPU:0, one launch (start us, length us, event | category | flops | bytes accessed | tf_op | source)
XLA Modules:
  0.0 1021.8 jit_solution(5868717483709755883)
XLA Ops:
  34.0 33.1 %delta_forward.1 = (f32[8,4,128,128]{3,2,1,0:T(8,128)S(1)}, f32[1024,512]{1,0:T(8,128)S(1)}, f32[1024,512]{1,0:T(8,128)}, f32[8,4,128,256]{3,2,1,0:T(8,128)}, f32[4,128,256]{2,1,0:T(8,128)S(1)}) custom-call(s32[7]{0:T(128)S(1)} %copy-done.25, s32[1]{0:T(128)} %bitcast.base, f32[1024,512]{1,0:T(8,128)} %copy-done.32, f32[1024,512]{1,0:T(8,128)} %copy-done.31, ...), custom_call_target="tpu_custom_call" | custom-call | flops 1 | bytes 1 | tf_op jit(solution)/shard_map/delta_forward/pallas_call | solution.py:450
  143.4 8.9 convolution_add_fusion.2
  169.8 9.1 multiply_reduce_fusion.1
  189.8 13.1 %multiply_convert_fusion.4 = (bf16[1024,1408]{1,0:T(8,128)(2,1)S(1)}, f32[1024,1408]{1,0:T(8,128)}) fusion(f32[1024,1408]{1,0:T(8,128)S(1)} %fusion.44, bf16[1024,2048]{1,0:T(8,128)(2,1)S(1)} %multiply_convert_fusion, bf16[2048,1408]{1,0:T(8,128)(2,1)} %param.33), kind=kOutput, calls=%fused_computation.10 | convolution fusion | flops 5914230784 | bytes 24379392 | tf_op jit(solution)/shard_map/dot_general | solution.py:775
  207.4 14.4 %multiply_convert_fusion.2 = (bf16[1024,1408]{1,0:T(8,128)(2,1)}, bf16[1024,1408]{1,0:T(8,128)(2,1)}) fusion(f32[1024,1408]{1,0:T(8,128)} %copy-done.77, f32[1024,1408]{1,0:T(8,128)} %get-tuple-element.137, bf16[1024,2048]{1,0:T(8,128)(2,1)S(1)} %copy-done.36, bf16[1408,2048]{1,0:T(8,128)(2,1)} %param.34), kind=kOutput, calls=%fused_computation.8 | convolution fusion | flops 5924323328 | bytes 27262976 | tf_op jit(solution)/shard_map/dot_general | solution.py:775
  221.8 11.2 %fusion.45 = f32[2048,1408]{1,0:T(8,128)} fusion(bf16[1024,2048]{1,0:T(8,128)(2,1)S(1)} %copy-done.52, bf16[1024,1408]{1,0:T(8,128)(2,1)} %get-tuple-element.75), kind=kOutput, calls=%fused_computation.112 | convolution fusion | flops 5905580032 | bytes 18612224 | tf_op jit(solution)/shard_map/dot_general | solution.py:775
  233.2 10.0 fusion.46
  270.9 9.6 fusion.48
  283.0 10.5 %fusion.47 = f32[1024,2048]{1,0:T(8,128)S(1)} fusion(bf16[1024,1408]{1,0:T(8,128)(2,1)} %copy-done.61, bf16[1408,2048]{1,0:T(8,128)(2,1)} %param.34), kind=kOutput, calls=%fused_computation.114 | convolution fusion | flops 5905580032 | bytes 17039360 | tf_op jit(solution)/shard_map/dot_general | solution.py:775
  303.3 126.0 %collective-permute-done.29 = f32[1024,1024]{1,0:T(8,128)} collective-permute-done((f32[1024,1024]{1,0:T(8,128)}, f32[1024,1024]{1,0:T(8,128)}, u32[]{:S(2)}, u32[]{:S(2)}) %collective-permute-start.29) | collective-permute-done | bytes 4194336 | tf_op jit(solution)/shard_map/ppermute | solution.py:643
  448.0 16.8 %norm_pull.2 = (f32[1024,2048]{1,0:T(8,128)}, bf16[1024,2048]{1,0:T(8,128)(2,1)S(1)}, f32[1,2048]{1,0:T(1,128)S(1)}) custom-call(s32[1]{0:T(128)} %bitcast.10.odd, f32[512,2048]{1,0:T(8,128)} %copy-done.33, f32[512,2048]{1,0:T(8,128)} %copy-done.54, f32[1024,2048]{1,0:T(8,128)} %get-tuple-element.135.values, f32[1,2048]{1,0:T(1,128)S(1)} %bitcast.82, ...), custom_call_target="tpu_custom_call" | custom-call | flops 1 | bytes 1 | tf_op jit(solution)/shard_map/norm_pull/pallas_call | solution.py:542
  496.0 9.5 collective-permute-done.26
  507.1 11.0 %collective-permute-done.22 = f32[2,128,128]{2,1,0:T(8,128)S(1)} collective-permute-done((f32[2,128,128]{2,1,0:T(8,128)S(1)}, f32[2,128,128]{2,1,0:T(8,128)S(1)}, u32[]{:S(2)}, u32[]{:S(2)}) %collective-permute-start.22) | collective-permute-done | bytes 131104 | tf_op jit(solution)/shard_map/ppermute | solution.py:649
  538.1 11.2 %collective-permute-done.24 = f32[2,128,128]{2,1,0:T(8,128)S(1)} collective-permute-done((f32[2,128,128]{2,1,0:T(8,128)S(1)}, f32[2,128,128]{2,1,0:T(8,128)S(1)}, u32[]{:S(2)}, u32[]{:S(2)}) %collective-permute-start.24) | collective-permute-done | bytes 131104 | tf_op jit(solution)/shard_map/ppermute | solution.py:649
  564.1 37.0 %delta_backward.1 = (f32[1024,512]{1,0:T(8,128)S(1)}, f32[1024,512]{1,0:T(8,128)S(1)}, f32[1024,512]{1,0:T(8,128)}, f32[8,1536]{1,0:T(8,128)S(1)}, f32[1024,4]{1...) custom-call(s32[7]{0:T(128)S(1)} %copy-done.26, s32[1]{0:T(128)} %bitcast.base, ...), custom_call_target="tpu_custom_call" | custom-call | flops 1 | bytes 1 | tf_op jit(solution)/shard_map/delta_backward/pallas_call | solution.py:608
  605.4 26.2 %collective-permute-done.31 = f32[1024,512]{1,0:T(8,128)S(1)} collective-permute-done((f32[1024,512]{1,0:T(8,128)S(1)}, f32[1024,512]{1,0:T(8,128)S(1)}, u32[]{:S(2)}, u32[]{:S(2)}) %collective-permute-start.31) | collective-permute-done | bytes 2097184 | tf_op jit(solution)/shard_map/ppermute | solution.py:643
  637.5 12.4 %fusion.50 = f32[2048,1536]{1,0:T(8,128)} fusion(bf16[1024,2048]{1,0:T(8,128)(2,1)} %copy-done.34, bf16[1024,1536]{1,0:T(8,128)(2,1)} %maximum_maximum_fusion), kind=kOutput, calls=%fused_computation.117 | convolution fusion | flops 6442450944 | bytes 19922944 | tf_op jit(solution)/shard_map/dot_general | solution.py:775
  670.4 13.3 %multiply_reduce_fusion = (f32[2048]{0:T(1024)S(1)}, f32[1024,2048]{1,0:T(8,128)}) fusion(f32[1024,2048]{1,0:T(8,128)S(1)} %bitcast.93, f32[1024]{0:T(1024)S(1)} %copy-done.64, bf16[1024,4]{1,0:T(8,128)(2,1)S(1)} %get-tuple-element.102, bf16[2048,4]{0,1:T(4,128)(2,1)S(1)} %copy-done.66, f32[1024,2048]{1,0:T(8,128)} %fusion.53, f32[1024,2048]{1,0:T(8,128)} %fusion.51, ...), kind=kOutput, calls=%fused_computation.2 | convolution fusion | flops 29358080 | bytes 41979904 | tf_op jit(solution)/shard_map/dot_general | solution.py:775
  711.3 91.0 %collective-permute-done.37 = f32[1024,256]{1,0:T(8,128)S(1)} collective-permute-done((f32[1024,256]{1,0:T(8,128)S(1)}, f32[1024,256]{1,0:T(8,128)S(1)}, u32[]{:S(2)}, u32[]{:S(2)}) %collective-permute-start.37) | collective-permute-done | bytes 1048608 | tf_op jit(solution)/shard_map/ppermute | solution.py:643
  803.5 9.8 collective-permute-done.36
  831.6 65.2 %collective-permute-done.40 = f32[18564]{0:T(1024)S(1)} collective-permute-done((f32[18564]{0:T(1024)S(1)}, f32[18564]{0:T(1024)S(1)}, u32[]{:S(2)}, u32[]{:S(2)}) %collective-permute-start.40) | collective-permute-done | bytes 74288 | tf_op jit(solution)/shard_map/ppermute | solution.py:643
  903.6 13.9 %fusion = f32[1024,2048]{1,0:T(8,128)} fusion(f32[1024,2048]{1,0:T(8,128)} %get-tuple-element.135.values, f32[512,2048]{1,0:T(8,128)} %collective-permute-done.18, f32[512,2048]{1,0:T(8,128)} %add.201, pred[]{:T(512)S(6)} %eq.10), kind=kLoop, calls=%fused_computation.1 | loop fusion | flops 8388608 | bytes 25165824 | tf_op jit(solution)/shard_map/add | solution.py:919
  922.4 66.9 %collective-permute-done.43 = f32[896,256]{1,0:T(8,128)} collective-permute-done((f32[896,256]{1,0:T(8,128)S(1)}, f32[896,256]{1,0:T(8,128)}, u32[]{:S(2)}, u32[]{:S(2)}) %collective-permute-start.43) | collective-permute-done | bytes 917536 | tf_op jit(solution)/shard_map/ppermute | solution.py:643
  994.2 18.0 %norm_pull.3 = (f32[1024,2048]{1,0:T(8,128)}, bf16[1024,2048]{1,0:T(8,128)(2,1)}, f32[1,2048]{1,0:T(1,128)}) custom-call(s32[1]{0:T(128)} %bitcast.10.odd, f32[512,2048]{1,0:T(8,128)} %add.223.part, f32[512,2048]{1,0:T(8,128)} %collective-permute-done.38.other, f32[1024,2048]{1,0:T(8,128)} %values.1, f32[1,2048]{1,0:T(1,128)S(1)} %bitcast.83, ...), custom_call_target="tpu_custom_call" | custom-call | flops 1 | bytes 1 | tf_op jit(solution)/shard_map/norm_pull/pallas_call | solution.py:542
  (373 shorter events, 357.6 us)
Async XLA Ops:
  7.2 630.3 %reduce-scatter.4.cloned.1.call-start = ((), (), s32[]{:S(2)}) async-start(), calls=%async_computation.3 | async-start | bytes 12976128 | tf_op jit(solution)/shard_map/reduce_scatter | solution.py:851
  11.5 100.7 %collective-permute-start.10 = (f32[512,2048]{1,0:T(8,128)}, f32[512,2048]{1,0:T(8,128)}, u32[]{:S(2)}, u32[]{:S(2)}) collective-permute-start(f32[512,2048]{1,0:T(8,128)} %convert_element_type.40.first), channel_id=1, source_target_pairs={{0,2},{1,3},{2,0},{3,1},{4,6},{5,7},{6,4},{7,5},{8,10},{9,11},{10,... | collective-permute-start | bytes 12582920 | tf_op jit(solution)/shard_map/ppermute | solution.py:643
  112.2 25.3 %collective-permute-start.13 = (f32[512,2048]{1,0:T(8,128)}, f32[512,2048]{1,0:T(8,128)}, u32[]{:S(2)}, u32[]{:S(2)}) collective-permute-start(f32[512,2048]{1,0:T(8,128)} %collective-permute-done.10.first), channel_id=1, source_target_pairs={{0,1},{1,0},{2,3},{3,2},{4,5},{5,4},{6,7},{7,6},{8,9},{9,8},{10,11... | collective-permute-start | bytes 12582920 | tf_op jit(solution)/shard_map/ppermute | solution.py:643
  112.7 48.4 %collective-permute-start.12 = (f32[1024,512]{1,0:T(8,128)}, f32[1024,512]{1,0:T(8,128)}, u32[]{:S(2)}, u32[]{:S(2)}) collective-permute-start(f32[1024,512]{1,0:T(8,128)} %get-tuple-element.68.first), channel_id=1, source_target_pairs={{0,2},{1,3},{2,0},{3,1},{4,6},{5,7},{6,4},{7,5},{8,10},{9,11},{10,... | collective-permute-start | bytes 6291464 | tf_op jit(solution)/shard_map/ppermute | solution.py:643
  233.1 584.3 %reduce-scatter.6.cloned.1.call-start = ((), (), s32[]{:S(2)}) async-start(), calls=%async_computation.4 | async-start | bytes 12976128 | tf_op jit(solution)/shard_map/reduce_scatter | solution.py:857
  280.5 731.8 %reduce-scatter.8.cloned.1.call-start = ((), (), s32[]{:S(2)}) async-start(), calls=%async_computation.5 | async-start | bytes 14155776 | tf_op jit(solution)/shard_map/reduce_scatter | solution.py:899
  280.5 148.8 %collective-permute-start.29 = (f32[1024,1024]{1,0:T(8,128)}, f32[1024,1024]{1,0:T(8,128)}, u32[]{:S(2)}, u32[]{:S(2)}) collective-permute-start(f32[1024,1024]{1,0:T(8,128)} %fusion.6), channel_id=1, source_target_pairs={{0,4},{4,0},{8,12},{12,8},{16,20},{20,16},{24,28},{28,24},{1,5},{5... | collective-permute-start | bytes 12582920 | tf_op jit(solution)/shard_map/ppermute | solution.py:643
  296.0 138.7 %collective-permute-start.16 = (f32[512,2048]{1,0:T(8,128)}, f32[512,2048]{1,0:T(8,128)S(1)}, u32[]{:S(2)}, u32[]{:S(2)}) collective-permute-start(f32[512,2048]{1,0:T(8,128)} %constant_dynamic-slice_fusion.1), channel_id=1, source_target_pairs={{0,1},{1,0},{2,3},{3,2},{4,5},{5,4},{6,7},{7,6},{8,9},{9,8},{10,11... | collective-permute-start | bytes 12582920 | tf_op jit(solution)/shard_map/ppermute | solution.py:643
  297.4 140.5 %collective-permute-start.19 = (f32[512,2048]{1,0:T(8,128)S(1)}, f32[512,2048]{1,0:T(8,128)S(1)}, u32[]{:S(2)}, u32[]{:S(2)}) collective-permute-start(f32[512,2048]{1,0:T(8,128)S(1)} %copy-done.37), channel_id=1, source_target_pairs={{0,2},{1,3},{2,0},{3,1},{4,6},{5,7},{6,4},{7,5},{8,10},{9,11},{10,... | collective-permute-start | bytes 12582920 | tf_op jit(solution)/shard_map/ppermute | solution.py:643
  440.4 117.1 %collective-permute-start.17 = (f32[512,2048]{1,0:T(8,128)}, f32[512,2048]{1,0:T(8,128)}, u32[]{:S(2)}, u32[]{:S(2)}) collective-permute-start(f32[512,2048]{1,0:T(8,128)} %dynamic-slice_add_fusion.1), channel_id=1, source_target_pairs={{0,2},{1,3},{2,0},{3,1},{4,6},{5,7},{6,4},{7,5},{8,10},{9,11},{10,... | collective-permute-start | bytes 12582920 | tf_op jit(solution)/shard_map/ppermute | solution.py:643
  494.7 23.4 %collective-permute-start.22 = (f32[2,128,128]{2,1,0:T(8,128)S(1)}, f32[2,128,128]{2,1,0:T(8,128)S(1)}, u32[]{:S(2)}, u32[]{:S(2)}) collective-permute-start(f32[2,128,128]{2,1,0:T(8,128)S(1)} %convolution_add_fusion.9), channel_id=1, source_target_pairs={{4,0},{8,4},{12,8},{16,12},{20,16},{24,20},{28,24},{5,1},{9,5},{13... | collective-permute-start | bytes 393224 | tf_op jit(solution)/shard_map/ppermute | solution.py:649
  505.8 21.6 %collective-permute-start.27 = (f32[2,128,128]{2,1,0:T(8,128)S(1)}, f32[2,128,128]{2,1,0:T(8,128)S(1)}, u32[]{:S(2)}, u32[]{:S(2)}) collective-permute-start(f32[2,128,128]{2,1,0:T(8,128)S(1)} %convolution_add_fusion.5), channel_id=1, source_target_pairs={{4,0},{8,4},{12,8},{16,12},{20,16},{24,20},{28,24},{5,1},{9,5},{13... | collective-permute-start | bytes 393224 | tf_op jit(solution)/shard_map/ppermute | solution.py:649
  527.7 21.6 %collective-permute-start.28 = (f32[2,128,128]{2,1,0:T(8,128)S(1)}, f32[2,128,128]{2,1,0:T(8,128)S(1)}, u32[]{:S(2)}, u32[]{:S(2)}) collective-permute-start(f32[2,128,128]{2,1,0:T(8,128)S(1)} %convolution_add_fusion.4), channel_id=1, source_target_pairs={{4,0},{8,4},{12,8},{16,12},{20,16},{24,20},{28,24},{5,1},{9,5},{13... | collective-permute-start | bytes 393224 | tf_op jit(solution)/shard_map/ppermute | solution.py:649
  549.5 82.1 %collective-permute-start.31 = (f32[1024,512]{1,0:T(8,128)S(1)}, f32[1024,512]{1,0:T(8,128)S(1)}, u32[]{:S(2)}, u32[]{:S(2)}) collective-permute-start(f32[1024,512]{1,0:T(8,128)S(1)} %copy-done.59), channel_id=1, source_target_pairs={{0,8},{4,12},{8,0},{12,4},{16,24},{20,28},{24,16},{28,20},{1,9},{5... | collective-permute-start | bytes 6291464 | tf_op jit(solution)/shard_map/ppermute | solution.py:643
  601.2 32.1 %collective-permute-start.30 = (f32[8,1536]{1,0:T(8,128)S(1)}, f32[8,1536]{1,0:T(8,128)S(1)}, u32[]{:S(2)}, u32[]{:S(2)}) collective-permute-start(f32[8,1536]{1,0:T(8,128)S(1)} %get-tuple-element.92), channel_id=1, source_target_pairs={{4,0},{8,4},{12,8},{16,12},{20,16},{24,20},{28,24},{5,1},{9,5},{13... | collective-permute-start | bytes 147464 | tf_op jit(solution)/shard_map/ppermute | solution.py:649
  705.0 112.4 %collective-permute-start.35 = (f32[512,2048]{1,0:T(8,128)}, f32[512,2048]{1,0:T(8,128)}, u32[]{:S(2)}, u32[]{:S(2)}) collective-permute-start(f32[512,2048]{1,0:T(8,128)} %dynamic-slice_add_fusion), channel_id=1, source_target_pairs={{0,2},{1,3},{2,0},{3,1},{4,6},{5,7},{6,4},{7,5},{8,10},{9,11},{10,... | collective-permute-start | bytes 12582920 | tf_op jit(solution)/shard_map/ppermute | solution.py:643
  706.0 107.3 %collective-permute-start.36 = (f32[896,1024]{1,0:T(8,128)S(1)}, f32[896,1024]{1,0:T(8,128)S(1)}, u32[]{:S(2)}, u32[]{:S(2)}) collective-permute-start(f32[896,1024]{1,0:T(8,128)S(1)} %copy-done.57), channel_id=1, source_target_pairs={{0,4},{4,0},{8,12},{12,8},{16,20},{20,16},{24,28},{28,24},{1,5},{5... | collective-permute-start | bytes 11010056 | tf_op jit(solution)/shard_map/ppermute | solution.py:643
  706.2 197.4 %collective-permute-start.18 = (f32[512,2048]{1,0:T(8,128)}, f32[512,2048]{1,0:T(8,128)}, u32[]{:S(2)}, u32[]{:S(2)}) collective-permute-start(f32[512,2048]{1,0:T(8,128)} %add.201), channel_id=1, source_target_pairs={{0,1},{1,0},{2,3},{3,2},{4,5},{5,4},{6,7},{7,6},{8,9},{9,8},{10,11... | collective-permute-start | bytes 12582920 | tf_op jit(solution)/shard_map/ppermute | solution.py:643
  706.2 96.1 %collective-permute-start.37 = (f32[1024,256]{1,0:T(8,128)S(1)}, f32[1024,256]{1,0:T(8,128)S(1)}, u32[]{:S(2)}, u32[]{:S(2)}) collective-permute-start(f32[1024,256]{1,0:T(8,128)S(1)} %copy-done.60), channel_id=1, source_target_pairs={{0,16},{4,20},{8,24},{12,28},{16,0},{20,4},{24,8},{28,12},{1,17},{... | collective-permute-start | bytes 3145736 | tf_op jit(solution)/shard_map/ppermute | solution.py:643
  824.1 170.1 %collective-permute-start.38 = (f32[512,2048]{1,0:T(8,128)}, f32[512,2048]{1,0:T(8,128)}, u32[]{:S(2)}, u32[]{:S(2)}) collective-permute-start(f32[512,2048]{1,0:T(8,128)} %add.223.part), channel_id=1, source_target_pairs={{0,1},{1,0},{2,3},{3,2},{4,5},{5,4},{6,7},{7,6},{8,9},{9,8},{10,11... | collective-permute-start | bytes 12582920 | tf_op jit(solution)/shard_map/ppermute | solution.py:643
  824.1 73.9 %collective-permute-start.42 = (f32[896,512]{1,0:T(8,128)}, f32[896,512]{1,0:T(8,128)}, u32[]{:S(2)}, u32[]{:S(2)}) collective-permute-start(f32[896,512]{1,0:T(8,128)} %slice.230), channel_id=1, source_target_pairs={{0,8},{4,12},{8,0},{12,4},{16,24},{20,28},{24,16},{28,20},{1,9},{5... | collective-permute-start | bytes 5505032 | tf_op jit(solution)/shard_map/ppermute | solution.py:643
  829.8 67.0 %collective-permute-start.40 = (f32[18564]{0:T(1024)S(1)}, f32[18564]{0:T(1024)S(1)}, u32[]{:S(2)}, u32[]{:S(2)}) collective-permute-start(f32[18564]{0:T(1024)S(1)} %add.224), channel_id=1, source_target_pairs={{0,8},{4,12},{8,0},{12,4},{16,24},{20,28},{24,16},{28,20},{1,9},{5... | collective-permute-start | bytes 222776 | tf_op jit(solution)/shard_map/ppermute | solution.py:643
  896.8 20.8 %collective-permute-start.41 = (f32[18564]{0:T(1024)S(1)}, f32[18564]{0:T(1024)S(1)}, u32[]{:S(2)}, u32[]{:S(2)}) collective-permute-start(f32[18564]{0:T(1024)S(1)} %add.225), channel_id=1, source_target_pairs={{0,16},{4,20},{8,24},{12,28},{16,0},{20,4},{24,8},{28,12},{1,17},{... | collective-permute-start | bytes 222776 | tf_op jit(solution)/shard_map/ppermute | solution.py:643
  901.8 87.5 %collective-permute-start.43 = (f32[896,256]{1,0:T(8,128)S(1)}, f32[896,256]{1,0:T(8,128)}, u32[]{:S(2)}, u32[]{:S(2)}) collective-permute-start(f32[896,256]{1,0:T(8,128)S(1)} %slice.244), channel_id=1, source_target_pairs={{0,16},{4,20},{8,24},{12,28},{16,0},{20,4},{24,8},{28,12},{1,17},{... | collective-permute-start | bytes 2752520 | tf_op jit(solution)/shard_map/ppermute | solution.py:643
  (106 other events, 1506.5 us)
Sparse Core Ops, SparseCore 0:
  233.2 225.6 reduce-scatter.3
  463.1 240.8 reduce-scatter.5
  707.6 289.2 reduce-scatter.7

commit v3 on v2

--- a/solution.py
+++ b/solution.py
@@ -847,38 +847,32 @@
     active_grad = matmul(ffn_cot, w_down, 1, 1)
     gate_cot = (active_grad * upward * sigma * (1.0 + gate_rows * (1.0 - sigma))).astype(BF16)
     up_cot = (active_grad * silu_gate).astype(BF16)
-    gate_term = matmul(normed_two, gate_cot, 0, 0)
-    w_gate_grad = lax.psum_scatter(gate_term, "seq", scatter_dimension=0, tiled=True)
-    gate_late, up_late = after(gate_cot, gate_term), after(up_cot, gate_term)
+    both_term = matmul(normed_two, jnp.concatenate([gate_cot, up_cot], axis=1), 0, 0)
+    both_grad = lax.psum_scatter(both_term, "seq", scatter_dimension=0, tiled=True)
+    gate_late, up_late = after((gate_cot, up_cot), both_term)
     two_part = matmul(gate_late, w_gate, 1, 1) + matmul(up_late, w_up, 1, 1)
     two_begun = begun_over_head(two_part)
     ffn_begun = begun_over_head(matmul(after(active, two_begun), w_down))
-    up_term = matmul(normed_two, after(up_cot, two_begun), 0, 0)
-    w_up_grad = lax.psum_scatter(up_term, "seq", scatter_dimension=0, tiled=True)
     cot_ordered = after(cot_ordered, two_begun)
     lead_kept = product(cot_ordered[:, half:], lead, False)
     rest_given = product(cot_ordered[:, :half], rest, False)
     rest_kept = product(cot_ordered[:, half:], rest, False)
     middle_grad, branch_cot, ffn_gain_part = norm_pulled(
         ended_over_head(
-            two_begun, ffn_begun, up_term, lead_kept, rest_given, rest_kept
+            two_begun, ffn_begun, lead_kept, rest_given, rest_kept
         ),
         middle,
         ffn_gain,
         out_grad,
     )
     headed_grad = matmul(branch_cot, w_output, 1, 1)
-    branch_ordered = arranged(after(branch_cot, headed_grad), relative_places())
-    mix_given = jnp.concatenate(
-        [rest_given, product(branch_ordered[:, :half], headed, False)], axis=0
-    )
     mixed_grad, head_gain_part, local_grad = norm_back(
         headed_grad, mixed_rows, effective, gain, heads, size
     )
     leaving = chain(transfer, local_grad, -1, True)
     lead_given, lead_kept = received(lead_given, lead_kept, 1, 0)
-    lead_given, mix_given = after((lead_given, mix_given), leaving)
-    leaving = after(leaving, lead_given, mix_given)
+    lead_given = after(lead_given, leaving)
+    leaving = after(leaving, lead_given)
     back = delta_backward(
         doc_starts, base, lins, edge, taps, rates, inverse, memories, entering, leaving, mixed_grad
     )
@@ -887,6 +881,11 @@
     returned, logit_grad = after(
         (shift(back[3], "seq", -1), back[4]), lead_given, ffn_halves[0]
     )
+    branch_ordered = arranged(after(branch_cot, back[3]), relative_places())
+    mix_given = jnp.concatenate(
+        [rest_given, product(branch_ordered[:, :half], headed, False)], axis=0
+    )
+    mix_given = after(mix_given, returned)
     cots = tuple(
         jnp.concatenate(
             [part[:-EDGE], part[-EDGE:] + returned[:, index * width : (index + 1) * width]], axis=0
@@ -894,14 +893,14 @@
         for index, part in enumerate(back[:3])
     )
     strength_cot = logit_grad.astype(BF16)
-    cot = after(jnp.concatenate(cots, axis=1), w_gate_grad, lead_given)
+    cot = after(jnp.concatenate(cots, axis=1), lead_given)
     lin_term = product(normed, cot, True)
     lin_grad = lax.psum_scatter(lin_term, "seq", scatter_dimension=0, tiled=True)
-    lin_grads = tuple(lin_grad[:, index * width : (index + 1) * width] for index in range(3))
     mix_kept = jnp.concatenate(
         [rest_kept, product(branch_ordered[:, half:], headed, False)], axis=0
     )
-    late_cots, strength_cot = after((cots, strength_cot), lin_term)
+    mix_given, mix_kept = received(mix_given, after(mix_kept, lin_term), 1, 0)
+    late_cots, strength_cot = after((cots, strength_cot), lin_term, mix_given)
     first_part = matmul(late_cots[0], w_query, 1, 1)
     first_part = first_part + matmul(late_cots[1], w_key, 1, 1)
     first_part = first_part + matmul(late_cots[2], w_value, 1, 1)
@@ -911,13 +910,16 @@
         jnp.concatenate([norm_gain_part, head_gain_part.reshape(-1)]), "head"
     )
     first_begun = after(begun_over_head(first_part), shared)
-    mix_given, mix_kept = received(mix_given, after(mix_kept, first_begun), 1, 0)
     lead_kept = finished(lead_given, lead_kept, 1, 2)
-    first_halves = ended_over_head(first_begun, mix_given, lead_kept, w_up_grad)
-    mix_given, mix_kept = received(mix_given, mix_kept, 1, 1)
+    mix_given, mix_kept = received(mix_given, after(mix_kept, first_begun), 1, 1)
+    first_halves = ended_over_head(first_begun, mix_given, lead_kept, both_grad)
     hidden_grad = norm_pulled(first_halves, hidden, norm_gain, middle_grad)[0]
     block_output = middle + whole_rows(*ffn_halves)
-    mix_kept = finished(mix_given, mix_kept, 1, 2)
+    mix_kept = finished(mix_given, after(mix_kept, hidden_grad, block_output), 1, 2)
+    hidden_units = gate_cot.shape[1]
+    w_gate_grad, w_up_grad = both_grad[:, :hidden_units], both_grad[:, hidden_units:]
+    lin_grad = after(lin_grad, hidden_grad, block_output, w_gate_grad, w_up_grad, mix_kept)
+    lin_grads = tuple(lin_grad[:, index * width : (index + 1) * width] for index in range(3))
     rest_rows = rest.shape[1]
     w_down_grad = jnp.concatenate([lead_kept, mix_kept[:rest_rows]], axis=0)
     w_output_grad = mix_kept[rest_rows:]

time: 1030 us -> 940 us (0.913)
  waiting for transfers between devices: 473 us -> 403 us
  other arithmetic: 83.3 us -> 71.7 us
    ppermute x26, waiting for transfers between devices: 422 us -> 368 us  [swap(): return lax.ppermute(block, axis, [(i, i ^ bit) for i in range(count)])]
    ppermute x18, waiting for transfers between devices: 50.1 us -> 35 us  [shift(): return lax.ppermute(block, axis, route)]
    dot_general x27 -> x26, matrix products: 178 us -> 169 us  [matmul(): lax.dot_general(left, right, (((left_dim,), (right_dim,)), ((), ())), pre...]
  transfers between devices with their start and end apart: 47 -> 46, of which waited for: 23 -> 27; matrix products, arithmetic and copies ran while one was open for 22% -> 21% of each run, Pallas kernels for 14% -> 16%
where the time goes in v3:
time: 940 us; the launch traced here: 930 us
  waiting for transfers between devices  403 us (43%)
  matrix products  172 us (18%)
  Pallas kernels  148 us (16%)
  starting transfers between devices  77.8 us (8%)
  other arithmetic  71.7 us (8%)
  local copies, waits for them, and re-layouts  40.9 us (4%)
  between operations  16.2 us (2%)
    ppermute x26, waiting for transfers between devices, swap(): return lax.ppermute(block, axis, [(i, i ^ bit) for i in range(count)])  368 us
    dot_general x26, matrix products, matmul(): lax.dot_general(left, right, (((left_dim,), (right_dim,)), ((), ())), pre...  169 us
    ppermute x18, starting transfers between devices, shift(): return lax.ppermute(block, axis, route)  49.5 us
    pallas_call x1, Pallas kernels, delta_backward(): on_chip(backward_kernel, 'delta_backward', grid=(blocks,), in_specs=[scal...  37 us
    pallas_call x2, Pallas kernels, norm_pulled(): on_chip(norm_pull_kernel, 'norm_pull', grid=(8,), in_specs=[scalars(), ha...  35.1 us
    ppermute x18, waiting for transfers between devices, shift(): return lax.ppermute(block, axis, route)  35 us
    pallas_call x1, Pallas kernels, delta_forward(): on_chip(forward_kernel, 'delta_forward', grid=(blocks,), in_specs=[scalar...  33.1 us
    ppermute x26, starting transfers between devices, swap(): return lax.ppermute(block, axis, [(i, i ^ bit) for i in range(count)])  28.2 us
  transfers between devices with their start and end apart: 46, of which 27 were waited for; matrix products, arithmetic and copies ran while one was open for 21% of the time, Pallas kernels for 16%

profile of v3, /device:TPU:0, one launch (start us, length us, event | category | flops | bytes accessed | tf_op | source)
XLA Modules:
  0.0 929.5 jit_solution(5639402625027613613)
XLA Ops:
  34.0 33.1 %delta_forward.1 = (f32[8,4,128,128]{3,2,1,0:T(8,128)S(1)}, f32[1024,512]{1,0:T(8,128)S(1)}, f32[1024,512]{1,0:T(8,128)}, f32[8,4,128,256]{3,2,1,0:T(8,128)}, f32[4,128,256]{2,1,0:T(8,128)S(1)}) custom-call(s32[7]{0:T(128)S(1)} %copy-done.25, s32[1]{0:T(128)} %bitcast.base, f32[1024,512]{1,0:T(8,128)} %copy-done.32, f32[1024,512]{1,0:T(8,128)} %copy-done.31, ...), custom_call_target="tpu_custom_call" | custom-call | flops 1 | bytes 1 | tf_op jit(solution)/shard_map/delta_forward/pallas_call | solution.py:450
  143.4 8.9 convolution_add_fusion.2
  152.3 8.8 collective-permute-done.12.first
  169.8 9.1 multiply_reduce_fusion.1
  189.8 13.1 %multiply_convert_fusion.4 = (bf16[1024,1408]{1,0:T(8,128)(2,1)S(1)}, f32[1024,1408]{1,0:T(8,128)}) fusion(f32[1024,1408]{1,0:T(8,128)S(1)} %fusion.52, bf16[1024,2048]{1,0:T(8,128)(2,1)S(1)} %multiply_convert_fusion, bf16[2048,1408]{1,0:T(8,128)(2,1)} %param.33), kind=kOutput, calls=%fused_computation.14 | convolution fusion | flops 5914230784 | bytes 24379392 | tf_op jit(solution)/shard_map/dot_general | solution.py:775
  207.5 14.4 %multiply_convert_fusion.2 = (bf16[1024,1408]{1,0:T(8,128)(2,1)}, bf16[1024,1408]{1,0:T(8,128)(2,1)}) fusion(f32[1024,1408]{1,0:T(8,128)} %copy-done.80, f32[1024,1408]{1,0:T(8,128)} %get-tuple-element.147, bf16[1024,2048]{1,0:T(8,128)(2,1)S(1)} %copy-done.37, bf16[1408,2048]{1,0:T(8,128)(2,1)} %param.34), kind=kOutput, calls=%fused_computation.12 | convolution fusion | flops 5924323328 | bytes 27262976 | tf_op jit(solution)/shard_map/dot_general | solution.py:775
  221.9 18.1 %fusion.1 = f32[2048,2816]{1,0:T(8,128)} fusion(bf16[1024,2048]{1,0:T(8,128)(2,1)S(1)} %copy-done.55, bf16[1024,1408]{1,0:T(8,128)(2,1)} %get-tuple-element.78, bf16[1024,1408]{1,0:T(8,128)(2,1)} %get-tuple-element.77), kind=kOutput, calls=%fused_computation.8 | convolution fusion | flops 11822694400 | bytes 33030144 | tf_op jit(solution)/shard_map/dot_general | solution.py:775
  240.1 10.0 %fusion.53 = f32[1024,2048]{1,0:T(8,128)S(1)} fusion(bf16[1024,1408]{1,0:T(8,128)(2,1)} %get-tuple-element.77, bf16[2048,1408]{1,0:T(8,128)(2,1)} %param.32), kind=kOutput, calls=%fused_computation.118 | convolution fusion | flops 5905580032 | bytes 17039360 | tf_op jit(solution)/shard_map/dot_general | solution.py:775
  250.1 8.8 convolution_add_fusion
  275.4 9.2 fusion.54
  291.4 102.5 %collective-permute-done.29 = f32[1024,1024]{1,0:T(8,128)} collective-permute-done((f32[1024,1024]{1,0:T(8,128)}, f32[1024,1024]{1,0:T(8,128)}, u32[]{:S(2)}, u32[]{:S(2)}) %collective-permute-start.29) | collective-permute-done | bytes 4194336 | tf_op jit(solution)/shard_map/ppermute | solution.py:643
  413.4 17.0 %norm_pull.2 = (f32[1024,2048]{1,0:T(8,128)}, bf16[1024,2048]{1,0:T(8,128)(2,1)S(1)}, f32[1,2048]{1,0:T(1,128)S(1)}) custom-call(s32[1]{0:T(128)} %bitcast.10.odd, f32[512,2048]{1,0:T(8,128)} %copy-done.33, f32[512,2048]{1,0:T(8,128)} %copy-done.56, f32[1024,2048]{1,0:T(8,128)} %get-tuple-element.145.values, f32[1,2048]{1,0:T(1,128)S(1)} %bitcast.79, ...), custom_call_target="tpu_custom_call" | custom-call | flops 1 | bytes 1 | tf_op jit(solution)/shard_map/norm_pull/pallas_call | solution.py:542
  440.6 8.1 collective-permute-done.21
  486.6 10.9 %collective-permute-done.17 = f32[512,2048]{1,0:T(8,128)} collective-permute-done((f32[512,2048]{1,0:T(8,128)}, f32[512,2048]{1,0:T(8,128)}, u32[]{:S(2)}, u32[]{:S(2)}) %collective-permute-start.17) | collective-permute-done | bytes 4194336 | tf_op jit(solution)/shard_map/ppermute | solution.py:643
  504.1 37.0 %delta_backward.1 = (f32[1024,512]{1,0:T(8,128)S(1)}, f32[1024,512]{1,0:T(8,128)S(1)}, f32[1024,512]{1,0:T(8,128)}, f32[8,1536]{1,0:T(8,128)S(1)}, f32[1024,4]{1...) custom-call(s32[7]{0:T(128)S(1)} %copy-done.26, s32[1]{0:T(128)} %bitcast.base, ...), custom_call_target="tpu_custom_call" | custom-call | flops 1 | bytes 1 | tf_op jit(solution)/shard_map/delta_backward/pallas_call | solution.py:608
  553.0 9.2 fusion.56
  580.8 107.3 %collective-permute-done.32 = f32[896,1024]{1,0:T(8,128)S(1)} collective-permute-done((f32[896,1024]{1,0:T(8,128)S(1)}, f32[896,1024]{1,0:T(8,128)S(1)}, u32[]{:S(2)}, u32[]{:S(2)}) %collective-permute-start.32) | collective-permute-done | bytes 3670048 | tf_op jit(solution)/shard_map/ppermute | solution.py:643
  708.6 13.2 %multiply_reduce_fusion = (f32[2048]{0:T(1024)S(1)}, f32[1024,2048]{1,0:T(8,128)}) fusion(f32[1024,2048]{1,0:T(8,128)S(1)} %bitcast.90, f32[1024]{0:T(1024)S(1)} %copy-done.68, bf16[1024,4]{1,0:T(8,128)(2,1)S(1)} %get-tuple-element.104, bf16[2048,4]{0,1:T(4,128)(2,1)S(1)} %copy-done.70, f32[1024,2048]{1,0:T(8,128)} %fusion.59, f32[1024,2048]{1,0:T(8,128)} %fusion.57, ...), kind=kOutput, calls=%fused_computation.2 | convolution fusion | flops 29358080 | bytes 41979904 | tf_op jit(solution)/shard_map/dot_general | solution.py:775
  744.8 69.7 %collective-permute-done.38 = f32[1024,256]{1,0:T(8,128)S(1)} collective-permute-done((f32[1024,256]{1,0:T(8,128)S(1)}, f32[1024,256]{1,0:T(8,128)S(1)}, u32[]{:S(2)}, u32[]{:S(2)}) %collective-permute-start.38) | collective-permute-done | bytes 1048608 | tf_op jit(solution)/shard_map/ppermute | solution.py:643
  818.3 14.6 %collective-permute-done.36 = f32[512,2048]{1,0:T(8,128)} collective-permute-done((f32[512,2048]{1,0:T(8,128)S(1)}, f32[512,2048]{1,0:T(8,128)}, u32[]{:S(2)}, u32[]{:S(2)}) %collective-permute-start.36) | collective-permute-done | bytes 4194336 | tf_op jit(solution)/shard_map/ppermute | solution.py:643
  845.4 11.1 %collective-permute-done.41 = f32[18564]{0:T(1024)S(1)} collective-permute-done((f32[18564]{0:T(1024)S(1)}, f32[18564]{0:T(1024)S(1)}, u32[]{:S(2)}, u32[]{:S(2)}) %collective-permute-start.41) | collective-permute-done | bytes 74288 | tf_op jit(solution)/shard_map/ppermute | solution.py:643
  856.6 13.9 %fusion = f32[1024,2048]{1,0:T(8,128)} fusion(f32[1024,2048]{1,0:T(8,128)} %get-tuple-element.145.values, f32[512,2048]{1,0:T(8,128)} %collective-permute-done.18, f32[512,2048]{1,0:T(8,128)} %add.199, pred[]{:T(512)S(6)} %eq.10), kind=kLoop, calls=%fused_computation.1 | loop fusion | flops 8388608 | bytes 25165824 | tf_op jit(solution)/shard_map/add | solution.py:917
  881.8 18.1 %norm_pull.3 = (f32[1024,2048]{1,0:T(8,128)}, bf16[1024,2048]{1,0:T(8,128)(2,1)}, f32[1,2048]{1,0:T(1,128)}) custom-call(s32[1]{0:T(128)} %bitcast.10.odd, f32[512,2048]{1,0:T(8,128)} %add.222.part, f32[512,2048]{1,0:T(8,128)} %collective-permute-done.39.other, f32[1024,2048]{1,0:T(8,128)} %values.1, f32[1,2048]{1,0:T(1,128)S(1)} %bitcast.80, ...), custom_call_target="tpu_custom_call" | custom-call | flops 1 | bytes 1 | tf_op jit(solution)/shard_map/norm_pull/pallas_call | solution.py:542
  899.9 16.5 %collective-permute-done.43 = f32[896,256]{1,0:T(8,128)} collective-permute-done((f32[896,256]{1,0:T(8,128)}, f32[896,256]{1,0:T(8,128)}, u32[]{:S(2)}, u32[]{:S(2)}) %collective-permute-start.43) | collective-permute-done | bytes 917536 | tf_op jit(solution)/shard_map/ppermute | solution.py:643
  (376 shorter events, 330.6 us)
Async XLA Ops:
  7.2 825.6 %reduce-scatter.3.cloned.1.call-start = ((), (), s32[]{:S(2)}) async-start(), calls=%async_computation.2 | async-start | bytes 25952256 | tf_op jit(solution)/shard_map/reduce_scatter | solution.py:851
  11.5 100.7 %collective-permute-start.10 = (f32[512,2048]{1,0:T(8,128)}, f32[512,2048]{1,0:T(8,128)}, u32[]{:S(2)}, u32[]{:S(2)}) collective-permute-start(f32[512,2048]{1,0:T(8,128)} %convert_element_type.40.first), channel_id=1, source_target_pairs={{0,2},{1,3},{2,0},{3,1},{4,6},{5,7},{6,4},{7,5},{8,10},{9,11},{10,... | collective-permute-start | bytes 12582920 | tf_op jit(solution)/shard_map/ppermute | solution.py:643
  112.2 19.4 %collective-permute-start.11 = (f32[512,2048]{1,0:T(8,128)}, f32[512,2048]{1,0:T(8,128)}, u32[]{:S(2)}, u32[]{:S(2)}) collective-permute-start(f32[512,2048]{1,0:T(8,128)} %convert_element_type.40.first), channel_id=1, source_target_pairs={{0,1},{1,0},{2,3},{3,2},{4,5},{5,4},{6,7},{7,6},{8,9},{9,8},{10,11... | collective-permute-start | bytes 12582920 | tf_op jit(solution)/shard_map/ppermute | solution.py:643
  112.2 25.3 %collective-permute-start.13 = (f32[512,2048]{1,0:T(8,128)}, f32[512,2048]{1,0:T(8,128)}, u32[]{:S(2)}, u32[]{:S(2)}) collective-permute-start(f32[512,2048]{1,0:T(8,128)} %collective-permute-done.10.first), channel_id=1, source_target_pairs={{0,1},{1,0},{2,3},{3,2},{4,5},{5,4},{6,7},{7,6},{8,9},{9,8},{10,11... | collective-permute-start | bytes 12582920 | tf_op jit(solution)/shard_map/ppermute | solution.py:643
  112.7 16.0 %collective-permute-start.9 = (f32[1024,512]{1,0:T(8,128)}, f32[1024,512]{1,0:T(8,128)}, u32[]{:S(2)}, u32[]{:S(2)}) collective-permute-start(f32[1024,512]{1,0:T(8,128)} %get-tuple-element.70.first), channel_id=1, source_target_pairs={{0,1},{1,0},{2,3},{3,2},{4,5},{5,4},{6,7},{7,6},{8,9},{9,8},{10,11... | collective-permute-start | bytes 6291464 | tf_op jit(solution)/shard_map/ppermute | solution.py:643
  112.7 48.4 %collective-permute-start.12 = (f32[1024,512]{1,0:T(8,128)}, f32[1024,512]{1,0:T(8,128)}, u32[]{:S(2)}, u32[]{:S(2)}) collective-permute-start(f32[1024,512]{1,0:T(8,128)} %get-tuple-element.70.first), channel_id=1, source_target_pairs={{0,2},{1,3},{2,0},{3,1},{4,6},{5,7},{6,4},{7,5},{8,10},{9,11},{10,... | collective-permute-start | bytes 6291464 | tf_op jit(solution)/shard_map/ppermute | solution.py:643
  240.1 678.4 %reduce-scatter.5.cloned.1.call-start = ((), (), s32[]{:S(2)}) async-start(), calls=%async_computation.3 | async-start | bytes 14155776 | tf_op jit(solution)/shard_map/reduce_scatter | solution.py:898
  263.7 130.1 %collective-permute-start.29 = (f32[1024,1024]{1,0:T(8,128)}, f32[1024,1024]{1,0:T(8,128)}, u32[]{:S(2)}, u32[]{:S(2)}) collective-permute-start(f32[1024,1024]{1,0:T(8,128)} %fusion.10), channel_id=1, source_target_pairs={{0,4},{4,0},{8,12},{12,8},{16,20},{20,16},{24,28},{28,24},{1,5},{5... | collective-permute-start | bytes 12582920 | tf_op jit(solution)/shard_map/ppermute | solution.py:643
  285.2 115.4 %collective-permute-start.16 = (f32[512,2048]{1,0:T(8,128)S(1)}, f32[512,2048]{1,0:T(8,128)S(1)}, u32[]{:S(2)}, u32[]{:S(2)}) collective-permute-start(f32[512,2048]{1,0:T(8,128)S(1)} %constant_dynamic-slice_fusion.1), channel_id=1, source_target_pairs={{0,1},{1,0},{2,3},{3,2},{4,5},{5,4},{6,7},{7,6},{8,9},{9,8},{10,11... | collective-permute-start | bytes 12582920 | tf_op jit(solution)/shard_map/ppermute | solution.py:643
  285.4 117.9 %collective-permute-start.19 = (f32[512,2048]{1,0:T(8,128)S(1)}, f32[512,2048]{1,0:T(8,128)S(1)}, u32[]{:S(2)}, u32[]{:S(2)}) collective-permute-start(f32[512,2048]{1,0:T(8,128)S(1)} %dynamic-slice_add_fusion.2), channel_id=1, source_target_pairs={{0,2},{1,3},{2,0},{3,1},{4,6},{5,7},{6,4},{7,5},{8,10},{9,11},{10,... | collective-permute-start | bytes 12582920 | tf_op jit(solution)/shard_map/ppermute | solution.py:643
  404.2 93.3 %collective-permute-start.17 = (f32[512,2048]{1,0:T(8,128)}, f32[512,2048]{1,0:T(8,128)}, u32[]{:S(2)}, u32[]{:S(2)}) collective-permute-start(f32[512,2048]{1,0:T(8,128)} %dynamic-slice_add_fusion.1), channel_id=1, source_target_pairs={{0,2},{1,3},{2,0},{3,1},{4,6},{5,7},{6,4},{7,5},{8,10},{9,11},{10,... | collective-permute-start | bytes 12582920 | tf_op jit(solution)/shard_map/ppermute | solution.py:643
  439.3 13.1 %collective-permute-start.25 = (f32[2,128,128]{2,1,0:T(8,128)S(1)}, f32[2,128,128]{2,1,0:T(8,128)S(1)}, u32[]{:S(2)}, u32[]{:S(2)}) collective-permute-start(f32[2,128,128]{2,1,0:T(8,128)S(1)} %get-tuple-element.134), channel_id=1, source_target_pairs={{4,0},{8,4},{12,8},{16,12},{20,16},{24,20},{28,24},{5,1},{9,5},{13... | collective-permute-start | bytes 393224 | tf_op jit(solution)/shard_map/ppermute | solution.py:649
  452.7 12.0 %collective-permute-start.26 = (f32[2,128,128]{2,1,0:T(8,128)S(1)}, f32[2,128,128]{2,1,0:T(8,128)S(1)}, u32[]{:S(2)}, u32[]{:S(2)}) collective-permute-start(f32[2,128,128]{2,1,0:T(8,128)S(1)} %convolution_add_fusion.6), channel_id=1, source_target_pairs={{4,0},{8,4},{12,8},{16,12},{20,16},{24,20},{28,24},{5,1},{9,5},{13... | collective-permute-start | bytes 393224 | tf_op jit(solution)/shard_map/ppermute | solution.py:649
  459.3 11.0 %collective-permute-start.23 = (f32[2,128,128]{2,1,0:T(8,128)S(1)}, f32[2,128,128]{2,1,0:T(8,128)S(1)}, u32[]{:S(2)}, u32[]{:S(2)}) collective-permute-start(f32[2,128,128]{2,1,0:T(8,128)S(1)} %convolution_add_fusion.8), channel_id=1, source_target_pairs={{4,0},{8,4},{12,8},{16,12},{20,16},{24,20},{28,24},{5,1},{9,5},{13... | collective-permute-start | bytes 393224 | tf_op jit(solution)/shard_map/ppermute | solution.py:649
  484.1 61.3 %collective-permute-start.31 = (f32[1024,512]{1,0:T(8,128)}, f32[1024,512]{1,0:T(8,128)}, u32[]{:S(2)}, u32[]{:S(2)}) collective-permute-start(f32[1024,512]{1,0:T(8,128)} %slice.230), channel_id=1, source_target_pairs={{0,8},{4,12},{8,0},{12,4},{16,24},{20,28},{24,16},{28,20},{1,9},{5... | collective-permute-start | bytes 6291464 | tf_op jit(solution)/shard_map/ppermute | solution.py:643
  573.2 114.8 %collective-permute-start.32 = (f32[896,1024]{1,0:T(8,128)S(1)}, f32[896,1024]{1,0:T(8,128)S(1)}, u32[]{:S(2)}, u32[]{:S(2)}) collective-permute-start(f32[896,1024]{1,0:T(8,128)S(1)} %pad_maximum_fusion.1), channel_id=1, source_target_pairs={{0,4},{4,0},{8,12},{12,8},{16,20},{20,16},{24,28},{28,24},{1,5},{5... | collective-permute-start | bytes 11010056 | tf_op jit(solution)/shard_map/ppermute | solution.py:643
  740.7 92.2 %collective-permute-start.36 = (f32[512,2048]{1,0:T(8,128)S(1)}, f32[512,2048]{1,0:T(8,128)}, u32[]{:S(2)}, u32[]{:S(2)}) collective-permute-start(f32[512,2048]{1,0:T(8,128)S(1)} %dynamic-slice_add_fusion), channel_id=1, source_target_pairs={{0,2},{1,3},{2,0},{3,1},{4,6},{5,7},{6,4},{7,5},{8,10},{9,11},{10,... | collective-permute-start | bytes 12582920 | tf_op jit(solution)/shard_map/ppermute | solution.py:643
  742.2 74.2 %collective-permute-start.37 = (f32[896,512]{1,0:T(8,128)S(1)}, f32[896,512]{1,0:T(8,128)S(1)}, u32[]{:S(2)}, u32[]{:S(2)}) collective-permute-start(f32[896,512]{1,0:T(8,128)S(1)} %copy-done.63), channel_id=1, source_target_pairs={{0,8},{4,12},{8,0},{12,4},{16,24},{20,28},{24,16},{28,20},{1,9},{5... | collective-permute-start | bytes 5505032 | tf_op jit(solution)/shard_map/ppermute | solution.py:643
  742.2 114.4 %collective-permute-start.18 = (f32[512,2048]{1,0:T(8,128)}, f32[512,2048]{1,0:T(8,128)}, u32[]{:S(2)}, u32[]{:S(2)}) collective-permute-start(f32[512,2048]{1,0:T(8,128)} %add.199), channel_id=1, source_target_pairs={{0,1},{1,0},{2,3},{3,2},{4,5},{5,4},{6,7},{7,6},{8,9},{9,8},{10,11... | collective-permute-start | bytes 12582920 | tf_op jit(solution)/shard_map/ppermute | solution.py:643
  742.2 72.2 %collective-permute-start.38 = (f32[1024,256]{1,0:T(8,128)S(1)}, f32[1024,256]{1,0:T(8,128)S(1)}, u32[]{:S(2)}, u32[]{:S(2)}) collective-permute-start(f32[1024,256]{1,0:T(8,128)S(1)} %copy-done.64), channel_id=1, source_target_pairs={{0,16},{4,20},{8,24},{12,28},{16,0},{20,4},{24,8},{28,12},{1,17},{... | collective-permute-start | bytes 3145736 | tf_op jit(solution)/shard_map/ppermute | solution.py:643
  839.6 42.2 %collective-permute-start.39 = (f32[512,2048]{1,0:T(8,128)}, f32[512,2048]{1,0:T(8,128)}, u32[]{:S(2)}, u32[]{:S(2)}) collective-permute-start(f32[512,2048]{1,0:T(8,128)} %add.222.part), channel_id=1, source_target_pairs={{0,1},{1,0},{2,3},{3,2},{4,5},{5,4},{6,7},{7,6},{8,9},{9,8},{10,11... | collective-permute-start | bytes 12582920 | tf_op jit(solution)/shard_map/ppermute | solution.py:643
  845.3 11.2 %collective-permute-start.41 = (f32[18564]{0:T(1024)S(1)}, f32[18564]{0:T(1024)S(1)}, u32[]{:S(2)}, u32[]{:S(2)}) collective-permute-start(f32[18564]{0:T(1024)S(1)} %add.223), channel_id=1, source_target_pairs={{0,8},{4,12},{8,0},{12,4},{16,24},{20,28},{24,16},{28,20},{1,9},{5... | collective-permute-start | bytes 222776 | tf_op jit(solution)/shard_map/ppermute | solution.py:643
  856.5 14.0 %collective-permute-start.42 = (f32[18564]{0:T(1024)S(1)}, f32[18564]{0:T(1024)S(1)}, u32[]{:S(2)}, u32[]{:S(2)}) collective-permute-start(f32[18564]{0:T(1024)S(1)} %add.224), channel_id=1, source_target_pairs={{0,16},{4,20},{8,24},{12,28},{16,0},{20,4},{24,8},{28,12},{1,17},{... | collective-permute-start | bytes 222776 | tf_op jit(solution)/shard_map/ppermute | solution.py:643
  871.6 44.8 %collective-permute-start.43 = (f32[896,256]{1,0:T(8,128)}, f32[896,256]{1,0:T(8,128)}, u32[]{:S(2)}, u32[]{:S(2)}) collective-permute-start(f32[896,256]{1,0:T(8,128)} %get-tuple-element.126), channel_id=1, source_target_pairs={{0,16},{4,20},{8,24},{12,28},{16,0},{20,4},{24,8},{28,12},{1,17},{... | collective-permute-start | bytes 2752520 | tf_op jit(solution)/shard_map/ppermute | solution.py:643
  (108 other events, 1506.6 us)
Sparse Core Ops, SparseCore 0:
  240.2 394.7 reduce-scatter.2
  638.6 260.5 reduce-scatter.4

commit v4 on v3

--- a/solution.py
+++ b/solution.py
@@ -900,7 +900,8 @@
         [rest_kept, product(branch_ordered[:, half:], headed, False)], axis=0
     )
     mix_given, mix_kept = received(mix_given, after(mix_kept, lin_term), 1, 0)
-    late_cots, strength_cot = after((cots, strength_cot), lin_term, mix_given)
+    lead_kept = finished(lead_given, after(lead_kept, lin_term), 1, 2)
+    late_cots, strength_cot = after((cots, strength_cot), lin_term, mix_given, lead_kept)
     first_part = matmul(late_cots[0], w_query, 1, 1)
     first_part = first_part + matmul(late_cots[1], w_key, 1, 1)
     first_part = first_part + matmul(late_cots[2], w_value, 1, 1)
@@ -910,12 +911,12 @@
         jnp.concatenate([norm_gain_part, head_gain_part.reshape(-1)]), "head"
     )
     first_begun = after(begun_over_head(first_part), shared)
-    lead_kept = finished(lead_given, lead_kept, 1, 2)
     mix_given, mix_kept = received(mix_given, after(mix_kept, first_begun), 1, 1)
-    first_halves = ended_over_head(first_begun, mix_given, lead_kept, both_grad)
+    first_halves = ended_over_head(first_begun, mix_given, both_grad)
+    mix_kept = finished(mix_given, after(mix_kept, first_halves[0]), 1, 2)
+    first_halves = after(first_halves, mix_kept)
     hidden_grad = norm_pulled(first_halves, hidden, norm_gain, middle_grad)[0]
     block_output = middle + whole_rows(*ffn_halves)
-    mix_kept = finished(mix_given, after(mix_kept, hidden_grad, block_output), 1, 2)
     hidden_units = gate_cot.shape[1]
     w_gate_grad, w_up_grad = both_grad[:, :hidden_units], both_grad[:, hidden_units:]
     lin_grad = after(lin_grad, hidden_grad, block_output, w_gate_grad, w_up_grad, mix_kept)

time: 940 us -> 987 us (1.050)
  waiting for transfers between devices: 403 us -> 453 us
    ppermute x26, waiting for transfers between devices: 368 us -> 417 us  [swap(): return lax.ppermute(block, axis, [(i, i ^ bit) for i in range(count)])]
  transfers between devices with their start and end apart: 46 -> 46, of which waited for: 27 -> 25; matrix products, arithmetic and copies ran while one was open for 21% -> 20% of each run, Pallas kernels for 16% -> 15%
where the time goes in v4:
time: 987 us; the launch traced here: 977 us
  waiting for transfers between devices  453 us (46%)
  matrix products  172 us (17%)
  Pallas kernels  148 us (15%)
  starting transfers between devices  79.8 us (8%)
  other arithmetic  69.6 us (7%)
  local copies, waits for them, and re-layouts  37.9 us (4%)
  between operations  16.2 us (2%)
    ppermute x26, waiting for transfers between devices, swap(): return lax.ppermute(block, axis, [(i, i ^ bit) for i in range(count)])  417 us
    dot_general x26, matrix products, matmul(): lax.dot_general(left, right, (((left_dim,), (right_dim,)), ((), ())), pre...  170 us
    ppermute x18, starting transfers between devices, shift(): return lax.ppermute(block, axis, route)  49.5 us
    pallas_call x1, Pallas kernels, delta_backward(): on_chip(backward_kernel, 'delta_backward', grid=(blocks,), in_specs=[scal...  37 us
    ppermute x18, waiting for transfers between devices, shift(): return lax.ppermute(block, axis, route)  36.1 us
    pallas_call x2, Pallas kernels, norm_pulled(): on_chip(norm_pull_kernel, 'norm_pull', grid=(8,), in_specs=[scalars(), ha...  35.1 us
    pallas_call x1, Pallas kernels, delta_forward(): on_chip(forward_kernel, 'delta_forward', grid=(blocks,), in_specs=[scalar...  33.1 us
    ppermute x26, starting transfers between devices, swap(): return lax.ppermute(block, axis, [(i, i ^ bit) for i in range(count)])  30.3 us
  transfers between devices with their start and end apart: 46, of which 25 were waited for; matrix products, arithmetic and copies ran while one was open for 20% of the time, Pallas kernels for 15%

profile of v4, /device:TPU:0, one launch (start us, length us, event | category | flops | bytes accessed | tf_op | source)
XLA Modules:
  0.0 977.1 jit_solution(12801539537417697945)
XLA Ops:
  34.0 33.1 %delta_forward.1 = (f32[8,4,128,128]{3,2,1,0:T(8,128)S(1)}, f32[1024,512]{1,0:T(8,128)S(1)}, f32[1024,512]{1,0:T(8,128)}, f32[8,4,128,256]{3,2,1,0:T(8,128)}, f32[4,128,256]{2,1,0:T(8,128)S(1)}) custom-call(s32[7]{0:T(128)S(1)} %copy-done.25, s32[1]{0:T(128)} %bitcast.base, f32[1024,512]{1,0:T(8,128)} %copy-done.32, f32[1024,512]{1,0:T(8,128)} %copy-done.31, ...), custom_call_target="tpu_custom_call" | custom-call | flops 1 | bytes 1 | tf_op jit(solution)/shard_map/delta_forward/pallas_call | solution.py:450
  143.4 8.9 convolution_add_fusion.2
  152.3 8.8 collective-permute-done.12.first
  169.9 9.1 multiply_reduce_fusion.1
  189.9 13.1 %multiply_convert_fusion.4 = (bf16[1024,1408]{1,0:T(8,128)(2,1)S(1)}, f32[1024,1408]{1,0:T(8,128)}) fusion(f32[1024,1408]{1,0:T(8,128)S(1)} %fusion.53, bf16[1024,2048]{1,0:T(8,128)(2,1)S(1)} %multiply_convert_fusion, bf16[2048,1408]{1,0:T(8,128)(2,1)} %param.33), kind=kOutput, calls=%fused_computation.14 | convolution fusion | flops 5914230784 | bytes 24379392 | tf_op jit(solution)/shard_map/dot_general | solution.py:775
  207.4 14.4 %multiply_convert_fusion.2 = (bf16[1024,1408]{1,0:T(8,128)(2,1)}, bf16[1024,1408]{1,0:T(8,128)(2,1)}) fusion(f32[1024,1408]{1,0:T(8,128)} %copy-done.78, f32[1024,1408]{1,0:T(8,128)} %get-tuple-element.155, bf16[1024,2048]{1,0:T(8,128)(2,1)S(1)} %copy-done.37, bf16[1408,2048]{1,0:T(8,128)(2,1)} %param.34), kind=kOutput, calls=%fused_computation.12 | convolution fusion | flops 5924323328 | bytes 27262976 | tf_op jit(solution)/shard_map/dot_general | solution.py:775
  221.8 18.2 %fusion.1 = f32[2048,2816]{1,0:T(8,128)} fusion(bf16[1024,2048]{1,0:T(8,128)(2,1)S(1)} %copy-done.53, bf16[1024,1408]{1,0:T(8,128)(2,1)} %get-tuple-element.81, bf16[1024,1408]{1,0:T(8,128)(2,1)} %get-tuple-element.80), kind=kOutput, calls=%fused_computation.8 | convolution fusion | flops 11822694400 | bytes 33030144 | tf_op jit(solution)/shard_map/dot_general | solution.py:775
  240.1 10.0 %fusion.54 = f32[1024,2048]{1,0:T(8,128)S(1)} fusion(bf16[1024,1408]{1,0:T(8,128)(2,1)} %get-tuple-element.80, bf16[2048,1408]{1,0:T(8,128)(2,1)} %param.32), kind=kOutput, calls=%fused_computation.118 | convolution fusion | flops 5905580032 | bytes 17039360 | tf_op jit(solution)/shard_map/dot_general | solution.py:775
  250.1 8.8 convolution_add_fusion
  275.4 9.2 fusion.55
  291.3 102.5 %collective-permute-done.29 = f32[1024,1024]{1,0:T(8,128)} collective-permute-done((f32[1024,1024]{1,0:T(8,128)}, f32[1024,1024]{1,0:T(8,128)}, u32[]{:S(2)}, u32[]{:S(2)}) %collective-permute-start.29) | collective-permute-done | bytes 4194336 | tf_op jit(solution)/shard_map/ppermute | solution.py:643
  413.4 17.0 %norm_pull.2 = (f32[1024,2048]{1,0:T(8,128)}, bf16[1024,2048]{1,0:T(8,128)(2,1)S(1)}, f32[1,2048]{1,0:T(1,128)S(1)}) custom-call(s32[1]{0:T(128)} %bitcast.10.odd, f32[512,2048]{1,0:T(8,128)} %copy-done.33, f32[512,2048]{1,0:T(8,128)} %copy-done.54, f32[1024,2048]{1,0:T(8,128)} %get-tuple-element.153.values, f32[1,2048]{1,0:T(1,128)S(1)} %bitcast.79, ...), custom_call_target="tpu_custom_call" | custom-call | flops 1 | bytes 1 | tf_op jit(solution)/shard_map/norm_pull/pallas_call | solution.py:542
  440.7 8.1 collective-permute-done.21
  486.7 10.7 %collective-permute-done.17 = f32[512,2048]{1,0:T(8,128)} collective-permute-done((f32[512,2048]{1,0:T(8,128)}, f32[512,2048]{1,0:T(8,128)}, u32[]{:S(2)}, u32[]{:S(2)}) %collective-permute-start.17) | collective-permute-done | bytes 4194336 | tf_op jit(solution)/shard_map/ppermute | solution.py:643
  504.0 37.0 %delta_backward.1 = (f32[1024,512]{1,0:T(8,128)S(1)}, f32[1024,512]{1,0:T(8,128)S(1)}, f32[1024,512]{1,0:T(8,128)}, f32[8,1536]{1,0:T(8,128)S(1)}, f32[1024,4]{1...) custom-call(s32[7]{0:T(128)S(1)} %copy-done.26, s32[1]{0:T(128)} %bitcast.base, ...), custom_call_target="tpu_custom_call" | custom-call | flops 1 | bytes 1 | tf_op jit(solution)/shard_map/delta_backward/pallas_call | solution.py:608
  552.3 9.3 fusion.57
  561.6 7.5 arrange.3
  584.5 90.6 %collective-permute-done.33 = f32[1024,256]{1,0:T(8,128)S(1)} collective-permute-done((f32[1024,256]{1,0:T(8,128)S(1)}, f32[1024,256]{1,0:T(8,128)S(1)}, u32[]{:S(2)}, u32[]{:S(2)}) %collective-permute-start.33) | collective-permute-done | bytes 1048608 | tf_op jit(solution)/shard_map/ppermute | solution.py:643
  696.2 13.3 %multiply_reduce_fusion = (f32[2048]{0:T(1024)S(1)}, f32[1024,2048]{1,0:T(8,128)}) fusion(f32[1024,2048]{1,0:T(8,128)S(1)} %bitcast.90, f32[1024]{0:T(1024)S(1)} %copy-done.66, bf16[1024,4]{1,0:T(8,128)(2,1)S(1)} %get-tuple-element.108, bf16[2048,4]{0,1:T(4,128)(2,1)S(1)} %copy-done.68, f32[1024,2048]{1,0:T(8,128)} %fusion.60, f32[1024,2048]{1,0:T(8,128)} %fusion.58, ...), kind=kOutput, calls=%fused_computation.2 | convolution fusion | flops 29358080 | bytes 41979904 | tf_op jit(solution)/shard_map/dot_general | solution.py:775
  729.8 101.3 %collective-permute-done.38 = f32[896,512]{1,0:T(8,128)S(1)} collective-permute-done((f32[896,512]{1,0:T(8,128)S(1)}, f32[896,512]{1,0:T(8,128)S(1)}, u32[]{:S(2)}, u32[]{:S(2)}) %collective-permute-start.38) | collective-permute-done | bytes 1835040 | tf_op jit(solution)/shard_map/ppermute | solution.py:643
  854.7 13.6 %fusion = f32[1024,2048]{1,0:T(8,128)} fusion(f32[1024,2048]{1,0:T(8,128)} %get-tuple-element.153.values, f32[512,2048]{1,0:T(8,128)} %collective-permute-done.18, f32[512,2048]{1,0:T(8,128)} %add.199, pred[]{:T(512)S(6)} %eq.10), kind=kLoop, calls=%fused_computation.1 | loop fusion | flops 8388608 | bytes 25165824 | tf_op jit(solution)/shard_map/add | solution.py:919
  868.3 15.6 %collective-permute-done.43 = f32[18564]{0:T(1024)S(1)} collective-permute-done((f32[18564]{0:T(1024)S(1)}, f32[18564]{0:T(1024)S(1)}, u32[]{:S(2)}, u32[]{:S(2)}) %collective-permute-start.43) | collective-permute-done | bytes 74288 | tf_op jit(solution)/shard_map/ppermute | solution.py:643
  888.7 55.2 %collective-permute-done.40 = f32[896,256]{1,0:T(8,128)} collective-permute-done((f32[896,256]{1,0:T(8,128)}, f32[896,256]{1,0:T(8,128)}, u32[]{:S(2)}, u32[]{:S(2)}) %collective-permute-start.40) | collective-permute-done | bytes 917536 | tf_op jit(solution)/shard_map/ppermute | solution.py:643
  949.3 18.0 %norm_pull.3 = (f32[1024,2048]{1,0:T(8,128)}, bf16[1024,2048]{1,0:T(8,128)(2,1)}, f32[1,2048]{1,0:T(1,128)}) custom-call(s32[1]{0:T(128)} %bitcast.10.odd, f32[512,2048]{1,0:T(8,128)} %add.222.part, f32[512,2048]{1,0:T(8,128)} %collective-permute-done.39.other, f32[1024,2048]{1,0:T(8,128)} %values.1, f32[1,2048]{1,0:T(1,128)S(1)} %bitcast.80, ...), custom_call_target="tpu_custom_call" | custom-call | flops 1 | bytes 1 | tf_op jit(solution)/shard_map/norm_pull/pallas_call | solution.py:542
  (372 shorter events, 327.5 us)
Async XLA Ops:
  7.2 825.7 %reduce-scatter.3.cloned.1.call-start = ((), (), s32[]{:S(2)}) async-start(), calls=%async_computation.2 | async-start | bytes 25952256 | tf_op jit(solution)/shard_map/reduce_scatter | solution.py:851
  11.5 100.7 %collective-permute-start.10 = (f32[512,2048]{1,0:T(8,128)}, f32[512,2048]{1,0:T(8,128)}, u32[]{:S(2)}, u32[]{:S(2)}) collective-permute-start(f32[512,2048]{1,0:T(8,128)} %convert_element_type.40.first), channel_id=1, source_target_pairs={{0,2},{1,3},{2,0},{3,1},{4,6},{5,7},{6,4},{7,5},{8,10},{9,11},{10,... | collective-permute-start | bytes 12582920 | tf_op jit(solution)/shard_map/ppermute | solution.py:643
  112.2 19.4 %collective-permute-start.11 = (f32[512,2048]{1,0:T(8,128)}, f32[512,2048]{1,0:T(8,128)}, u32[]{:S(2)}, u32[]{:S(2)}) collective-permute-start(f32[512,2048]{1,0:T(8,128)} %convert_element_type.40.first), channel_id=1, source_target_pairs={{0,1},{1,0},{2,3},{3,2},{4,5},{5,4},{6,7},{7,6},{8,9},{9,8},{10,11... | collective-permute-start | bytes 12582920 | tf_op jit(solution)/shard_map/ppermute | solution.py:643
  112.2 25.3 %collective-permute-start.13 = (f32[512,2048]{1,0:T(8,128)}, f32[512,2048]{1,0:T(8,128)}, u32[]{:S(2)}, u32[]{:S(2)}) collective-permute-start(f32[512,2048]{1,0:T(8,128)} %collective-permute-done.10.first), channel_id=1, source_target_pairs={{0,1},{1,0},{2,3},{3,2},{4,5},{5,4},{6,7},{7,6},{8,9},{9,8},{10,11... | collective-permute-start | bytes 12582920 | tf_op jit(solution)/shard_map/ppermute | solution.py:643
  112.7 16.0 %collective-permute-start.9 = (f32[1024,512]{1,0:T(8,128)}, f32[1024,512]{1,0:T(8,128)}, u32[]{:S(2)}, u32[]{:S(2)}) collective-permute-start(f32[1024,512]{1,0:T(8,128)} %get-tuple-element.73.first), channel_id=1, source_target_pairs={{0,1},{1,0},{2,3},{3,2},{4,5},{5,4},{6,7},{7,6},{8,9},{9,8},{10,11... | collective-permute-start | bytes 6291464 | tf_op jit(solution)/shard_map/ppermute | solution.py:643
  112.8 48.4 %collective-permute-start.12 = (f32[1024,512]{1,0:T(8,128)}, f32[1024,512]{1,0:T(8,128)}, u32[]{:S(2)}, u32[]{:S(2)}) collective-permute-start(f32[1024,512]{1,0:T(8,128)} %get-tuple-element.73.first), channel_id=1, source_target_pairs={{0,2},{1,3},{2,0},{3,1},{4,6},{5,7},{6,4},{7,5},{8,10},{9,11},{10,... | collective-permute-start | bytes 6291464 | tf_op jit(solution)/shard_map/ppermute | solution.py:643
  240.0 727.3 %reduce-scatter.5.cloned.1.call-start = ((), (), s32[]{:S(2)}) async-start(), calls=%async_computation.3 | async-start | bytes 14155776 | tf_op jit(solution)/shard_map/reduce_scatter | solution.py:898
  263.7 130.1 %collective-permute-start.29 = (f32[1024,1024]{1,0:T(8,128)}, f32[1024,1024]{1,0:T(8,128)}, u32[]{:S(2)}, u32[]{:S(2)}) collective-permute-start(f32[1024,1024]{1,0:T(8,128)} %fusion.10), channel_id=1, source_target_pairs={{0,4},{4,0},{8,12},{12,8},{16,20},{20,16},{24,28},{28,24},{1,5},{5... | collective-permute-start | bytes 12582920 | tf_op jit(solution)/shard_map/ppermute | solution.py:643
  285.1 115.4 %collective-permute-start.16 = (f32[512,2048]{1,0:T(8,128)S(1)}, f32[512,2048]{1,0:T(8,128)S(1)}, u32[]{:S(2)}, u32[]{:S(2)}) collective-permute-start(f32[512,2048]{1,0:T(8,128)S(1)} %constant_dynamic-slice_fusion.1), channel_id=1, source_target_pairs={{0,1},{1,0},{2,3},{3,2},{4,5},{5,4},{6,7},{7,6},{8,9},{9,8},{10,11... | collective-permute-start | bytes 12582920 | tf_op jit(solution)/shard_map/ppermute | solution.py:643
  285.3 118.0 %collective-permute-start.19 = (f32[512,2048]{1,0:T(8,128)S(1)}, f32[512,2048]{1,0:T(8,128)S(1)}, u32[]{:S(2)}, u32[]{:S(2)}) collective-permute-start(f32[512,2048]{1,0:T(8,128)S(1)} %dynamic-slice_add_fusion.2), channel_id=1, source_target_pairs={{0,2},{1,3},{2,0},{3,1},{4,6},{5,7},{6,4},{7,5},{8,10},{9,11},{10,... | collective-permute-start | bytes 12582920 | tf_op jit(solution)/shard_map/ppermute | solution.py:643
  404.1 93.3 %collective-permute-start.17 = (f32[512,2048]{1,0:T(8,128)}, f32[512,2048]{1,0:T(8,128)}, u32[]{:S(2)}, u32[]{:S(2)}) collective-permute-start(f32[512,2048]{1,0:T(8,128)} %dynamic-slice_add_fusion.1), channel_id=1, source_target_pairs={{0,2},{1,3},{2,0},{3,1},{4,6},{5,7},{6,4},{7,5},{8,10},{9,11},{10,... | collective-permute-start | bytes 12582920 | tf_op jit(solution)/shard_map/ppermute | solution.py:643
  439.4 12.9 %collective-permute-start.25 = (f32[2,128,128]{2,1,0:T(8,128)S(1)}, f32[2,128,128]{2,1,0:T(8,128)S(1)}, u32[]{:S(2)}, u32[]{:S(2)}) collective-permute-start(f32[2,128,128]{2,1,0:T(8,128)S(1)} %get-tuple-element.142), channel_id=1, source_target_pairs={{4,0},{8,4},{12,8},{16,12},{20,16},{24,20},{28,24},{5,1},{9,5},{13... | collective-permute-start | bytes 393224 | tf_op jit(solution)/shard_map/ppermute | solution.py:649
  452.6 12.2 %collective-permute-start.26 = (f32[2,128,128]{2,1,0:T(8,128)S(1)}, f32[2,128,128]{2,1,0:T(8,128)S(1)}, u32[]{:S(2)}, u32[]{:S(2)}) collective-permute-start(f32[2,128,128]{2,1,0:T(8,128)S(1)} %convolution_add_fusion.6), channel_id=1, source_target_pairs={{4,0},{8,4},{12,8},{16,12},{20,16},{24,20},{28,24},{5,1},{9,5},{13... | collective-permute-start | bytes 393224 | tf_op jit(solution)/shard_map/ppermute | solution.py:649
  459.5 11.0 %collective-permute-start.23 = (f32[2,128,128]{2,1,0:T(8,128)S(1)}, f32[2,128,128]{2,1,0:T(8,128)S(1)}, u32[]{:S(2)}, u32[]{:S(2)}) collective-permute-start(f32[2,128,128]{2,1,0:T(8,128)S(1)} %convolution_add_fusion.8), channel_id=1, source_target_pairs={{4,0},{8,4},{12,8},{16,12},{20,16},{24,20},{28,24},{5,1},{9,5},{13... | collective-permute-start | bytes 393224 | tf_op jit(solution)/shard_map/ppermute | solution.py:649
  465.1 10.9 %collective-permute-start.27 = (f32[2,128,128]{2,1,0:T(8,128)S(1)}, f32[2,128,128]{2,1,0:T(8,128)S(1)}, u32[]{:S(2)}, u32[]{:S(2)}) collective-permute-start(f32[2,128,128]{2,1,0:T(8,128)S(1)} %convolution_add_fusion.5), channel_id=1, source_target_pairs={{4,0},{8,4},{12,8},{16,12},{20,16},{24,20},{28,24},{5,1},{9,5},{13... | collective-permute-start | bytes 393224 | tf_op jit(solution)/shard_map/ppermute | solution.py:649
  484.1 61.2 %collective-permute-start.31 = (f32[1024,512]{1,0:T(8,128)S(1)}, f32[1024,512]{1,0:T(8,128)}, u32[]{:S(2)}, u32[]{:S(2)}) collective-permute-start(f32[1024,512]{1,0:T(8,128)S(1)} %slice.230), channel_id=1, source_target_pairs={{0,8},{4,12},{8,0},{12,4},{16,24},{20,28},{24,16},{28,20},{1,9},{5... | collective-permute-start | bytes 6291464 | tf_op jit(solution)/shard_map/ppermute | solution.py:643
  572.6 102.6 %collective-permute-start.32 = (f32[896,1024]{1,0:T(8,128)S(1)}, f32[896,1024]{1,0:T(8,128)S(1)}, u32[]{:S(2)}, u32[]{:S(2)}) collective-permute-start(f32[896,1024]{1,0:T(8,128)S(1)} %pad_maximum_fusion.1), channel_id=1, source_target_pairs={{0,4},{4,0},{8,12},{12,8},{16,20},{20,16},{24,28},{28,24},{1,5},{5... | collective-permute-start | bytes 11010056 | tf_op jit(solution)/shard_map/ppermute | solution.py:643
  576.9 98.1 %collective-permute-start.33 = (f32[1024,256]{1,0:T(8,128)S(1)}, f32[1024,256]{1,0:T(8,128)S(1)}, u32[]{:S(2)}, u32[]{:S(2)}) collective-permute-start(f32[1024,256]{1,0:T(8,128)S(1)} %copy-done.62), channel_id=1, source_target_pairs={{0,16},{4,20},{8,24},{12,28},{16,0},{20,4},{24,8},{28,12},{1,17},{... | collective-permute-start | bytes 3145736 | tf_op jit(solution)/shard_map/ppermute | solution.py:643
  728.4 104.6 %collective-permute-start.37 = (f32[512,2048]{1,0:T(8,128)S(1)}, f32[512,2048]{1,0:T(8,128)}, u32[]{:S(2)}, u32[]{:S(2)}) collective-permute-start(f32[512,2048]{1,0:T(8,128)S(1)} %dynamic-slice_add_fusion), channel_id=1, source_target_pairs={{0,2},{1,3},{2,0},{3,1},{4,6},{5,7},{6,4},{7,5},{8,10},{9,11},{10,... | collective-permute-start | bytes 12582920 | tf_op jit(solution)/shard_map/ppermute | solution.py:643
  729.8 101.3 %collective-permute-start.38 = (f32[896,512]{1,0:T(8,128)S(1)}, f32[896,512]{1,0:T(8,128)S(1)}, u32[]{:S(2)}, u32[]{:S(2)}) collective-permute-start(f32[896,512]{1,0:T(8,128)S(1)} %copy-done.61), channel_id=1, source_target_pairs={{0,8},{4,12},{8,0},{12,4},{16,24},{20,28},{24,16},{28,20},{1,9},{5... | collective-permute-start | bytes 5505032 | tf_op jit(solution)/shard_map/ppermute | solution.py:643
  729.8 124.9 %collective-permute-start.18 = (f32[512,2048]{1,0:T(8,128)}, f32[512,2048]{1,0:T(8,128)}, u32[]{:S(2)}, u32[]{:S(2)}) collective-permute-start(f32[512,2048]{1,0:T(8,128)} %add.199), channel_id=1, source_target_pairs={{0,1},{1,0},{2,3},{3,2},{4,5},{5,4},{6,7},{7,6},{8,9},{9,8},{10,11... | collective-permute-start | bytes 12582920 | tf_op jit(solution)/shard_map/ppermute | solution.py:643
  839.7 109.6 %collective-permute-start.39 = (f32[512,2048]{1,0:T(8,128)}, f32[512,2048]{1,0:T(8,128)}, u32[]{:S(2)}, u32[]{:S(2)}) collective-permute-start(f32[512,2048]{1,0:T(8,128)} %add.222.part), channel_id=1, source_target_pairs={{0,1},{1,0},{2,3},{3,2},{4,5},{5,4},{6,7},{7,6},{8,9},{9,8},{10,11... | collective-permute-start | bytes 12582920 | tf_op jit(solution)/shard_map/ppermute | solution.py:643
  851.7 32.2 %collective-permute-start.43 = (f32[18564]{0:T(1024)S(1)}, f32[18564]{0:T(1024)S(1)}, u32[]{:S(2)}, u32[]{:S(2)}) collective-permute-start(f32[18564]{0:T(1024)S(1)} %add.225), channel_id=1, source_target_pairs={{0,16},{4,20},{8,24},{12,28},{16,0},{20,4},{24,8},{28,12},{1,17},{... | collective-permute-start | bytes 222776 | tf_op jit(solution)/shard_map/ppermute | solution.py:643
  852.7 91.1 %collective-permute-start.40 = (f32[896,256]{1,0:T(8,128)}, f32[896,256]{1,0:T(8,128)}, u32[]{:S(2)}, u32[]{:S(2)}) collective-permute-start(f32[896,256]{1,0:T(8,128)} %get-tuple-element.134), channel_id=1, source_target_pairs={{0,16},{4,20},{8,24},{12,28},{16,0},{20,4},{24,8},{28,12},{1,17},{... | collective-permute-start | bytes 2752520 | tf_op jit(solution)/shard_map/ppermute | solution.py:643
  (106 other events, 1573.0 us)
Sparse Core Ops, SparseCore 0:
  240.1 439.4 reduce-scatter.2
  683.2 266.0 reduce-scatter.4

commit v5 on v4

--- a/solution.py
+++ b/solution.py
@@ -910,9 +910,9 @@
     shared = summed_everywhere(
         jnp.concatenate([norm_gain_part, head_gain_part.reshape(-1)]), "head"
     )
-    first_begun = after(begun_over_head(first_part), shared)
-    mix_given, mix_kept = received(mix_given, after(mix_kept, first_begun), 1, 1)
-    first_halves = ended_over_head(first_begun, mix_given, both_grad)
+    mix_given, mix_kept = received(mix_given, after(mix_kept, first_part), 1, 1)
+    first_begun = after(begun_over_head(first_part), shared, mix_given)
+    first_halves = ended_over_head(first_begun, both_grad)
     mix_kept = finished(mix_given, after(mix_kept, first_halves[0]), 1, 2)
     first_halves = after(first_halves, mix_kept)
     hidden_grad = norm_pulled(first_halves, hidden, norm_gain, middle_grad)[0]

time: 987 us -> 1040 us (1.054)
  waiting for transfers between devices: 453 us -> 502 us
    ppermute x26, waiting for transfers between devices: 417 us -> 466 us  [swap(): return lax.ppermute(block, axis, [(i, i ^ bit) for i in range(count)])]
  transfers between devices with their start and end apart: 46 -> 46, of which waited for: 25 -> 26; matrix products, arithmetic and copies ran while one was open for 20% -> 19% of each run, Pallas kernels for 15% -> 14%
where the time goes in v5:
time: 1040 us; the launch traced here: 1030 us
  waiting for transfers between devices  502 us (48%)
  matrix products  172 us (17%)
  Pallas kernels  148 us (14%)
  starting transfers between devices  78.3 us (8%)
  other arithmetic  70.3 us (7%)
  local copies, waits for them, and re-layouts  39.7 us (4%)
  between operations  16.2 us (2%)
    ppermute x26, waiting for transfers between devices, swap(): return lax.ppermute(block, axis, [(i, i ^ bit) for i in range(count)])  466 us
    dot_general x26, matrix products, matmul(): lax.dot_general(left, right, (((left_dim,), (right_dim,)), ((), ())), pre...  169 us
    ppermute x18, starting transfers between devices, shift(): return lax.ppermute(block, axis, route)  49.5 us
    pallas_call x1, Pallas kernels, delta_backward(): on_chip(backward_kernel, 'delta_backward', grid=(blocks,), in_specs=[scal...  37 us
    ppermute x18, waiting for transfers between devices, shift(): return lax.ppermute(block, axis, route)  36.1 us
    pallas_call x2, Pallas kernels, norm_pulled(): on_chip(norm_pull_kernel, 'norm_pull', grid=(8,), in_specs=[scalars(), ha...  35 us
    pallas_call x1, Pallas kernels, delta_forward(): on_chip(forward_kernel, 'delta_forward', grid=(blocks,), in_specs=[scalar...  33.1 us
    ppermute x26, starting transfers between devices, swap(): return lax.ppermute(block, axis, [(i, i ^ bit) for i in range(count)])  28.8 us
  transfers between devices with their start and end apart: 46, of which 26 were waited for; matrix products, arithmetic and copies ran while one was open for 19% of the time, Pallas kernels for 14%

profile of v5, /device:TPU:0, one launch (start us, length us, event | category | flops | bytes accessed | tf_op | source)
XLA Modules:
  0.0 1026.8 jit_solution(13216466329904967517)
XLA Ops:
  34.0 33.1 %delta_forward.1 = (f32[8,4,128,128]{3,2,1,0:T(8,128)S(1)}, f32[1024,512]{1,0:T(8,128)S(1)}, f32[1024,512]{1,0:T(8,128)}, f32[8,4,128,256]{3,2,1,0:T(8,128)}, f32[4,128,256]{2,1,0:T(8,128)S(1)}) custom-call(s32[7]{0:T(128)S(1)} %copy-done.25, s32[1]{0:T(128)} %bitcast.base, f32[1024,512]{1,0:T(8,128)} %copy-done.33, f32[1024,512]{1,0:T(8,128)} %copy-done.32, ...), custom_call_target="tpu_custom_call" | custom-call | flops 1 | bytes 1 | tf_op jit(solution)/shard_map/delta_forward/pallas_call | solution.py:450
  143.4 8.9 convolution_add_fusion.2
  152.3 8.8 collective-permute-done.12.first
  169.9 9.1 multiply_reduce_fusion.1
  189.9 13.1 %multiply_convert_fusion.4 = (bf16[1024,1408]{1,0:T(8,128)(2,1)S(1)}, f32[1024,1408]{1,0:T(8,128)}) fusion(f32[1024,1408]{1,0:T(8,128)S(1)} %fusion.53, bf16[1024,2048]{1,0:T(8,128)(2,1)S(1)} %multiply_convert_fusion, bf16[2048,1408]{1,0:T(8,128)(2,1)} %param.33), kind=kOutput, calls=%fused_computation.14 | convolution fusion | flops 5914230784 | bytes 24379392 | tf_op jit(solution)/shard_map/dot_general | solution.py:775
  207.4 14.4 %multiply_convert_fusion.2 = (bf16[1024,1408]{1,0:T(8,128)(2,1)}, bf16[1024,1408]{1,0:T(8,128)(2,1)}) fusion(f32[1024,1408]{1,0:T(8,128)} %copy-done.77, f32[1024,1408]{1,0:T(8,128)} %get-tuple-element.155, bf16[1024,2048]{1,0:T(8,128)(2,1)S(1)} %copy-done.38, bf16[1408,2048]{1,0:T(8,128)(2,1)} %param.34), kind=kOutput, calls=%fused_computation.12 | convolution fusion | flops 5924323328 | bytes 27262976 | tf_op jit(solution)/shard_map/dot_general | solution.py:775
  221.8 18.2 %fusion.1 = f32[2048,2816]{1,0:T(8,128)} fusion(bf16[1024,2048]{1,0:T(8,128)(2,1)S(1)} %copy-done.53, bf16[1024,1408]{1,0:T(8,128)(2,1)} %get-tuple-element.81, bf16[1024,1408]{1,0:T(8,128)(2,1)} %get-tuple-element.80), kind=kOutput, calls=%fused_computation.8 | convolution fusion | flops 11822694400 | bytes 33030144 | tf_op jit(solution)/shard_map/dot_general | solution.py:775
  240.1 10.0 fusion.54
  250.1 8.8 convolution_add_fusion
  275.4 9.2 fusion.55
  291.3 102.5 %collective-permute-done.29 = f32[1024,1024]{1,0:T(8,128)} collective-permute-done((f32[1024,1024]{1,0:T(8,128)}, f32[1024,1024]{1,0:T(8,128)}, u32[]{:S(2)}, u32[]{:S(2)}) %collective-permute-start.29) | collective-permute-done | bytes 4194336 | tf_op jit(solution)/shard_map/ppermute | solution.py:643
  413.4 17.0 %norm_pull.2 = (f32[1024,2048]{1,0:T(8,128)}, bf16[1024,2048]{1,0:T(8,128)(2,1)S(1)}, f32[1,2048]{1,0:T(1,128)S(1)}) custom-call(s32[1]{0:T(128)} %bitcast.10.odd, f32[512,2048]{1,0:T(8,128)} %copy-done.34, f32[512,2048]{1,0:T(8,128)} %copy-done.54, f32[1024,2048]{1,0:T(8,128)} %get-tuple-element.153.values, f32[1,2048]{1,0:T(1,128)S(1)} %bitcast.79, ...), custom_call_target="tpu_custom_call" | custom-call | flops 1 | bytes 1 | tf_op jit(solution)/shard_map/norm_pull/pallas_call | solution.py:542
  440.7 8.1 collective-permute-done.21
  486.7 10.7 %collective-permute-done.17 = f32[512,2048]{1,0:T(8,128)} collective-permute-done((f32[512,2048]{1,0:T(8,128)}, f32[512,2048]{1,0:T(8,128)}, u32[]{:S(2)}, u32[]{:S(2)}) %collective-permute-start.17) | collective-permute-done | bytes 4194336 | tf_op jit(solution)/shard_map/ppermute | solution.py:643
  504.0 37.0 %delta_backward.1 = (f32[1024,512]{1,0:T(8,128)S(1)}, f32[1024,512]{1,0:T(8,128)S(1)}, f32[1024,512]{1,0:T(8,128)}, f32[8,1536]{1,0:T(8,128)S(1)}, f32[1024,4]{1...) custom-call(s32[7]{0:T(128)S(1)} %copy-done.26, s32[1]{0:T(128)} %bitcast.base, ...), custom_call_target="tpu_custom_call" | custom-call | flops 1 | bytes 1 | tf_op jit(solution)/shard_map/delta_backward/pallas_call | solution.py:608
  552.3 9.3 fusion.57
  584.4 90.6 %collective-permute-done.33 = f32[1024,256]{1,0:T(8,128)S(1)} collective-permute-done((f32[1024,256]{1,0:T(8,128)S(1)}, f32[1024,256]{1,0:T(8,128)S(1)}, u32[]{:S(2)}, u32[]{:S(2)}) %collective-permute-start.33) | collective-permute-done | bytes 1048608 | tf_op jit(solution)/shard_map/ppermute | solution.py:643
  696.2 13.3 %multiply_reduce_fusion = (f32[2048]{0:T(1024)S(1)}, f32[1024,2048]{1,0:T(8,128)}) fusion(f32[1024,2048]{1,0:T(8,128)S(1)} %bitcast.90, f32[1024]{0:T(1024)S(1)} %copy-done.65, bf16[1024,4]{1,0:T(8,128)(2,1)S(1)} %get-tuple-element.108, bf16[2048,4]{0,1:T(4,128)(2,1)S(1)} %copy-done.67, f32[1024,2048]{1,0:T(8,128)} %fusion.60, f32[1024,2048]{1,0:T(8,128)} %fusion.58, ...), kind=kOutput, calls=%fused_computation.2 | convolution fusion | flops 29358080 | bytes 41979904 | tf_op jit(solution)/shard_map/dot_general | solution.py:775
  723.5 107.0 %collective-permute-done.37 = f32[896,512]{1,0:T(8,128)} collective-permute-done((f32[896,512]{1,0:T(8,128)}, f32[896,512]{1,0:T(8,128)}, u32[]{:S(2)}, u32[]{:S(2)}) %collective-permute-start.37) | collective-permute-done | bytes 1835040 | tf_op jit(solution)/shard_map/ppermute | solution.py:643
  840.7 91.4 %collective-permute-done.38 = f32[512,2048]{1,0:T(8,128)} collective-permute-done((f32[512,2048]{1,0:T(8,128)S(1)}, f32[512,2048]{1,0:T(8,128)}, u32[]{:S(2)}, u32[]{:S(2)}) %collective-permute-start.38) | collective-permute-done | bytes 4194336 | tf_op jit(solution)/shard_map/ppermute | solution.py:643
  951.9 13.7 %fusion = f32[1024,2048]{1,0:T(8,128)} fusion(f32[1024,2048]{1,0:T(8,128)} %get-tuple-element.153.values, f32[512,2048]{1,0:T(8,128)} %collective-permute-done.18, f32[512,2048]{1,0:T(8,128)} %add.199, pred[]{:T(512)S(6)} %eq.10), kind=kLoop, calls=%fused_computation.1 | loop fusion | flops 8388608 | bytes 25165824 | tf_op jit(solution)/shard_map/add | solution.py:919
  965.7 9.3 collective-permute-done.43
  979.7 13.9 %collective-permute-done.40 = f32[896,256]{1,0:T(8,128)} collective-permute-done((f32[896,256]{1,0:T(8,128)}, f32[896,256]{1,0:T(8,128)}, u32[]{:S(2)}, u32[]{:S(2)}) %collective-permute-start.40) | collective-permute-done | bytes 917536 | tf_op jit(solution)/shard_map/ppermute | solution.py:643
  999.0 18.0 %norm_pull.3 = (f32[1024,2048]{1,0:T(8,128)}, bf16[1024,2048]{1,0:T(8,128)(2,1)}, f32[1,2048]{1,0:T(1,128)}) custom-call(s32[1]{0:T(128)} %bitcast.10.odd, f32[512,2048]{1,0:T(8,128)} %add.222.part, f32[512,2048]{1,0:T(8,128)} %collective-permute-done.39.other, f32[1024,2048]{1,0:T(8,128)} %values.1, f32[1,2048]{1,0:T(1,128)S(1)} %bitcast.80, ...), custom_call_target="tpu_custom_call" | custom-call | flops 1 | bytes 1 | tf_op jit(solution)/shard_map/norm_pull/pallas_call | solution.py:542
  (370 shorter events, 335.2 us)
Async XLA Ops:
  7.2 924.9 %reduce-scatter.3.cloned.1.call-start = ((), (), s32[]{:S(2)}) async-start(), calls=%async_computation.2 | async-start | bytes 25952256 | tf_op jit(solution)/shard_map/reduce_scatter | solution.py:851
  11.5 100.7 %collective-permute-start.10 = (f32[512,2048]{1,0:T(8,128)}, f32[512,2048]{1,0:T(8,128)}, u32[]{:S(2)}, u32[]{:S(2)}) collective-permute-start(f32[512,2048]{1,0:T(8,128)} %convert_element_type.40.first), channel_id=1, source_target_pairs={{0,2},{1,3},{2,0},{3,1},{4,6},{5,7},{6,4},{7,5},{8,10},{9,11},{10,... | collective-permute-start | bytes 12582920 | tf_op jit(solution)/shard_map/ppermute | solution.py:643
  112.2 19.4 %collective-permute-start.11 = (f32[512,2048]{1,0:T(8,128)}, f32[512,2048]{1,0:T(8,128)}, u32[]{:S(2)}, u32[]{:S(2)}) collective-permute-start(f32[512,2048]{1,0:T(8,128)} %convert_element_type.40.first), channel_id=1, source_target_pairs={{0,1},{1,0},{2,3},{3,2},{4,5},{5,4},{6,7},{7,6},{8,9},{9,8},{10,11... | collective-permute-start | bytes 12582920 | tf_op jit(solution)/shard_map/ppermute | solution.py:643
  112.2 25.3 %collective-permute-start.13 = (f32[512,2048]{1,0:T(8,128)}, f32[512,2048]{1,0:T(8,128)}, u32[]{:S(2)}, u32[]{:S(2)}) collective-permute-start(f32[512,2048]{1,0:T(8,128)} %collective-permute-done.10.first), channel_id=1, source_target_pairs={{0,1},{1,0},{2,3},{3,2},{4,5},{5,4},{6,7},{7,6},{8,9},{9,8},{10,11... | collective-permute-start | bytes 12582920 | tf_op jit(solution)/shard_map/ppermute | solution.py:643
  112.7 16.0 %collective-permute-start.9 = (f32[1024,512]{1,0:T(8,128)}, f32[1024,512]{1,0:T(8,128)}, u32[]{:S(2)}, u32[]{:S(2)}) collective-permute-start(f32[1024,512]{1,0:T(8,128)} %get-tuple-element.73.first), channel_id=1, source_target_pairs={{0,1},{1,0},{2,3},{3,2},{4,5},{5,4},{6,7},{7,6},{8,9},{9,8},{10,11... | collective-permute-start | bytes 6291464 | tf_op jit(solution)/shard_map/ppermute | solution.py:643
  112.7 48.4 %collective-permute-start.12 = (f32[1024,512]{1,0:T(8,128)}, f32[1024,512]{1,0:T(8,128)}, u32[]{:S(2)}, u32[]{:S(2)}) collective-permute-start(f32[1024,512]{1,0:T(8,128)} %get-tuple-element.73.first), channel_id=1, source_target_pairs={{0,2},{1,3},{2,0},{3,1},{4,6},{5,7},{6,4},{7,5},{8,10},{9,11},{10,... | collective-permute-start | bytes 6291464 | tf_op jit(solution)/shard_map/ppermute | solution.py:643
  240.0 777.0 %reduce-scatter.5.cloned.1.call-start = ((), (), s32[]{:S(2)}) async-start(), calls=%async_computation.3 | async-start | bytes 14155776 | tf_op jit(solution)/shard_map/reduce_scatter | solution.py:898
  263.7 130.1 %collective-permute-start.29 = (f32[1024,1024]{1,0:T(8,128)}, f32[1024,1024]{1,0:T(8,128)}, u32[]{:S(2)}, u32[]{:S(2)}) collective-permute-start(f32[1024,1024]{1,0:T(8,128)} %fusion.10), channel_id=1, source_target_pairs={{0,4},{4,0},{8,12},{12,8},{16,20},{20,16},{24,28},{28,24},{1,5},{5... | collective-permute-start | bytes 12582920 | tf_op jit(solution)/shard_map/ppermute | solution.py:643
  285.1 115.4 %collective-permute-start.16 = (f32[512,2048]{1,0:T(8,128)S(1)}, f32[512,2048]{1,0:T(8,128)S(1)}, u32[]{:S(2)}, u32[]{:S(2)}) collective-permute-start(f32[512,2048]{1,0:T(8,128)S(1)} %constant_dynamic-slice_fusion.1), channel_id=1, source_target_pairs={{0,1},{1,0},{2,3},{3,2},{4,5},{5,4},{6,7},{7,6},{8,9},{9,8},{10,11... | collective-permute-start | bytes 12582920 | tf_op jit(solution)/shard_map/ppermute | solution.py:643
  285.3 118.0 %collective-permute-start.19 = (f32[512,2048]{1,0:T(8,128)S(1)}, f32[512,2048]{1,0:T(8,128)S(1)}, u32[]{:S(2)}, u32[]{:S(2)}) collective-permute-start(f32[512,2048]{1,0:T(8,128)S(1)} %dynamic-slice_add_fusion.2), channel_id=1, source_target_pairs={{0,2},{1,3},{2,0},{3,1},{4,6},{5,7},{6,4},{7,5},{8,10},{9,11},{10,... | collective-permute-start | bytes 12582920 | tf_op jit(solution)/shard_map/ppermute | solution.py:643
  404.1 93.3 %collective-permute-start.17 = (f32[512,2048]{1,0:T(8,128)}, f32[512,2048]{1,0:T(8,128)}, u32[]{:S(2)}, u32[]{:S(2)}) collective-permute-start(f32[512,2048]{1,0:T(8,128)} %dynamic-slice_add_fusion.1), channel_id=1, source_target_pairs={{0,2},{1,3},{2,0},{3,1},{4,6},{5,7},{6,4},{7,5},{8,10},{9,11},{10,... | collective-permute-start | bytes 12582920 | tf_op jit(solution)/shard_map/ppermute | solution.py:643
  439.4 12.9 %collective-permute-start.25 = (f32[2,128,128]{2,1,0:T(8,128)S(1)}, f32[2,128,128]{2,1,0:T(8,128)S(1)}, u32[]{:S(2)}, u32[]{:S(2)}) collective-permute-start(f32[2,128,128]{2,1,0:T(8,128)S(1)} %get-tuple-element.142), channel_id=1, source_target_pairs={{4,0},{8,4},{12,8},{16,12},{20,16},{24,20},{28,24},{5,1},{9,5},{13... | collective-permute-start | bytes 393224 | tf_op jit(solution)/shard_map/ppermute | solution.py:649
  452.6 12.3 %collective-permute-start.26 = (f32[2,128,128]{2,1,0:T(8,128)S(1)}, f32[2,128,128]{2,1,0:T(8,128)S(1)}, u32[]{:S(2)}, u32[]{:S(2)}) collective-permute-start(f32[2,128,128]{2,1,0:T(8,128)S(1)} %convolution_add_fusion.6), channel_id=1, source_target_pairs={{4,0},{8,4},{12,8},{16,12},{20,16},{24,20},{28,24},{5,1},{9,5},{13... | collective-permute-start | bytes 393224 | tf_op jit(solution)/shard_map/ppermute | solution.py:649
  459.6 11.0 %collective-permute-start.23 = (f32[2,128,128]{2,1,0:T(8,128)S(1)}, f32[2,128,128]{2,1,0:T(8,128)S(1)}, u32[]{:S(2)}, u32[]{:S(2)}) collective-permute-start(f32[2,128,128]{2,1,0:T(8,128)S(1)} %convolution_add_fusion.8), channel_id=1, source_target_pairs={{4,0},{8,4},{12,8},{16,12},{20,16},{24,20},{28,24},{5,1},{9,5},{13... | collective-permute-start | bytes 393224 | tf_op jit(solution)/shard_map/ppermute | solution.py:649
  484.1 61.2 %collective-permute-start.31 = (f32[1024,512]{1,0:T(8,128)S(1)}, f32[1024,512]{1,0:T(8,128)}, u32[]{:S(2)}, u32[]{:S(2)}) collective-permute-start(f32[1024,512]{1,0:T(8,128)S(1)} %slice.230), channel_id=1, source_target_pairs={{0,8},{4,12},{8,0},{12,4},{16,24},{20,28},{24,16},{28,20},{1,9},{5... | collective-permute-start | bytes 6291464 | tf_op jit(solution)/shard_map/ppermute | solution.py:643
  572.5 102.6 %collective-permute-start.32 = (f32[896,1024]{1,0:T(8,128)S(1)}, f32[896,1024]{1,0:T(8,128)S(1)}, u32[]{:S(2)}, u32[]{:S(2)}) collective-permute-start(f32[896,1024]{1,0:T(8,128)S(1)} %pad_maximum_fusion.1), channel_id=1, source_target_pairs={{0,4},{4,0},{8,12},{12,8},{16,20},{20,16},{24,28},{28,24},{1,5},{5... | collective-permute-start | bytes 11010056 | tf_op jit(solution)/shard_map/ppermute | solution.py:643
  576.9 98.1 %collective-permute-start.33 = (f32[1024,256]{1,0:T(8,128)S(1)}, f32[1024,256]{1,0:T(8,128)S(1)}, u32[]{:S(2)}, u32[]{:S(2)}) collective-permute-start(f32[1024,256]{1,0:T(8,128)S(1)} %copy-done.61), channel_id=1, source_target_pairs={{0,16},{4,20},{8,24},{12,28},{16,0},{20,4},{24,8},{28,12},{1,17},{... | collective-permute-start | bytes 3145736 | tf_op jit(solution)/shard_map/ppermute | solution.py:643
  714.2 120.2 %collective-permute-start.34 = (f32[512,2048]{1,0:T(8,128)}, f32[512,2048]{1,0:T(8,128)}, u32[]{:S(2)}, u32[]{:S(2)}) collective-permute-start(f32[512,2048]{1,0:T(8,128)} %constant_dynamic-slice_fusion), channel_id=1, source_target_pairs={{0,1},{1,0},{2,3},{3,2},{4,5},{5,4},{6,7},{7,6},{8,9},{9,8},{10,11... | collective-permute-start | bytes 12582920 | tf_op jit(solution)/shard_map/ppermute | solution.py:643
  714.3 116.3 %collective-permute-start.37 = (f32[896,512]{1,0:T(8,128)}, f32[896,512]{1,0:T(8,128)}, u32[]{:S(2)}, u32[]{:S(2)}) collective-permute-start(f32[896,512]{1,0:T(8,128)} %get-tuple-element.128), channel_id=1, source_target_pairs={{0,8},{4,12},{8,0},{12,4},{16,24},{20,28},{24,16},{28,20},{1,9},{5... | collective-permute-start | bytes 5505032 | tf_op jit(solution)/shard_map/ppermute | solution.py:643
  839.4 92.7 %collective-permute-start.38 = (f32[512,2048]{1,0:T(8,128)S(1)}, f32[512,2048]{1,0:T(8,128)}, u32[]{:S(2)}, u32[]{:S(2)}) collective-permute-start(f32[512,2048]{1,0:T(8,128)S(1)} %dynamic-slice_add_fusion), channel_id=1, source_target_pairs={{0,2},{1,3},{2,0},{3,1},{4,6},{5,7},{6,4},{7,5},{8,10},{9,11},{10,... | collective-permute-start | bytes 12582920 | tf_op jit(solution)/shard_map/ppermute | solution.py:643
  840.7 111.3 %collective-permute-start.18 = (f32[512,2048]{1,0:T(8,128)}, f32[512,2048]{1,0:T(8,128)}, u32[]{:S(2)}, u32[]{:S(2)}) collective-permute-start(f32[512,2048]{1,0:T(8,128)} %add.199), channel_id=1, source_target_pairs={{0,1},{1,0},{2,3},{3,2},{4,5},{5,4},{6,7},{7,6},{8,9},{9,8},{10,11... | collective-permute-start | bytes 12582920 | tf_op jit(solution)/shard_map/ppermute | solution.py:643
  938.8 60.2 %collective-permute-start.39 = (f32[512,2048]{1,0:T(8,128)}, f32[512,2048]{1,0:T(8,128)}, u32[]{:S(2)}, u32[]{:S(2)}) collective-permute-start(f32[512,2048]{1,0:T(8,128)} %add.222.part), channel_id=1, source_target_pairs={{0,1},{1,0},{2,3},{3,2},{4,5},{5,4},{6,7},{7,6},{8,9},{9,8},{10,11... | collective-permute-start | bytes 12582920 | tf_op jit(solution)/shard_map/ppermute | solution.py:643
  949.0 26.0 %collective-permute-start.43 = (f32[18564]{0:T(1024)S(1)}, f32[18564]{0:T(1024)S(1)}, u32[]{:S(2)}, u32[]{:S(2)}) collective-permute-start(f32[18564]{0:T(1024)S(1)} %add.225), channel_id=1, source_target_pairs={{0,16},{4,20},{8,24},{12,28},{16,0},{20,4},{24,8},{28,12},{1,17},{... | collective-permute-start | bytes 222776 | tf_op jit(solution)/shard_map/ppermute | solution.py:643
  949.2 44.4 %collective-permute-start.40 = (f32[896,256]{1,0:T(8,128)}, f32[896,256]{1,0:T(8,128)}, u32[]{:S(2)}, u32[]{:S(2)}) collective-permute-start(f32[896,256]{1,0:T(8,128)} %get-tuple-element.134), channel_id=1, source_target_pairs={{0,16},{4,20},{8,24},{12,28},{16,0},{20,4},{24,8},{28,12},{1,17},{... | collective-permute-start | bytes 2752520 | tf_op jit(solution)/shard_map/ppermute | solution.py:643
  (105 other events, 1426.0 us)
Sparse Core Ops, SparseCore 0:
  240.1 439.5 reduce-scatter.2
  683.3 244.6 reduce-scatter.4

commit v6 on v3

--- a/solution.py
+++ b/solution.py
@@ -840,7 +840,7 @@
     silu_gate = gate_rows * sigma
     active = (silu_gate * upward).astype(BF16)
     half = ffn_cot.shape[1] // 2
-    split = active.shape[1] // 128 * 3 // 4 * 128
+    split = active.shape[1] // 128 * 7 // 8 * 128
     lead, rest = active[:, :split], active[:, split:]
     lead_given = product(cot_ordered[:, :half], lead, False)
     ffn_cot = after(ffn_cot, lead_given)

time: 940 us -> 976 us (1.038)
  starting transfers between devices: 77.8 us -> 125 us
    ppermute x26, starting transfers between devices: 28.2 us -> 75 us  [swap(): return lax.ppermute(block, axis, [(i, i ^ bit) for i in range(count)])]
  transfers between devices with their start and end apart: 46 -> 46, of which waited for: 27 -> 26; matrix products, arithmetic and copies ran while one was open for 21% -> 20% of each run, Pallas kernels for 16% -> 15%
where the time goes in v6:
time: 976 us; the launch traced here: 970 us
  waiting for transfers between devices  399 us (41%)
  matrix products  172 us (18%)
  Pallas kernels  148 us (15%)
  starting transfers between devices  125 us (13%)
  other arithmetic  69.5 us (7%)
  local copies, waits for them, and re-layouts  40.8 us (4%)
  between operations  15.9 us (2%)
    ppermute x26, waiting for transfers between devices, swap(): return lax.ppermute(block, axis, [(i, i ^ bit) for i in range(count)])  365 us
    dot_general x26, matrix products, matmul(): lax.dot_general(left, right, (((left_dim,), (right_dim,)), ((), ())), pre...  169 us
    ppermute x26, starting transfers between devices, swap(): return lax.ppermute(block, axis, [(i, i ^ bit) for i in range(count)])  75 us
    ppermute x18, starting transfers between devices, shift(): return lax.ppermute(block, axis, route)  49.6 us
    pallas_call x1, Pallas kernels, delta_backward(): on_chip(backward_kernel, 'delta_backward', grid=(blocks,), in_specs=[scal...  37.1 us
    pallas_call x2, Pallas kernels, norm_pulled(): on_chip(norm_pull_kernel, 'norm_pull', grid=(8,), in_specs=[scalars(), ha...  35.9 us
    ppermute x18, waiting for transfers between devices, shift(): return lax.ppermute(block, axis, route)  33.4 us
    pallas_call x1, Pallas kernels, delta_forward(): on_chip(forward_kernel, 'delta_forward', grid=(blocks,), in_specs=[scalar...  33.1 us
  transfers between devices with their start and end apart: 46, of which 26 were waited for; matrix products, arithmetic and copies ran while one was open for 20% of the time, Pallas kernels for 15%

profile of v6, /device:TPU:0, one launch (start us, length us, event | category | flops | bytes accessed | tf_op | source)
XLA Modules:
  0.0 969.8 jit_solution(8935938989081563997)
XLA Ops:
  34.0 33.1 %delta_forward.1 = (f32[8,4,128,128]{3,2,1,0:T(8,128)S(1)}, f32[1024,512]{1,0:T(8,128)S(1)}, f32[1024,512]{1,0:T(8,128)}, f32[8,4,128,256]{3,2,1,0:T(8,128)}, f32[4,128,256]{2,1,0:T(8,128)S(1)}) custom-call(s32[7]{0:T(128)S(1)} %copy-done.25, s32[1]{0:T(128)} %bitcast.base, f32[1024,512]{1,0:T(8,128)} %copy-done.32, f32[1024,512]{1,0:T(8,128)} %copy-done.31, ...), custom_call_target="tpu_custom_call" | custom-call | flops 1 | bytes 1 | tf_op jit(solution)/shard_map/delta_forward/pallas_call | solution.py:450
  143.5 8.9 convolution_add_fusion.2
  152.4 8.8 collective-permute-done.12.first
  169.8 9.0 multiply_reduce_fusion.1
  183.1 9.3 fusion.52
  205.9 14.3 %multiply_convert_fusion.2 = (bf16[1024,1408]{1,0:T(8,128)(2,1)}, bf16[1024,1408]{1,0:T(8,128)(2,1)}) fusion(f32[1024,1408]{1,0:T(8,128)} %copy-done.77, f32[1024,1408]{1,0:T(8,128)} %get-tuple-element.147, bf16[1024,2048]{1,0:T(8,128)(2,1)S(1)} %copy-done.39, bf16[1408,2048]{1,0:T(8,128)(2,1)} %param.34), kind=kOutput, calls=%fused_computation.12 | convolution fusion | flops 5924323328 | bytes 27262976 | tf_op jit(solution)/shard_map/dot_general | solution.py:775
  220.2 18.1 %fusion.1 = f32[2048,2816]{1,0:T(8,128)} fusion(bf16[1024,2048]{1,0:T(8,128)(2,1)S(1)} %multiply_convert_fusion, bf16[1024,1408]{1,0:T(8,128)(2,1)} %get-tuple-element.78, bf16[1024,1408]{1,0:T(8,128)(2,1)} %get-tuple-element.77), kind=kOutput, calls=%fused_computation.8 | convolution fusion | flops 11822694400 | bytes 33030144 | tf_op jit(solution)/shard_map/dot_general | solution.py:775
  238.4 9.9 %fusion.53 = f32[1024,2048]{1,0:T(8,128)S(1)} fusion(bf16[1024,1408]{1,0:T(8,128)(2,1)} %get-tuple-element.77, bf16[2048,1408]{1,0:T(8,128)(2,1)} %param.32), kind=kOutput, calls=%fused_computation.118 | convolution fusion | flops 5905580032 | bytes 17039360 | tf_op jit(solution)/shard_map/dot_general | solution.py:775
  290.3 123.1 %collective-permute-done.29 = f32[1152,1024]{1,0:T(8,128)} collective-permute-done((f32[1152,1024]{1,0:T(8,128)}, f32[1152,1024]{1,0:T(8,128)}, u32[]{:S(2)}, u32[]{:S(2)}) %collective-permute-start.29) | collective-permute-done | bytes 4718624 | tf_op jit(solution)/shard_map/ppermute | solution.py:643
  433.1 17.8 %norm_pull.2 = (f32[1024,2048]{1,0:T(8,128)}, bf16[1024,2048]{1,0:T(8,128)(2,1)S(1)}, f32[1,2048]{1,0:T(1,128)S(1)}) custom-call(s32[1]{0:T(128)} %bitcast.10.odd, f32[512,2048]{1,0:T(8,128)} %copy-done.33, f32[512,2048]{1,0:T(8,128)} %copy-done.53, f32[1024,2048]{1,0:T(8,128)} %get-tuple-element.145.values, f32[1,2048]{1,0:T(1,128)S(1)} %bitcast.79, ...), custom_call_target="tpu_custom_call" | custom-call | flops 1 | bytes 1 | tf_op jit(solution)/shard_map/norm_pull/pallas_call | solution.py:542
  504.2 13.1 %collective-permute-done.17 = f32[512,2048]{1,0:T(8,128)} collective-permute-done((f32[512,2048]{1,0:T(8,128)}, f32[512,2048]{1,0:T(8,128)}, u32[]{:S(2)}, u32[]{:S(2)}) %collective-permute-start.17) | collective-permute-done | bytes 4194336 | tf_op jit(solution)/shard_map/ppermute | solution.py:643
  523.9 37.1 %delta_backward.1 = (f32[1024,512]{1,0:T(8,128)S(1)}, f32[1024,512]{1,0:T(8,128)S(1)}, f32[1024,512]{1,0:T(8,128)}, f32[8,1536]{1,0:T(8,128)S(1)}, f32[1024,4]{1...) custom-call(s32[7]{0:T(128)S(1)} %copy-done.26, s32[1]{0:T(128)} %bitcast.base, ...), custom_call_target="tpu_custom_call" | custom-call | flops 1 | bytes 1 | tf_op jit(solution)/shard_map/delta_backward/pallas_call | solution.py:608
  563.3 37.7 %collective-permute-done.31 = f32[1152,512]{1,0:T(8,128)S(1)} collective-permute-done((f32[1152,512]{1,0:T(8,128)S(1)}, f32[1152,512]{1,0:T(8,128)S(1)}, u32[]{:S(2)}, u32[]{:S(2)}) %collective-permute-start.31) | collective-permute-done | bytes 2359328 | tf_op jit(solution)/shard_map/ppermute | solution.py:643
  607.2 9.2 fusion.56
  633.0 63.7 %collective-permute-done.32 = f32[768,1024]{1,0:T(8,128)S(1)} collective-permute-done((f32[768,1024]{1,0:T(8,128)S(1)}, f32[768,1024]{1,0:T(8,128)S(1)}, u32[]{:S(2)}, u32[]{:S(2)}) %collective-permute-start.32) | collective-permute-done | bytes 3145760 | tf_op jit(solution)/shard_map/ppermute | solution.py:643
  716.9 14.1 %multiply_reduce_fusion = (f32[2048]{0:T(1024)S(1)}, f32[1024,2048]{1,0:T(8,128)}) fusion(f32[1024,2048]{1,0:T(8,128)S(1)} %bitcast.90, f32[1024]{0:T(1024)S(1)} %copy-done.65, bf16[1024,4]{1,0:T(8,128)(2,1)S(1)} %get-tuple-element.104, bf16[2048,4]{0,1:T(4,128)(2,1)S(1)} %copy-done.67, f32[1024,2048]{1,0:T(8,128)} %fusion.59, f32[1024,2048]{1,0:T(8,128)} %fusion.57, ...), kind=kOutput, calls=%fused_computation.2 | convolution fusion | flops 29358080 | bytes 41979904 | tf_op jit(solution)/shard_map/dot_general | solution.py:775
  750.8 23.1 %collective-permute-start.38 = (f32[1152,256]{1,0:T(8,128)S(1)}, f32[1152,256]{1,0:T(8,128)S(1)}, u32[]{:S(2)}, u32[]{:S(2)}) collective-permute-start(f32[1152,256]{1,0:T(8,128)S(1)} %copy-done.60), channel_id=1, source_target_pairs={{0,16},{4,20},{8,24},{12,28},{16,0},{20,4},{24,8},{28,12},{1,17},{... | collective-permute-start | bytes 3538952 | tf_op jit(solution)/shard_map/ppermute | solution.py:643
  773.9 11.5 %collective-permute-start.37 = (f32[768,512]{1,0:T(8,128)S(1)}, f32[768,512]{1,0:T(8,128)S(1)}, u32[]{:S(2)}, u32[]{:S(2)}) collective-permute-start(f32[768,512]{1,0:T(8,128)S(1)} %copy-done.59), channel_id=1, source_target_pairs={{0,8},{4,12},{8,0},{12,4},{16,24},{20,28},{24,16},{28,20},{1,9},{5... | collective-permute-start | bytes 4718600 | tf_op jit(solution)/shard_map/ppermute | solution.py:643
  785.4 60.1 %collective-permute-done.38 = f32[1152,256]{1,0:T(8,128)S(1)} collective-permute-done((f32[1152,256]{1,0:T(8,128)S(1)}, f32[1152,256]{1,0:T(8,128)S(1)}, u32[]{:S(2)}, u32[]{:S(2)}) %collective-permute-start.38) | collective-permute-done | bytes 1179680 | tf_op jit(solution)/shard_map/ppermute | solution.py:643
  846.7 13.4 %collective-permute-done.37 = f32[768,512]{1,0:T(8,128)S(1)} collective-permute-done((f32[768,512]{1,0:T(8,128)S(1)}, f32[768,512]{1,0:T(8,128)S(1)}, u32[]{:S(2)}, u32[]{:S(2)}) %collective-permute-start.37) | collective-permute-done | bytes 1572896 | tf_op jit(solution)/shard_map/ppermute | solution.py:643
  882.7 24.7 %collective-permute-start.42 = (f32[18564]{0:T(1024)S(1)}, f32[18564]{0:T(1024)S(1)}, u32[]{:S(2)}, u32[]{:S(2)}) collective-permute-start(f32[18564]{0:T(1024)S(1)} %add.224), channel_id=1, source_target_pairs={{0,16},{4,20},{8,24},{12,28},{16,0},{20,4},{24,8},{28,12},{1,17},{... | collective-permute-start | bytes 222776 | tf_op jit(solution)/shard_map/ppermute | solution.py:643
  907.5 13.2 %fusion = f32[1024,2048]{1,0:T(8,128)} fusion(f32[1024,2048]{1,0:T(8,128)} %get-tuple-element.145.values, f32[512,2048]{1,0:T(8,128)} %collective-permute-done.18, f32[512,2048]{1,0:T(8,128)} %add.199, pred[]{:T(512)S(6)} %eq.10), kind=kLoop, calls=%fused_computation.1 | loop fusion | flops 8388608 | bytes 25165824 | tf_op jit(solution)/shard_map/add | solution.py:917
  929.1 18.1 %norm_pull.3 = (f32[1024,2048]{1,0:T(8,128)}, bf16[1024,2048]{1,0:T(8,128)(2,1)}, f32[1,2048]{1,0:T(1,128)}) custom-call(s32[1]{0:T(128)} %bitcast.10.odd, f32[512,2048]{1,0:T(8,128)} %add.222.part, f32[512,2048]{1,0:T(8,128)} %collective-permute-done.39.other, f32[1024,2048]{1,0:T(8,128)} %values.1, f32[1,2048]{1,0:T(1,128)S(1)} %bitcast.80, ...), custom_call_target="tpu_custom_call" | custom-call | flops 1 | bytes 1 | tf_op jit(solution)/shard_map/norm_pull/pallas_call | solution.py:542
  947.2 9.7 collective-permute-done.43
  (370 shorter events, 352.7 us)
Async XLA Ops:
  7.2 854.6 %reduce-scatter.3.cloned.1.call-start = ((), (), s32[]{:S(2)}) async-start(), calls=%async_computation.2 | async-start | bytes 25952256 | tf_op jit(solution)/shard_map/reduce_scatter | solution.py:851
  11.5 100.8 %collective-permute-start.10 = (f32[512,2048]{1,0:T(8,128)}, f32[512,2048]{1,0:T(8,128)}, u32[]{:S(2)}, u32[]{:S(2)}) collective-permute-start(f32[512,2048]{1,0:T(8,128)} %convert_element_type.40.first), channel_id=1, source_target_pairs={{0,2},{1,3},{2,0},{3,1},{4,6},{5,7},{6,4},{7,5},{8,10},{9,11},{10,... | collective-permute-start | bytes 12582920 | tf_op jit(solution)/shard_map/ppermute | solution.py:643
  112.3 19.4 %collective-permute-start.11 = (f32[512,2048]{1,0:T(8,128)}, f32[512,2048]{1,0:T(8,128)}, u32[]{:S(2)}, u32[]{:S(2)}) collective-permute-start(f32[512,2048]{1,0:T(8,128)} %convert_element_type.40.first), channel_id=1, source_target_pairs={{0,1},{1,0},{2,3},{3,2},{4,5},{5,4},{6,7},{7,6},{8,9},{9,8},{10,11... | collective-permute-start | bytes 12582920 | tf_op jit(solution)/shard_map/ppermute | solution.py:643
  112.3 25.3 %collective-permute-start.13 = (f32[512,2048]{1,0:T(8,128)}, f32[512,2048]{1,0:T(8,128)}, u32[]{:S(2)}, u32[]{:S(2)}) collective-permute-start(f32[512,2048]{1,0:T(8,128)} %collective-permute-done.10.first), channel_id=1, source_target_pairs={{0,1},{1,0},{2,3},{3,2},{4,5},{5,4},{6,7},{7,6},{8,9},{9,8},{10,11... | collective-permute-start | bytes 12582920 | tf_op jit(solution)/shard_map/ppermute | solution.py:643
  112.8 16.0 %collective-permute-start.9 = (f32[1024,512]{1,0:T(8,128)}, f32[1024,512]{1,0:T(8,128)}, u32[]{:S(2)}, u32[]{:S(2)}) collective-permute-start(f32[1024,512]{1,0:T(8,128)} %get-tuple-element.70.first), channel_id=1, source_target_pairs={{0,1},{1,0},{2,3},{3,2},{4,5},{5,4},{6,7},{7,6},{8,9},{9,8},{10,11... | collective-permute-start | bytes 6291464 | tf_op jit(solution)/shard_map/ppermute | solution.py:643
  112.8 48.4 %collective-permute-start.12 = (f32[1024,512]{1,0:T(8,128)}, f32[1024,512]{1,0:T(8,128)}, u32[]{:S(2)}, u32[]{:S(2)}) collective-permute-start(f32[1024,512]{1,0:T(8,128)} %get-tuple-element.70.first), channel_id=1, source_target_pairs={{0,2},{1,3},{2,0},{3,1},{4,6},{5,7},{6,4},{7,5},{8,10},{9,11},{10,... | collective-permute-start | bytes 6291464 | tf_op jit(solution)/shard_map/ppermute | solution.py:643
  238.3 720.7 %reduce-scatter.5.cloned.1.call-start = ((), (), s32[]{:S(2)}) async-start(), calls=%async_computation.3 | async-start | bytes 14155776 | tf_op jit(solution)/shard_map/reduce_scatter | solution.py:898
  261.9 151.4 %collective-permute-start.29 = (f32[1152,1024]{1,0:T(8,128)}, f32[1152,1024]{1,0:T(8,128)}, u32[]{:S(2)}, u32[]{:S(2)}) collective-permute-start(f32[1152,1024]{1,0:T(8,128)} %fusion.10), channel_id=1, source_target_pairs={{0,4},{4,0},{8,12},{12,8},{16,20},{20,16},{24,28},{28,24},{1,5},{5... | collective-permute-start | bytes 14155784 | tf_op jit(solution)/shard_map/ppermute | solution.py:643
  283.0 137.1 %collective-permute-start.16 = (f32[512,2048]{1,0:T(8,128)S(1)}, f32[512,2048]{1,0:T(8,128)S(1)}, u32[]{:S(2)}, u32[]{:S(2)}) collective-permute-start(f32[512,2048]{1,0:T(8,128)S(1)} %constant_dynamic-slice_fusion.1), channel_id=1, source_target_pairs={{0,1},{1,0},{2,3},{3,2},{4,5},{5,4},{6,7},{7,6},{8,9},{9,8},{10,11... | collective-permute-start | bytes 12582920 | tf_op jit(solution)/shard_map/ppermute | solution.py:643
  283.3 139.8 %collective-permute-start.19 = (f32[512,2048]{1,0:T(8,128)S(1)}, f32[512,2048]{1,0:T(8,128)S(1)}, u32[]{:S(2)}, u32[]{:S(2)}) collective-permute-start(f32[512,2048]{1,0:T(8,128)S(1)} %dynamic-slice_add_fusion.2), channel_id=1, source_target_pairs={{0,2},{1,3},{2,0},{3,1},{4,6},{5,7},{6,4},{7,5},{8,10},{9,11},{10,... | collective-permute-start | bytes 12582920 | tf_op jit(solution)/shard_map/ppermute | solution.py:643
  424.0 93.3 %collective-permute-start.17 = (f32[512,2048]{1,0:T(8,128)}, f32[512,2048]{1,0:T(8,128)}, u32[]{:S(2)}, u32[]{:S(2)}) collective-permute-start(f32[512,2048]{1,0:T(8,128)} %dynamic-slice_add_fusion.1), channel_id=1, source_target_pairs={{0,2},{1,3},{2,0},{3,1},{4,6},{5,7},{6,4},{7,5},{8,10},{9,11},{10,... | collective-permute-start | bytes 12582920 | tf_op jit(solution)/shard_map/ppermute | solution.py:643
  467.5 11.4 %collective-permute-start.22 = (f32[2,128,128]{2,1,0:T(8,128)S(1)}, f32[2,128,128]{2,1,0:T(8,128)S(1)}, u32[]{:S(2)}, u32[]{:S(2)}) collective-permute-start(f32[2,128,128]{2,1,0:T(8,128)S(1)} %convolution_add_fusion.9), channel_id=1, source_target_pairs={{4,0},{8,4},{12,8},{16,12},{20,16},{24,20},{28,24},{5,1},{9,5},{13... | collective-permute-start | bytes 393224 | tf_op jit(solution)/shard_map/ppermute | solution.py:649
  470.4 14.1 %collective-permute-start.26 = (f32[2,128,128]{2,1,0:T(8,128)S(1)}, f32[2,128,128]{2,1,0:T(8,128)S(1)}, u32[]{:S(2)}, u32[]{:S(2)}) collective-permute-start(f32[2,128,128]{2,1,0:T(8,128)S(1)} %convolution_add_fusion.6), channel_id=1, source_target_pairs={{4,0},{8,4},{12,8},{16,12},{20,16},{24,20},{28,24},{5,1},{9,5},{13... | collective-permute-start | bytes 393224 | tf_op jit(solution)/shard_map/ppermute | solution.py:649
  479.2 11.0 %collective-permute-start.23 = (f32[2,128,128]{2,1,0:T(8,128)S(1)}, f32[2,128,128]{2,1,0:T(8,128)S(1)}, u32[]{:S(2)}, u32[]{:S(2)}) collective-permute-start(f32[2,128,128]{2,1,0:T(8,128)S(1)} %convolution_add_fusion.8), channel_id=1, source_target_pairs={{4,0},{8,4},{12,8},{16,12},{20,16},{24,20},{28,24},{5,1},{9,5},{13... | collective-permute-start | bytes 393224 | tf_op jit(solution)/shard_map/ppermute | solution.py:649
  503.1 97.9 %collective-permute-start.31 = (f32[1152,512]{1,0:T(8,128)S(1)}, f32[1152,512]{1,0:T(8,128)S(1)}, u32[]{:S(2)}, u32[]{:S(2)}) collective-permute-start(f32[1152,512]{1,0:T(8,128)S(1)} %slice.230), channel_id=1, source_target_pairs={{0,8},{4,12},{8,0},{12,4},{16,24},{20,28},{24,16},{28,20},{1,9},{5... | collective-permute-start | bytes 7077896 | tf_op jit(solution)/shard_map/ppermute | solution.py:643
  561.1 43.5 %collective-permute-start.30 = (f32[8,1536]{1,0:T(8,128)S(1)}, f32[8,1536]{1,0:T(8,128)S(1)}, u32[]{:S(2)}, u32[]{:S(2)}) collective-permute-start(f32[8,1536]{1,0:T(8,128)S(1)} %get-tuple-element.91), channel_id=1, source_target_pairs={{4,0},{8,4},{12,8},{16,12},{20,16},{24,20},{28,24},{5,1},{9,5},{13... | collective-permute-start | bytes 147464 | tf_op jit(solution)/shard_map/ppermute | solution.py:649
  627.1 69.5 %collective-permute-start.32 = (f32[768,1024]{1,0:T(8,128)S(1)}, f32[768,1024]{1,0:T(8,128)S(1)}, u32[]{:S(2)}, u32[]{:S(2)}) collective-permute-start(f32[768,1024]{1,0:T(8,128)S(1)} %pad_maximum_fusion.1), channel_id=1, source_target_pairs={{0,4},{4,0},{8,12},{12,8},{16,20},{20,16},{24,28},{28,24},{1,5},{5... | collective-permute-start | bytes 9437192 | tf_op jit(solution)/shard_map/ppermute | solution.py:643
  749.9 111.9 %collective-permute-start.36 = (f32[512,2048]{1,0:T(8,128)S(1)}, f32[512,2048]{1,0:T(8,128)}, u32[]{:S(2)}, u32[]{:S(2)}) collective-permute-start(f32[512,2048]{1,0:T(8,128)S(1)} %dynamic-slice_add_fusion), channel_id=1, source_target_pairs={{0,2},{1,3},{2,0},{3,1},{4,6},{5,7},{6,4},{7,5},{8,10},{9,11},{10,... | collective-permute-start | bytes 12582920 | tf_op jit(solution)/shard_map/ppermute | solution.py:643
  750.8 94.7 %collective-permute-start.38 = (f32[1152,256]{1,0:T(8,128)S(1)}, f32[1152,256]{1,0:T(8,128)S(1)}, u32[]{:S(2)}, u32[]{:S(2)}) collective-permute-start(f32[1152,256]{1,0:T(8,128)S(1)} %copy-done.60), channel_id=1, source_target_pairs={{0,16},{4,20},{8,24},{12,28},{16,0},{20,4},{24,8},{28,12},{1,17},{... | collective-permute-start | bytes 3538952 | tf_op jit(solution)/shard_map/ppermute | solution.py:643
  773.9 86.2 %collective-permute-start.37 = (f32[768,512]{1,0:T(8,128)S(1)}, f32[768,512]{1,0:T(8,128)S(1)}, u32[]{:S(2)}, u32[]{:S(2)}) collective-permute-start(f32[768,512]{1,0:T(8,128)S(1)} %copy-done.59), channel_id=1, source_target_pairs={{0,8},{4,12},{8,0},{12,4},{16,24},{20,28},{24,16},{28,20},{1,9},{5... | collective-permute-start | bytes 4718600 | tf_op jit(solution)/shard_map/ppermute | solution.py:643
  785.4 122.1 %collective-permute-start.18 = (f32[512,2048]{1,0:T(8,128)}, f32[512,2048]{1,0:T(8,128)}, u32[]{:S(2)}, u32[]{:S(2)}) collective-permute-start(f32[512,2048]{1,0:T(8,128)} %add.199), channel_id=1, source_target_pairs={{0,1},{1,0},{2,3},{3,2},{4,5},{5,4},{6,7},{7,6},{8,9},{9,8},{10,11... | collective-permute-start | bytes 12582920 | tf_op jit(solution)/shard_map/ppermute | solution.py:643
  868.7 60.4 %collective-permute-start.39 = (f32[512,2048]{1,0:T(8,128)}, f32[512,2048]{1,0:T(8,128)}, u32[]{:S(2)}, u32[]{:S(2)}) collective-permute-start(f32[512,2048]{1,0:T(8,128)} %add.222.part), channel_id=1, source_target_pairs={{0,1},{1,0},{2,3},{3,2},{4,5},{5,4},{6,7},{7,6},{8,9},{9,8},{10,11... | collective-permute-start | bytes 12582920 | tf_op jit(solution)/shard_map/ppermute | solution.py:643
  882.7 38.0 %collective-permute-start.42 = (f32[18564]{0:T(1024)S(1)}, f32[18564]{0:T(1024)S(1)}, u32[]{:S(2)}, u32[]{:S(2)}) collective-permute-start(f32[18564]{0:T(1024)S(1)} %add.224), channel_id=1, source_target_pairs={{0,16},{4,20},{8,24},{12,28},{16,0},{20,4},{24,8},{28,12},{1,17},{... | collective-permute-start | bytes 222776 | tf_op jit(solution)/shard_map/ppermute | solution.py:643
  920.7 36.2 %collective-permute-start.43 = (f32[768,256]{1,0:T(8,128)}, f32[768,256]{1,0:T(8,128)}, u32[]{:S(2)}, u32[]{:S(2)}) collective-permute-start(f32[768,256]{1,0:T(8,128)} %get-tuple-element.129), channel_id=1, source_target_pairs={{0,16},{4,20},{8,24},{12,28},{16,0},{20,4},{24,8},{28,12},{1,17},{... | collective-permute-start | bytes 2359304 | tf_op jit(solution)/shard_map/ppermute | solution.py:643
  (105 other events, 1651.4 us)
Sparse Core Ops, SparseCore 0:
  238.4 414.5 reduce-scatter.2
  656.6 235.5 reduce-scatter.4
